TPU v7x, 128 devices: a whole 4x4x4 slice. The times are simulated.
128 devices in a mesh: lat: 8 (over x, y_lo), lon: 16 (over y_hi, z, core).
Axes of the slice: x: 4, y: 4 (y_hi: 2, y_lo: 2; y = y_hi * 2 + y_lo), z: 4, core: 2. Of those that a mesh axis runs over, the one named last changes fastest.
Arguments:
- pool: bfloat16 [64, 768, 1152], P('lat', 'lon'), may hold values from -6 to 6
- vec_ids: int32 [8], replicated, may hold values from 0 to 7, as said below
- winds: float32 [64, 768, 288], P('lat', 'lon'), may hold values from -0.3 to 0.3
- wind_ids: int32 [4], replicated, may hold values from 0 to 1
- mixing: float32 [142], replicated, may hold values from 0.01 to 0.05
- basis: bfloat16 [64, 768, 1152], P('lat', 'lon'), may hold values from -6 to 6
Outputs:
- sensitivity: float32 [64, 768, 1152], P('lat', 'lon')
- ritz: float32 [1152, 1152], P('lat', 'lon')
Inputs may be any that keep to these rules, and one draw needn't show every extreme that they name: `vec_ids`: the entries are distinct and one of them is 7.
All inputs are finite; a program needn't handle non-finite values.
Results may differ from a plain program's by a relative error of at most 0.0029.
Values sent between devices are 32-bit elements; how exact they have to be, the bound alone decides.
No kernel may reach another device: no remote copies, remote signals or barrier semaphores. Data moves between devices by JAX's collectives and lax.ppermute only.
A program may use at most 128 MiB of HBM per device.

v0:
```python
import math

import jax
import jax.numpy as jnp
from jax import lax
from jax.sharding import PartitionSpec as P

LEV = 72
TR = 2
VEC = 8
POOL = 8
NSLAB = 2
STEPS = 4


DIFFUSE = 0.075


def with_halo(block, sides, width, periodic):
    for axis, dim in sides:
        count = lax.axis_size(axis)
        forward = [(i, i + 1) for i in range(count - 1)]
        if periodic:
            forward.append((count - 1, 0))
        backward = [(target, source) for source, target in forward]
        low = lax.ppermute(
            lax.slice_in_dim(block, block.shape[dim] - width, None, axis=dim), axis, forward
        )
        high = lax.ppermute(lax.slice_in_dim(block, 0, width, axis=dim), axis, backward)
        block = jnp.concatenate([low, block, high], axis=dim)
    return block


def passed_along(value, axis, steps):
    count = lax.axis_size(axis)
    pairs = [(source, (source + steps) % count) for source in range(count)]
    return lax.ppermute(value, axis, pairs)


def channel_coefficients(mixing):
    level_mix = mixing.reshape(TR, LEV - 1)
    padded = jnp.concatenate([level_mix, jnp.zeros((TR, 1), mixing.dtype)], axis=1)
    return jnp.tile(padded.reshape(TR * LEV), VEC)


def select_winds(winds, slab_index):
    tile_rows, tile_cols = (winds.shape[0], winds.shape[1])
    layered = winds.reshape(tile_rows, tile_cols, NSLAB, 2, LEV)
    chosen = lax.dynamic_index_in_dim(layered, slab_index, axis=2, keepdims=False)
    wind_east = jnp.tile(chosen[:, :, 0], (1, 1, VEC * TR))
    wind_north = jnp.tile(chosen[:, :, 1], (1, 1, VEC * TR))
    return (wind_east, wind_north)


def update(
    state_now, north_side, south_side, east_side, west_side, wind_east, wind_north, coefficient
):
    advect = (
        jnp.maximum(wind_east, 0.0) * (east_side - state_now)
        + jnp.maximum(-wind_east, 0.0) * (west_side - state_now)
        + jnp.maximum(wind_north, 0.0) * (north_side - state_now)
        + jnp.maximum(-wind_north, 0.0) * (south_side - state_now)
    )
    spread = DIFFUSE * (north_side + south_side + (east_side + west_side) - 4.0 * state_now)
    flux_up = coefficient * (jnp.roll(state_now, -1, axis=-1) - state_now)
    vertical = flux_up - jnp.roll(flux_up, 1, axis=-1)
    return state_now + advect + spread + vertical


def advance(state_now, winds, slab_index, coefficient, lat_index, lat_count):
    wind_east, wind_north = select_winds(winds, slab_index)
    beside = with_halo(state_now, (("lat", 0),), 1, False)
    pole_rows = jnp.where(lat_index == 0, state_now[:1], state_now[-1:])
    folded = passed_along(pole_rows, "lon", lax.axis_size("lon") // 2)
    lower_rim = jnp.where(lat_index == 0, folded, beside[:1])
    upper_rim = jnp.where(lat_index == lat_count - 1, folded, beside[-1:])
    zonal = with_halo(state_now, (("lon", 1),), 1, True)
    north_side = jnp.concatenate([state_now[1:], upper_rim], axis=0)
    south_side = jnp.concatenate([lower_rim, state_now[:-1]], axis=0)
    return update(
        state_now,
        north_side,
        south_side,
        zonal[:, 2:],
        zonal[:, :-2],
        wind_east,
        wind_north,
        coefficient,
    )


def shards(pool, vec_ids, winds, wind_ids, mixing, basis):
    tile_rows, tile_cols = (pool.shape[0], pool.shape[1])
    channels = VEC * TR * LEV
    basis_rows = basis.shape[2]
    lat_count = lax.axis_size("lat")
    lon_count = lax.axis_size("lon")
    lat_index = lax.axis_index("lat")
    lon_index = lax.axis_index("lon")
    grouped = pool.reshape(tile_rows, tile_cols, POOL, TR * LEV)
    state_now = (
        jnp.take(grouped, vec_ids, axis=2)
        .reshape(tile_rows, tile_cols, channels)
        .astype(jnp.float32)
    )
    coefficient = channel_coefficients(mixing)
    for step_index in range(STEPS):
        state_now = advance(
            state_now, winds, wind_ids[step_index], coefficient, lat_index, lat_count
        )
    global_rows = (jnp.arange(tile_rows, dtype=jnp.int32) + lat_index * tile_rows).astype(
        jnp.float32
    )
    weights = jnp.cos((global_rows + 0.5) * (math.pi / (tile_rows * lat_count)) - math.pi / 2)
    weighted = (
        (weights[:, None, None] * state_now)
        .astype(jnp.bfloat16)
        .reshape(tile_rows * tile_cols, channels)
    )
    flat_basis = basis.reshape(tile_rows * tile_cols, basis_rows)
    scale = 1.0 / math.sqrt(tile_rows * lat_count * tile_cols * lon_count)
    row_share_count = basis_rows // lat_count
    column_share_count = channels // lon_count
    summed = lax.psum(
        lax.dot_general(
            flat_basis, weighted, (((0,), (0,)), ((), ())), preferred_element_type=jnp.float32
        ),
        ("lat", "lon"),
    )
    owned = lax.dynamic_slice(
        summed,
        (lat_index * row_share_count, lon_index * column_share_count),
        (row_share_count, column_share_count),
    )
    return (state_now, owned * scale)


def solution(mesh):
    in_specs = (P("lat", "lon", None), P(), P("lat", "lon", None), P(), P(), P("lat", "lon", None))
    out_specs = (P("lat", "lon", None), P("lat", "lon"))
    return jax.shard_map(shards, mesh=mesh, in_specs=in_specs, out_specs=out_specs, check_vma=False)
```

profile of v0, /device:TPU:0, one launch (start us, length us, event | category | flops | bytes accessed | tf_op | source)
XLA Modules:
  0.0 393.5 jit_solution(10574336004809795614)
XLA Ops:
  26.2 5.2 %collective-permute-start.4 = (f32[1,48,1152]{2,1,0:T(8,128)}, f32[1,48,1152]{2,1,0:T(8,128)}, u32[]{:S(2)}, u32[]{:S(2)}) collective-permute-start(f32[1,48,1152]{2,1,0:T(8,128)} %get-tuple-element.33), channel_id=1, source_target_pairs={{0,16},{16,32},{32,48},{48,64},{64,80},{80,96},{96,112},{1,17},{17... | collective-permute-start | bytes 663560 | tf_op jit(solution)/shard_map/ppermute | solution.py:26
  54.0 4.6 %max.162 = f32[8,48,1152]{2,1,0:T(8,128)} reshape(f32[8,48,16,72]{3,2,1,0:T(8,128)} %tile.71) | data formatting | bytes 3538944 | tf_op jit(solution)/shard_map/max | solution.py:59
  61.4 4.2 %max.165 = f32[8,48,1152]{2,1,0:T(8,128)} reshape(f32[8,48,16,72]{3,2,1,0:T(8,128)} %tile.72) | data formatting | bytes 3538944 | tf_op jit(solution)/shard_map/max | solution.py:60
  68.4 4.2 %max.168 = f32[8,48,1152]{2,1,0:T(8,128)} reshape(f32[8,48,16,72]{3,2,1,0:T(8,128)} %tile.73) | data formatting | bytes 3538944 | tf_op jit(solution)/shard_map/max | solution.py:61
  75.3 4.2 %max.171 = f32[8,48,1152]{2,1,0:T(8,128)} reshape(f32[8,48,16,72]{3,2,1,0:T(8,128)} %tile.74) | data formatting | bytes 3538944 | tf_op jit(solution)/shard_map/max | solution.py:62
  83.1 4.2 %max.174 = f32[8,48,1152]{2,1,0:T(8,128)} reshape(f32[8,48,16,72]{3,2,1,0:T(8,128)} %tile.77) | data formatting | bytes 3538944 | tf_op jit(solution)/shard_map/max | solution.py:59
  89.2 4.2 %max.177 = f32[8,48,1152]{2,1,0:T(8,128)} reshape(f32[8,48,16,72]{3,2,1,0:T(8,128)} %tile.78) | data formatting | bytes 3538944 | tf_op jit(solution)/shard_map/max | solution.py:60
  95.2 4.2 %max.180 = f32[8,48,1152]{2,1,0:T(8,128)} reshape(f32[8,48,16,72]{3,2,1,0:T(8,128)} %tile.79) | data formatting | bytes 3538944 | tf_op jit(solution)/shard_map/max | solution.py:61
  101.3 4.2 %max.183 = f32[8,48,1152]{2,1,0:T(8,128)} reshape(f32[8,48,16,72]{3,2,1,0:T(8,128)} %tile.80) | data formatting | bytes 3538944 | tf_op jit(solution)/shard_map/max | solution.py:62
  107.4 4.2 %max.186 = f32[8,48,1152]{2,1,0:T(8,128)} reshape(f32[8,48,16,72]{3,2,1,0:T(8,128)} %tile.81) | data formatting | bytes 3538944 | tf_op jit(solution)/shard_map/max | solution.py:59
  113.5 4.2 %max.189 = f32[8,48,1152]{2,1,0:T(8,128)} reshape(f32[8,48,16,72]{3,2,1,0:T(8,128)} %tile.82) | data formatting | bytes 3538944 | tf_op jit(solution)/shard_map/max | solution.py:60
  119.5 4.3 %max.192 = f32[8,48,1152]{2,1,0:T(8,128)} reshape(f32[8,48,16,72]{3,2,1,0:T(8,128)} %tile.83) | data formatting | bytes 3538944 | tf_op jit(solution)/shard_map/max | solution.py:61
  125.7 4.2 %max.195 = f32[8,48,1152]{2,1,0:T(8,128)} reshape(f32[8,48,16,72]{3,2,1,0:T(8,128)} %tile.84) | data formatting | bytes 3538944 | tf_op jit(solution)/shard_map/max | solution.py:62
  143.8 4.2 %max.204 = f32[8,48,1152]{2,1,0:T(8,128)} reshape(f32[8,48,16,72]{3,2,1,0:T(8,128)} %tile.87) | data formatting | bytes 3538944 | tf_op jit(solution)/shard_map/max | solution.py:61
  149.9 4.3 %max.207 = f32[8,48,1152]{2,1,0:T(8,128)} reshape(f32[8,48,16,72]{3,2,1,0:T(8,128)} %tile.88) | data formatting | bytes 3538944 | tf_op jit(solution)/shard_map/max | solution.py:62
  155.4 6.1 %fusion.8 = f32[8,48,1152]{2,1,0:T(8,128)S(1)} fusion(f32[8,48,1152]{2,1,0:T(8,128)} %max.171, f32[8,48,1152]{2,1,0:T(8,128)} %max.168, f32[8,48,1152]{2,1,0:T(8,128)} %max.165, f32[8,48,1152]{2,1,0:T(8,128)} %max.162, f32[8,48,1152]{2,1,0:T(8,128)} %copy-done.3, f32[8,48,1151]{2,1,0:T(8,128)} %bitcast.88, f32[8,48,1]{2,1,0:T(8,128)} %slice.272, ...), kind=kLoop, calls=%fused_computation.17 | loop fusion | flops 12386304 | bytes 18654336 | tf_op jit(solution)/shard_map/add | solution.py:67
  166.4 4.6 %collective-permute-start.9 = (f32[1,48,1152]{2,1,0:T(8,128)S(1)}, f32[1,48,1152]{2,1,0:T(8,128)S(1)}, u32[]{:S(2)}, u32[]{:S(2)}) collective-permute-start(f32[1,48,1152]{2,1,0:T(8,128)S(1)} %get-tuple-element.26), channel_id=1, source_target_pairs={{0,16},{16,32},{32,48},{48,64},{64,80},{80,96},{96,112},{1,17},{17... | collective-permute-start | bytes 663560 | tf_op jit(solution)/shard_map/ppermute | solution.py:26
  171.4 4.6 %collective-permute-start.5 = (f32[8,1,1152]{2,1,0:T(1,128)S(1)}, f32[8,1,1152]{2,1,0:T(1,128)S(1)}, u32[]{:S(2)}, u32[]{:S(2)}) collective-permute-start(f32[8,1,1152]{2,1,0:T(1,128)S(1)} %get-tuple-element.27), channel_id=1, source_target_pairs={{1,0},{2,1},{3,2},{4,3},{5,4},{6,5},{7,6},{8,7},{9,8},{10,9},{11,1... | collective-permute-start | bytes 110600 | tf_op jit(solution)/shard_map/ppermute | solution.py:29
  178.5 5.2 %collective-permute-done.6 = f32[8,1,1152]{2,1,0:T(1,128)S(1)} collective-permute-done((f32[8,1,1152]{2,1,0:T(1,128)S(1)}, f32[8,1,1152]{2,1,0:T(1,128)S(1)}, u32[]{:S(2)}, u32[]{:S(2)}) %collective-permute-start.6) | collective-permute-done | bytes 36896 | tf_op jit(solution)/shard_map/ppermute | solution.py:26
  188.8 4.6 %collective-permute-start.14 = (f32[1,48,1152]{2,1,0:T(8,128)S(1)}, f32[1,48,1152]{2,1,0:T(8,128)S(1)}, u32[]{:S(2)}, u32[]{:S(2)}) collective-permute-start(f32[1,48,1152]{2,1,0:T(8,128)S(1)} %get-tuple-element.19), channel_id=1, source_target_pairs={{0,16},{16,32},{32,48},{48,64},{64,80},{80,96},{96,112},{1,17},{17... | collective-permute-start | bytes 663560 | tf_op jit(solution)/shard_map/ppermute | solution.py:26
  198.9 4.2 %collective-permute-done.11 = f32[8,1,1152]{2,1,0:T(1,128)S(1)} collective-permute-done((f32[8,1,1152]{2,1,0:T(1,128)S(1)}, f32[8,1,1152]{2,1,0:T(1,128)S(1)}, u32[]{:S(2)}, u32[]{:S(2)}) %collective-permute-start.11) | collective-permute-done | bytes 36896 | tf_op jit(solution)/shard_map/ppermute | solution.py:26
  209.2 4.6 %collective-permute-start.19 = (f32[1,48,1152]{2,1,0:T(8,128)S(1)}, f32[1,48,1152]{2,1,0:T(8,128)S(1)}, u32[]{:S(2)}, u32[]{:S(2)}) collective-permute-start(f32[1,48,1152]{2,1,0:T(8,128)S(1)} %get-tuple-element.12), channel_id=1, source_target_pairs={{0,16},{16,32},{32,48},{48,64},{64,80},{80,96},{96,112},{1,17},{17... | collective-permute-start | bytes 663560 | tf_op jit(solution)/shard_map/ppermute | solution.py:26
  218.5 4.8 %collective-permute-done.16 = f32[8,1,1152]{2,1,0:T(1,128)S(1)} collective-permute-done((f32[8,1,1152]{2,1,0:T(1,128)S(1)}, f32[8,1,1152]{2,1,0:T(1,128)S(1)}, u32[]{:S(2)}, u32[]{:S(2)}) %collective-permute-start.16) | collective-permute-done | bytes 36896 | tf_op jit(solution)/shard_map/ppermute | solution.py:26
  229.7 155.0 %all-reduce.3.cloned.1.call-done = f32[1152,1152]{0,1:T(8,128)} async-done(((f32[1152,1152]{0,1:T(8,128)}), f32[1152,1152]{0,1:T(8,128)}) %all-reduce.3.cloned.1.call-update) | async-done | bytes 5308432 | tf_op jit(solution)/shard_map/psum | solution.py:124
  (181 shorter events, 113.2 us)
Async XLA Ops:
  7.2 218.3 %copy-start = (bf16[8,48,1152]{2,1,0:T(8,128)(2,1)S(1)}, bf16[8,48,1152]{2,1,0:T(8,128)(2,1)}, u32[]{:S(2)}) copy-start(bf16[8,48,1152]{2,1,0:T(8,128)(2,1)} %param.11) | copy-start | bytes 2654212
  7.2 377.5 %all-reduce.3.cloned.1.call-start = ((), (), s32[]{:S(2)}) async-start(), calls=%async_computation | async-start | bytes 10616832 | tf_op jit(solution)/shard_map/psum | solution.py:124
  20.7 21.2 %copy-start.1 = (f32[8,48,1152]{2,1,0:T(8,128)}, f32[8,48,1152]{2,1,0:T(8,128)S(1)}, u32[]{:S(2)}) copy-start(f32[8,48,1152]{2,1,0:T(8,128)S(1)} %fusion.58) | copy-start | bytes 5308420
  21.7 132.6 %collective-permute-start.2 = (f32[1,48,1152]{2,1,0:T(8,128)}, f32[1,48,1152]{2,1,0:T(8,128)}, u32[]{:S(2)}, u32[]{:S(2)}) collective-permute-start(f32[1,48,1152]{2,1,0:T(8,128)} %get-tuple-element.32), channel_id=1, source_target_pairs={{0,8},{1,9},{2,10},{3,11},{4,12},{5,13},{6,14},{7,15},{8,0},{9,1},... | collective-permute-start | bytes 663560 | tf_op jit(solution)/shard_map/ppermute | solution.py:37
  25.0 129.3 %collective-permute-start.3 = (f32[1,48,1152]{2,1,0:T(8,128)}, f32[1,48,1152]{2,1,0:T(8,128)}, u32[]{:S(2)}, u32[]{:S(2)}) collective-permute-start(f32[1,48,1152]{2,1,0:T(8,128)} %get-tuple-element.31), channel_id=1, source_target_pairs={{16,0},{32,16},{48,32},{64,48},{80,64},{96,80},{112,96},{17,1},{33... | collective-permute-start | bytes 663560 | tf_op jit(solution)/shard_map/ppermute | solution.py:29
  26.2 128.1 %collective-permute-start.4 = (f32[1,48,1152]{2,1,0:T(8,128)}, f32[1,48,1152]{2,1,0:T(8,128)}, u32[]{:S(2)}, u32[]{:S(2)}) collective-permute-start(f32[1,48,1152]{2,1,0:T(8,128)} %get-tuple-element.33), channel_id=1, source_target_pairs={{0,16},{16,32},{32,48},{48,64},{64,80},{80,96},{96,112},{1,17},{17... | collective-permute-start | bytes 663560 | tf_op jit(solution)/shard_map/ppermute | solution.py:26
  32.1 123.2 %collective-permute-start = (f32[8,1,1152]{2,1,0:T(1,128)}, f32[8,1,1152]{2,1,0:T(1,128)}, u32[]{:S(2)}, u32[]{:S(2)}) collective-permute-start(f32[8,1,1152]{2,1,0:T(1,128)} %get-tuple-element.35), channel_id=1, source_target_pairs={{1,0},{2,1},{3,2},{4,3},{5,4},{6,5},{7,6},{8,7},{9,8},{10,9},{11,1... | collective-permute-start | bytes 110600 | tf_op jit(solution)/shard_map/ppermute | solution.py:29
  35.0 120.4 %collective-permute-start.1 = (f32[8,1,1152]{2,1,0:T(1,128)}, f32[8,1,1152]{2,1,0:T(1,128)}, u32[]{:S(2)}, u32[]{:S(2)}) collective-permute-start(f32[8,1,1152]{2,1,0:T(1,128)} %get-tuple-element.34), channel_id=1, source_target_pairs={{0,1},{1,2},{2,3},{3,4},{4,5},{5,6},{6,7},{7,8},{8,9},{9,10},{10,1... | collective-permute-start | bytes 110600 | tf_op jit(solution)/shard_map/ppermute | solution.py:26
  51.3 28.2 %copy-start.3 = (f32[8,48,1152]{2,1,0:T(8,128)}, f32[8,48,1152]{2,1,0:T(8,128)S(1)}, u32[]{:S(2)}) copy-start(f32[8,48,1152]{2,1,0:T(8,128)S(1)} %fusion.11) | copy-start | bytes 5308420
  162.3 13.7 %collective-permute-start.7 = (f32[1,48,1152]{2,1,0:T(8,128)S(1)}, f32[1,48,1152]{2,1,0:T(8,128)S(1)}, u32[]{:S(2)}, u32[]{:S(2)}) collective-permute-start(f32[1,48,1152]{2,1,0:T(8,128)S(1)} %get-tuple-element.25), channel_id=1, source_target_pairs={{0,8},{1,9},{2,10},{3,11},{4,12},{5,13},{6,14},{7,15},{8,0},{9,1},... | collective-permute-start | bytes 663560 | tf_op jit(solution)/shard_map/ppermute | solution.py:37
  165.1 10.9 %collective-permute-start.8 = (f32[1,48,1152]{2,1,0:T(8,128)S(1)}, f32[1,48,1152]{2,1,0:T(8,128)S(1)}, u32[]{:S(2)}, u32[]{:S(2)}) collective-permute-start(f32[1,48,1152]{2,1,0:T(8,128)S(1)} %get-tuple-element.24), channel_id=1, source_target_pairs={{16,0},{32,16},{48,32},{64,48},{80,64},{96,80},{112,96},{17,1},{33... | collective-permute-start | bytes 663560 | tf_op jit(solution)/shard_map/ppermute | solution.py:29
  166.4 11.6 %collective-permute-start.9 = (f32[1,48,1152]{2,1,0:T(8,128)S(1)}, f32[1,48,1152]{2,1,0:T(8,128)S(1)}, u32[]{:S(2)}, u32[]{:S(2)}) collective-permute-start(f32[1,48,1152]{2,1,0:T(8,128)S(1)} %get-tuple-element.26), channel_id=1, source_target_pairs={{0,16},{16,32},{32,48},{48,64},{64,80},{80,96},{96,112},{1,17},{17... | collective-permute-start | bytes 663560 | tf_op jit(solution)/shard_map/ppermute | solution.py:26
  171.4 7.0 %collective-permute-start.5 = (f32[8,1,1152]{2,1,0:T(1,128)S(1)}, f32[8,1,1152]{2,1,0:T(1,128)S(1)}, u32[]{:S(2)}, u32[]{:S(2)}) collective-permute-start(f32[8,1,1152]{2,1,0:T(1,128)S(1)} %get-tuple-element.27), channel_id=1, source_target_pairs={{1,0},{2,1},{3,2},{4,3},{5,4},{6,5},{7,6},{8,7},{9,8},{10,9},{11,1... | collective-permute-start | bytes 110600 | tf_op jit(solution)/shard_map/ppermute | solution.py:29
  176.0 7.7 %collective-permute-start.6 = (f32[8,1,1152]{2,1,0:T(1,128)S(1)}, f32[8,1,1152]{2,1,0:T(1,128)S(1)}, u32[]{:S(2)}, u32[]{:S(2)}) collective-permute-start(f32[8,1,1152]{2,1,0:T(1,128)S(1)} %get-tuple-element.28), channel_id=1, source_target_pairs={{0,1},{1,2},{2,3},{3,4},{4,5},{5,6},{6,7},{7,8},{8,9},{9,10},{10,1... | collective-permute-start | bytes 110600 | tf_op jit(solution)/shard_map/ppermute | solution.py:26
  186.6 9.9 %collective-permute-start.12 = (f32[1,48,1152]{2,1,0:T(8,128)S(1)}, f32[1,48,1152]{2,1,0:T(8,128)S(1)}, u32[]{:S(2)}, u32[]{:S(2)}) collective-permute-start(f32[1,48,1152]{2,1,0:T(8,128)S(1)} %get-tuple-element.18), channel_id=1, source_target_pairs={{0,8},{1,9},{2,10},{3,11},{4,12},{5,13},{6,14},{7,15},{8,0},{9,1},... | collective-permute-start | bytes 663560 | tf_op jit(solution)/shard_map/ppermute | solution.py:37
  187.5 9.0 %collective-permute-start.13 = (f32[1,48,1152]{2,1,0:T(8,128)S(1)}, f32[1,48,1152]{2,1,0:T(8,128)S(1)}, u32[]{:S(2)}, u32[]{:S(2)}) collective-permute-start(f32[1,48,1152]{2,1,0:T(8,128)S(1)} %get-tuple-element.17), channel_id=1, source_target_pairs={{16,0},{32,16},{48,32},{64,48},{80,64},{96,80},{112,96},{17,1},{33... | collective-permute-start | bytes 663560 | tf_op jit(solution)/shard_map/ppermute | solution.py:29
  188.8 9.7 %collective-permute-start.14 = (f32[1,48,1152]{2,1,0:T(8,128)S(1)}, f32[1,48,1152]{2,1,0:T(8,128)S(1)}, u32[]{:S(2)}, u32[]{:S(2)}) collective-permute-start(f32[1,48,1152]{2,1,0:T(8,128)S(1)} %get-tuple-element.19), channel_id=1, source_target_pairs={{0,16},{16,32},{32,48},{48,64},{64,80},{80,96},{96,112},{1,17},{17... | collective-permute-start | bytes 663560 | tf_op jit(solution)/shard_map/ppermute | solution.py:26
  193.8 5.1 %collective-permute-start.10 = (f32[8,1,1152]{2,1,0:T(1,128)S(1)}, f32[8,1,1152]{2,1,0:T(1,128)S(1)}, u32[]{:S(2)}, u32[]{:S(2)}) collective-permute-start(f32[8,1,1152]{2,1,0:T(1,128)S(1)} %get-tuple-element.20), channel_id=1, source_target_pairs={{1,0},{2,1},{3,2},{4,3},{5,4},{6,5},{7,6},{8,7},{9,8},{10,9},{11,1... | collective-permute-start | bytes 110600 | tf_op jit(solution)/shard_map/ppermute | solution.py:29
  194.1 9.0 %collective-permute-start.11 = (f32[8,1,1152]{2,1,0:T(1,128)S(1)}, f32[8,1,1152]{2,1,0:T(1,128)S(1)}, u32[]{:S(2)}, u32[]{:S(2)}) collective-permute-start(f32[8,1,1152]{2,1,0:T(1,128)S(1)} %get-tuple-element.21), channel_id=1, source_target_pairs={{0,1},{1,2},{2,3},{3,4},{4,5},{5,6},{6,7},{7,8},{8,9},{9,10},{10,1... | collective-permute-start | bytes 110600 | tf_op jit(solution)/shard_map/ppermute | solution.py:26
  206.0 12.1 %collective-permute-start.17 = (f32[1,48,1152]{2,1,0:T(8,128)S(1)}, f32[1,48,1152]{2,1,0:T(8,128)S(1)}, u32[]{:S(2)}, u32[]{:S(2)}) collective-permute-start(f32[1,48,1152]{2,1,0:T(8,128)S(1)} %get-tuple-element.11), channel_id=1, source_target_pairs={{0,8},{1,9},{2,10},{3,11},{4,12},{5,13},{6,14},{7,15},{8,0},{9,1},... | collective-permute-start | bytes 663560 | tf_op jit(solution)/shard_map/ppermute | solution.py:37
  208.0 10.2 %collective-permute-start.18 = (f32[1,48,1152]{2,1,0:T(8,128)S(1)}, f32[1,48,1152]{2,1,0:T(8,128)S(1)}, u32[]{:S(2)}, u32[]{:S(2)}) collective-permute-start(f32[1,48,1152]{2,1,0:T(8,128)S(1)} %get-tuple-element.10), channel_id=1, source_target_pairs={{16,0},{32,16},{48,32},{64,48},{80,64},{96,80},{112,96},{17,1},{33... | collective-permute-start | bytes 663560 | tf_op jit(solution)/shard_map/ppermute | solution.py:29
  209.2 8.9 %collective-permute-start.19 = (f32[1,48,1152]{2,1,0:T(8,128)S(1)}, f32[1,48,1152]{2,1,0:T(8,128)S(1)}, u32[]{:S(2)}, u32[]{:S(2)}) collective-permute-start(f32[1,48,1152]{2,1,0:T(8,128)S(1)} %get-tuple-element.12), channel_id=1, source_target_pairs={{0,16},{16,32},{32,48},{48,64},{64,80},{80,96},{96,112},{1,17},{17... | collective-permute-start | bytes 663560 | tf_op jit(solution)/shard_map/ppermute | solution.py:26
  214.3 4.3 %collective-permute-start.15 = (f32[8,1,1152]{2,1,0:T(1,128)S(1)}, f32[8,1,1152]{2,1,0:T(1,128)S(1)}, u32[]{:S(2)}, u32[]{:S(2)}) collective-permute-start(f32[8,1,1152]{2,1,0:T(1,128)S(1)} %get-tuple-element.13), channel_id=1, source_target_pairs={{1,0},{2,1},{3,2},{4,3},{5,4},{6,5},{7,6},{8,7},{9,8},{10,9},{11,1... | collective-permute-start | bytes 110600 | tf_op jit(solution)/shard_map/ppermute | solution.py:29
  215.2 8.2 %collective-permute-start.16 = (f32[8,1,1152]{2,1,0:T(1,128)S(1)}, f32[8,1,1152]{2,1,0:T(1,128)S(1)}, u32[]{:S(2)}, u32[]{:S(2)}) collective-permute-start(f32[8,1,1152]{2,1,0:T(1,128)S(1)} %get-tuple-element.14), channel_id=1, source_target_pairs={{0,1},{1,2},{2,3},{3,4},{4,5},{5,6},{6,7},{7,8},{8,9},{9,10},{10,1... | collective-permute-start | bytes 110600 | tf_op jit(solution)/shard_map/ppermute | solution.py:26
  (30 other events, 199.4 us)
Sparse Core Ops, SparseCore 0:
  229.8 154.8 all-reduce.2
where the time goes:
time: 401 us; the launch traced here: 393 us
  waiting for transfers between devices  179 us (45%)
  local copies, waits for them, and re-layouts  124 us (31%)
  starting transfers between devices  42.1 us (10%)
  between operations  21.8 us (5%)
  other arithmetic  21.7 us (5%)
  matrix products  4.13 us (1%)
    psum x1, waiting for transfers between devices, shards(): lax.psum(lax.dot_general(flat_basis, weighted, (((0,), (0,)), ((), ())),...  155 us
    ppermute x8, starting transfers between devices, with_halo(): lax.ppermute(lax.slice_in_dim(block, block.shape[dim] - width, None, axis...  19.4 us
    ppermute x8, waiting for transfers between devices, with_halo(): lax.ppermute(lax.slice_in_dim(block, block.shape[dim] - width, None, axis...  18.4 us
    max x4, local copies, waits for them, and re-layouts, update(): jnp.maximum(wind_east, 0.0) * (east_side - state_now)  17.2 us
    max x4, local copies, waits for them, and re-layouts, update(): jnp.maximum(-wind_north, 0.0) * (south_side - state_now)  17 us
    max x4, local copies, waits for them, and re-layouts, update(): jnp.maximum(wind_north, 0.0) * (north_side - state_now)  16.9 us
    max x4, local copies, waits for them, and re-layouts, update(): jnp.maximum(-wind_east, 0.0) * (west_side - state_now)  16.8 us
    another operation x8, local copies, waits for them, and re-layouts, select_winds(): wind_north = jnp.tile(chosen[:, :, 1], (1, 1, VEC * TR))  16.6 us
  transfers between devices with their start and end apart: 21, of which 11 were waited for; matrix products, arithmetic and copies ran while one was open for 29% of the time, Pallas kernels for 0%

commit v1 on v0

v1 whole, which is shorter than its diff:
```python
import functools
import math

import jax
import jax.numpy as jnp
import numpy as np
from jax import lax
from jax.experimental import pallas as pl
from jax.experimental.pallas import tpu as pltpu
from jax.sharding import PartitionSpec as P

LEV = 72
TR = 2
VEC = 8
POOL = 8
NSLAB = 2
STEPS = 4
DIFFUSE = 0.075
ALL = ("lat", "lon")

ROWS = 8
COLS = 48
CH = VEC * TR * LEV
GROUP = TR * LEV
WCH = NSLAB * 2 * LEV
D = STEPS
EXT = ROWS + 2 * D
PITCH = 80
FIRST = 16
SPAN = 64
WPACK = 896
BLOCK = 88


def place(x, y, z, core):
    return (x * 2 + y % 2) * 16 + (y // 2) * 8 + z * 2 + core


PLACES = [(x, y, z, c) for x in range(4) for y in range(4) for z in range(4) for c in range(2)]


def moved(dx=0, dy=0, dz=0, dc=0):
    return [
        (place(x, y, z, c), place((x + dx) % 4, (y + dy) % 4, (z + dz) % 4, c ^ dc))
        for x, y, z, c in PLACES
    ]


def meridian():
    pairs = []
    for b in range(8):
        for a in range(8):
            pairs.append((a * 16 + b, (a + 1) * 16 + b if a < 7 else a * 16 + b + 8))
            pairs.append((a * 16 + b + 8, (a - 1) * 16 + b + 8 if a > 0 else a * 16 + b))
    return pairs


FORWARD = meridian()
OVER = [(b, b + 8) for b in range(8)] + [(7 * 16 + b + 8, 7 * 16 + b) for b in range(8)]
BACKWARD = [(t, s) for s, t in FORWARD if (t, s) not in OVER]
OVER_FIRST = [(b, 16 + b + 8) for b in range(8)] + [(7 * 16 + b + 8, 6 * 16 + b) for b in range(8)]
OVER_SECOND = [(16 + b + 8, b + 8) for b in range(8)] + [(6 * 16 + b, 7 * 16 + b) for b in range(8)]
EASTWARD = [(b, (b + 1) % 16) for b in range(16)]
WESTWARD = [(t, s) for s, t in EASTWARD]


def along_meridian(to_next, to_last):
    before = lax.ppermute(to_next, ALL, FORWARD)
    over = lax.ppermute(to_last, ALL, OVER_FIRST)
    after = lax.ppermute(to_last, ALL, BACKWARD)
    return before, after, lax.ppermute(over, ALL, OVER_SECOND)


def pack_kernel(info, vec_ids, pool, winds, low, high, wind, to_next, to_last, chosen):
    lane = lax.broadcasted_iota(jnp.int32, (1, CH), 1)
    source = lane
    for k in range(VEC):
        inside = (lane >= k * GROUP) & (lane < (k + 1) * GROUP)
        source = jnp.where(inside, lane + (vec_ids[k] - k) * GROUP, source)
    for i in range(CH // 128):
        row = lax.broadcasted_iota(jnp.int32, (128, CH), 0) + i * 128
        chosen[i * 128 : (i + 1) * 128, :] = jnp.where(row == source, 1.0, 0.0).astype(jnp.bfloat16)
    for half in range(2):
        rows = pool[half * 4 : half * 4 + 4].reshape(4 * COLS, CH)
        picked = jnp.dot(rows, chosen[...], preferred_element_type=jnp.float32)
        picked = picked.reshape(4, COLS, CH)

        @pl.when(info[0] == 0)
        def _():
            (low, high)[half][...] = picked

        @pl.when(info[0] != 0)
        def _():
            for r in range(4):
                (high, low)[half][3 - r] = picked[r]

    place_in_slab = lax.rem(lax.broadcasted_iota(jnp.int32, (1, WCH), 1), 2 * LEV)
    turn = jnp.where((place_in_slab >= LEV) & (info[0] != 0), -1.0, 1.0)
    for r in range(ROWS):
        own = jnp.where(info[0] == 0, r, ROWS - 1 - r)
        line = winds[own] * turn
        wind[r] = line
        if r < 3:
            to_last[:, r * WCH : (r + 1) * WCH] = line
        if r >= ROWS - 3:
            to_next[:, (r - ROWS + 3) * WCH : (r - ROWS + 4) * WCH] = line


def pack(info, vec_ids, pool, winds):
    shapes = [(4, COLS, CH), (4, COLS, CH), (ROWS, COLS, WCH), (COLS, WPACK), (COLS, WPACK)]
    return pl.pallas_call(
        pack_kernel,
        out_shape=[jax.ShapeDtypeStruct(s, jnp.float32) for s in shapes],
        in_specs=[pl.BlockSpec(memory_space=pltpu.SMEM)] * 2
        + [pl.BlockSpec(memory_space=pltpu.VMEM)] * 2,
        out_specs=[pl.BlockSpec(memory_space=pltpu.VMEM)] * 5,
        scratch_shapes=[pltpu.VMEM((CH, CH), jnp.bfloat16)],
        compiler_params=pltpu.CompilerParams(vmem_limit_bytes=40 << 20),
        cost_estimate=pl.CostEstimate(flops=1 << 30, bytes_accessed=4 << 20, transcendentals=0),
        name="pack",
    )(info, vec_ids, pool, winds)


def main_kernel(
    info, wind_ids, cosine, south, low, high, north, over, west, east,
    wind_south, wind, wind_north, wind_over, wind_west, wind_east,
    levels, mix, basis_main, basis_rest,
    out, mine, theirs,
    state_a, state_b, wind_ext, spread, weighted, gram, rest,
):
    flip, mx, my, mz, mc, is_over, turn_west, turn_east = (info[i] for i in range(8))
    inner = slice(FIRST, FIRST + COLS)

    for r in range(4):
        state_a[r, inner] = south[r]
        state_a[4 + r, inner] = low[r]
        state_a[8 + r, inner] = high[r]

    @pl.when(is_over == 0)
    def _():
        for r in range(4):
            state_a[12 + r, inner] = north[r]

    @pl.when(is_over != 0)
    def _():
        for r in range(4):
            state_a[12 + r, inner] = over[r]

    for r in range(EXT):
        from_west = jnp.where(turn_west == 0, r, EXT - 1 - r)
        from_east = jnp.where(turn_east == 0, r, EXT - 1 - r)
        state_a[r, FIRST - 4 : FIRST] = west[from_west]
        state_a[r, FIRST + COLS : FIRST + COLS + 4] = east[from_east]

    for r in range(3):
        lanes = slice(r * WCH, (r + 1) * WCH)
        wind_ext[r, 8 : 8 + COLS] = wind_south[:, lanes]
        after = jnp.where(is_over == 0, wind_north[:, lanes], wind_over[:, lanes])
        wind_ext[11 + r, 8 : 8 + COLS] = after
    for r in range(ROWS):
        wind_ext[3 + r, 8 : 8 + COLS] = wind[r]
    lane = lax.rem(lax.broadcasted_iota(jnp.int32, (1, WCH), 1), 2 * LEV)
    for r in range(EXT - 2):
        from_west = jnp.where(turn_west == 0, r, EXT - 3 - r)
        from_east = jnp.where(turn_east == 0, r, EXT - 3 - r)
        sign_west = jnp.where((lane >= LEV) & (turn_west != 0), -1.0, 1.0)
        sign_east = jnp.where((lane >= LEV) & (turn_east != 0), -1.0, 1.0)
        wind_ext[r, 4:8] = wind_west[from_west] * sign_west
        wind_ext[r, 8 + COLS : 12 + COLS] = wind_east[from_east] * sign_east

    level = lax.broadcasted_iota(jnp.int32, (2 * LEV, CH), 0)
    level = jnp.where(level >= LEV, level - LEV, level)
    repeat = jnp.where(level == levels[...], 1.0, 0.0).astype(jnp.bfloat16)
    flat = wind_ext[...].reshape((EXT - 2) * SPAN, WCH)
    for i in range(2 * NSLAB):
        value = flat[:, i * LEV : (i + 1) * LEV]
        coarse = value.astype(jnp.bfloat16)
        fine = (value - coarse.astype(jnp.float32)).astype(jnp.bfloat16)
        both = jnp.concatenate([coarse, fine], axis=1)
        spread[i] = jnp.dot(both, repeat, preferred_element_type=jnp.float32).reshape(
            EXT - 2, SPAN, CH
        )

    up, down = mix[0:1, :], mix[1:2, :]

    def updated(source, slab, r, c):
        now = source[r, pl.ds(c, 8), :]
        after = source[r + 1, pl.ds(c, 8), :]
        before = source[r - 1, pl.ds(c, 8), :]
        east_side = source[r, pl.ds(c + 1, 8), :]
        west_side = source[r, pl.ds(c - 1, 8), :]
        u = spread[2 * slab, r - 1, pl.ds(c - FIRST + 8, 8), :]
        v = spread[2 * slab + 1, r - 1, pl.ds(c - FIRST + 8, 8), :]
        gain_east = jnp.maximum(u, 0.0) + DIFFUSE
        gain_after = jnp.maximum(v, 0.0) + DIFFUSE
        change = gain_east * (east_side - now) + (gain_east - u) * (west_side - now)
        change += gain_after * (after - now) + (gain_after - v) * (before - now)
        change += up * (pltpu.roll(now, CH - 1, 1) - now) - down * (now - pltpu.roll(now, 1, 1))
        return now + change

    buffers = (state_a, state_b)
    for step in range(STEPS - 1):
        source, target = buffers[step % 2], buffers[(step + 1) % 2]
        slab = wind_ids[step]

        def body(r, carry):
            for c in range(FIRST - 8, FIRST - 8 + SPAN, 8):
                target[r, c : c + 8, :] = updated(source, slab, r, c)
            return carry

        lax.fori_loop(1 + step, EXT - 1 - step, body, 0)

    source = buffers[(STEPS - 1) % 2]
    slab = wind_ids[STEPS - 1]

    def last(r, carry):
        own = jnp.where(flip == 0, r - D, ROWS - 1 - (r - D))
        share = cosine[own]
        for c in range(0, COLS, 16):
            first = updated(source, slab, r, FIRST + c)
            second = updated(source, slab, r, FIRST + c + 8)
            out[own, c : c + 8, :] = first
            out[own, c + 8 : c + 16, :] = second
            both = jnp.concatenate([first, second], axis=0) * share
            weighted[own, c : c + 16, :] = both.astype(jnp.bfloat16)
        return carry

    lax.fori_loop(D, D + ROWS, last, 0)

    flat_weighted = weighted[...].reshape(ROWS * COLS, CH)
    across = (((0,), (0,)), ((), ()))
    for i in range(CH // 128):
        gram[i * 128 : (i + 1) * 128, :] = lax.dot_general(
            flat_weighted[:, i * 128 : (i + 1) * 128],
            basis_main[...],
            across,
            preferred_element_type=jnp.float32,
        )
    tail = lax.dot_general(
        basis_rest[...], flat_weighted, across, preferred_element_type=jnp.float32
    )
    for g in range(VEC * TR):
        rest[g, :, :LEV] = tail[:, g * LEV : (g + 1) * LEV]

    def place_blocks(i, carry):
        rz, rx, ry = i // 16, (i // 4) % 4, i % 4
        z, x, y = (mz + rz) % 4, (mx + rx) % 4, (my + ry) % 4
        at_first = (rz * 2 + rx // 2) * 4 + (rx % 2) * 2 + ry % 2
        at_second = (rx * 2 + rz // 2) * 4 + (rz % 2) * 2 + ry % 2
        at = jnp.where(ry < 2, at_first, at_second)
        a = x * 2 + y % 2
        for dc, target in ((0, mine), (1, theirs)):
            g = (y // 2) * 8 + z * 2 + (mc ^ dc)
            target[ry // 2, at, :LEV] = gram[
                pl.ds(pl.multiple_of(g * LEV, 8), LEV), pl.ds(pl.multiple_of(a * 128, 128), 128)
            ]
            target[ry // 2, at, LEV:] = rest[g, pl.ds(pl.multiple_of(a * 16, 16), 16), :]
        return carry

    lax.fori_loop(0, 64, place_blocks, 0)


def main(scalars, arrays):
    blocks = jax.ShapeDtypeStruct((2, 32, BLOCK, 128), jnp.float32)
    vmem = pl.BlockSpec(memory_space=pltpu.VMEM)
    return pl.pallas_call(
        main_kernel,
        out_shape=[jax.ShapeDtypeStruct((ROWS, COLS, CH), jnp.float32), blocks, blocks],
        in_specs=[pl.BlockSpec(memory_space=pltpu.SMEM)] * len(scalars) + [vmem] * len(arrays),
        out_specs=[vmem] * 3,
        scratch_shapes=[
            pltpu.VMEM((EXT, PITCH, CH), jnp.float32),
            pltpu.VMEM((EXT, PITCH, CH), jnp.float32),
            pltpu.VMEM((EXT - 2, SPAN, WCH), jnp.float32),
            pltpu.VMEM((2 * NSLAB, EXT - 2, SPAN, CH), jnp.float32),
            pltpu.VMEM((ROWS, COLS, CH), jnp.bfloat16),
            pltpu.VMEM((CH, 1024), jnp.float32),
            pltpu.VMEM((VEC * TR, 128, 128), jnp.float32),
        ],
        compiler_params=pltpu.CompilerParams(vmem_limit_bytes=60 << 20),
        cost_estimate=pl.CostEstimate(flops=4 << 30, bytes_accessed=16 << 20, transcendentals=0),
        name="window",
    )(*scalars, *arrays)


def ring_sum(parts, up, down):
    from_below = lax.ppermute(parts[3:5], ALL, up)
    from_above = lax.ppermute(parts[5:7], ALL, down)
    last_below = lax.ppermute(parts[2] + from_below[1], ALL, up)
    last_above = lax.ppermute(parts[7] + from_above[0], ALL, down)
    return jnp.stack(
        [parts[0] + from_above[1] + last_below, parts[1] + from_below[0] + last_above]
    )


def shards(pool, vec_ids, winds, wind_ids, mixing, basis):
    lat_index = lax.axis_index("lat").astype(jnp.int32)
    lon_index = lax.axis_index("lon").astype(jnp.int32)
    flip = lon_index // 8
    is_over = ((lat_index == 0) & (flip == 1)) | ((lat_index == 7) & (flip == 0))
    info = jnp.stack(
        [
            flip,
            lat_index // 2,
            flip * 2 + lat_index % 2,
            (lon_index // 2) % 4,
            lon_index % 2,
            is_over.astype(jnp.int32),
            (lon_index % 8 == 0).astype(jnp.int32),
            (lon_index % 8 == 7).astype(jnp.int32),
        ]
    )
    low, high, wind, wind_up, wind_down = pack(info, vec_ids, pool, winds)

    wind_south, wind_north, wind_over = along_meridian(wind_up, wind_down)
    south, north, over = along_meridian(high, low)

    crossed = info[5] != 0
    wind_after = jnp.where(crossed, wind_over, wind_north)

    def wind_edge(columns):
        count = 4
        before = wind_south[columns, : 3 * WCH].reshape(count, 3, WCH).transpose(1, 0, 2)
        after = wind_after[columns, : 3 * WCH].reshape(count, 3, WCH).transpose(1, 0, 2)
        return jnp.concatenate([before, wind[:, columns], after], axis=0)

    wind_west = lax.ppermute(wind_edge(slice(COLS - 4, COLS)), "lon", EASTWARD)
    wind_east = lax.ppermute(wind_edge(slice(0, 4)), "lon", WESTWARD)

    def edge(columns):
        after = jnp.where(crossed, over[:, columns], north[:, columns])
        return jnp.concatenate([south[:, columns], low[:, columns], high[:, columns], after], axis=0)

    west = lax.ppermute(edge(slice(COLS - 4, COLS)), "lon", EASTWARD)
    east = lax.ppermute(edge(slice(0, 4)), "lon", WESTWARD)

    level_mix = jnp.concatenate(
        [mixing.reshape(TR, LEV - 1), jnp.zeros((TR, 1), mixing.dtype)], axis=1
    )
    upper = jnp.tile(level_mix.reshape(GROUP), VEC)
    mix = jnp.stack([upper, jnp.roll(upper, 1)])
    levels = jnp.asarray(np.arange(CH, dtype=np.int32)[None] % LEV)
    rows = (jnp.arange(ROWS, dtype=jnp.int32) + lat_index * ROWS).astype(jnp.float32)
    cosine = jnp.cos((rows + 0.5) * (math.pi / (ROWS * 8)) - math.pi / 2)
    grouped = basis.reshape(ROWS * COLS, 8, 144)
    basis_main = grouped[:, :, :128].reshape(ROWS * COLS, 1024)
    basis_rest = grouped[:, :, 128:].reshape(ROWS * COLS, 128)

    sensitivity, mine, theirs = main(
        (info, wind_ids, cosine),
        (
            south, low, high, north, over, west, east,
            wind_south, wind, wind_north, wind_over, wind_west, wind_east,
            levels, mix, basis_main, basis_rest,
        ),
    )

    total = mine + lax.ppermute(theirs, ALL, moved(dc=1))
    z_up, z_down, x_up, x_down = moved(dz=1), moved(dz=-1), moved(dx=1), moved(dx=-1)
    first = ring_sum(total[0].reshape(8, 4, BLOCK, 128), z_up, z_down)
    second = ring_sum(total[1].reshape(8, 4, BLOCK, 128), x_up, x_down)
    first = ring_sum(first.reshape(8, BLOCK, 128), x_up, x_down)
    second = ring_sum(second.reshape(8, BLOCK, 128), z_up, z_down)
    block = first[0] + lax.ppermute(first[1], ALL, moved(dy=1))
    block += lax.ppermute(second[0], ALL, moved(dy=2)) + lax.ppermute(second[1], ALL, moved(dy=3))
    ritz = jnp.concatenate([block[:LEV].T, block[LEV:, :LEV]], axis=0)
    return sensitivity, ritz * (1.0 / math.sqrt(ROWS * COLS * 128))


def solution(mesh):
    in_specs = (P("lat", "lon", None), P(), P("lat", "lon", None), P(), P(), P("lat", "lon", None))
    out_specs = (P("lat", "lon", None), P("lat", "lon"))
    return jax.shard_map(shards, mesh=mesh, in_specs=in_specs, out_specs=out_specs, check_vma=False)
```

time: 401 us -> 183 us (0.46); the launches traced: 393 us -> 182 us
  waiting for transfers between devices: 179 us -> 54.5 us
  local copies, waits for them, and re-layouts: 124 us -> 19.1 us
  Pallas kernels: 0 us -> 33.4 us
  starting transfers between devices: 42.1 us -> 66.7 us
  between operations: 21.8 us -> 1.12 us
  other arithmetic: 21.7 us -> 7.24 us
  matrix products: 4.13 us -> 0 us
    psum x1 -> x0, waiting for transfers between devices: 155 us -> none  [shards(): lax.psum(lax.dot_general(flat_basis, weighted, (((0,), (0,)), ((), ())),...]
    max x16 -> x0, local copies, waits for them, and re-layouts: 67.9 us -> none  [the longest x4 17.2 us: update(): jnp.maximum(wind_east, 0.0) * (east_side - state_now)]
    pallas_call x0 -> x2, Pallas kernels: none -> 33.4 us  [the longest x1 31 us: main(): pl.pallas_call(main_kernel, out_shape=[jax.ShapeDtypeStruct((ROWS, COLS,...]
    another operation x18 -> x6, local copies, waits for them, and re-layouts: 33.3 us -> 0.35 us  [the longest x3 0.17 us: shards(): upper = jnp.tile(level_mix.reshape(GROUP), VEC)]
    ppermute x20 -> x32, waiting for transfers between devices: 24.2 us -> 54.5 us  [the longest x2 24.3 us: along_meridian(): before = lax.ppermute(to_next, ALL, FORWARD)]
    ppermute x20 -> x32, starting transfers between devices: 42.1 us -> 66.7 us  [the longest x1 17 us: shards(): east = lax.ppermute(edge(slice(0, 4)), 'lon', WESTWARD)]
    add x4 -> x7, other arithmetic: 12.3 us -> 2.26 us  [the longest x1 2.1 us: shards(): total = mine + lax.ppermute(theirs, ALL, moved(dc=1))]
    gather x3 -> x0, local copies, waits for them, and re-layouts: 6.92 us -> none  [shards(): jnp.take(grouped, vec_ids, axis=2).reshape(tile_rows, tile_cols, channels)]
  transfers between devices with their start and end apart: 21 -> 32, of which waited for: 11 -> 16; matrix products, arithmetic and copies ran while one was open for 29% -> 11% of each run, Pallas kernels for 0% -> 0%
where the time goes in v1:
time: 183 us; the launch traced here: 182 us
  starting transfers between devices  66.7 us (36%)
  waiting for transfers between devices  54.5 us (30%)
  Pallas kernels  33.4 us (18%)
  local copies, waits for them, and re-layouts  19.1 us (10%)
  other arithmetic  7.24 us (4%)
    pallas_call x1, Pallas kernels, main(): pl.pallas_call(main_kernel, out_shape=[jax.ShapeDtypeStruct((ROWS, COLS,...  31 us
    ppermute x2, waiting for transfers between devices, along_meridian(): before = lax.ppermute(to_next, ALL, FORWARD)  24.3 us
    ppermute x1, starting transfers between devices, shards(): east = lax.ppermute(edge(slice(0, 4)), 'lon', WESTWARD)  17 us
    ppermute x4, starting transfers between devices, ring_sum(): from_above = lax.ppermute(parts[5:7], ALL, down)  11.1 us
    ppermute x4, starting transfers between devices, ring_sum(): last_above = lax.ppermute(parts[7] + from_above[0], ALL, down)  10.1 us
    ppermute x2, starting transfers between devices, along_meridian(): over = lax.ppermute(to_last, ALL, OVER_FIRST)  9.96 us
    unnamed x35, local copies, waits for them, and re-layouts  5.94 us
    ppermute x1, waiting for transfers between devices, shards(): total = mine + lax.ppermute(theirs, ALL, moved(dc=1))  5.49 us
  transfers between devices with their start and end apart: 32, of which 16 were waited for; matrix products, arithmetic and copies ran while one was open for 11% of the time, Pallas kernels for 0%

profile of v1, /device:TPU:0, one launch (start us, length us, event | category | flops | bytes accessed | tf_op | source)
XLA Modules:
  0.0 182.1 jit_solution(15109359070672616036)
XLA Ops:
  3.7 2.5 %pack.1 = (f32[4,48,1152]{2,1,0:T(8,128)S(1)}, f32[4,48,1152]{2,1,0:T(8,128)S(1)}, f32[8,48,288]{2,1,0:T(8,128)S(1)}, f32[48,896]{1,0:T(8,128)S(1)}, f32[48,896]{1,0:T(8,128)S(1)}) custom-call(s32[8]{0:T(128)S(1)} %stack.67.info, s32[8]{0:T(128)S(1)} %copy-done.6, bf16[8,48,1152]{2,1,0:T(8,128)(2,1)S(1)} %copy-done.4, f32[8,48,288]{2,1,0:T(8,128)S(1)} %copy-done.5), custom_call_target="tpu_custom_call" | custom-call | flops 1073741824 | bytes 4194304 | tf_op jit(solution)/shard_map/pack/pallas_call | solution.py:111
  6.2 5.7 %collective-permute-start.8 = (f32[48,896]{1,0:T(8,128)S(1)}, f32[48,896]{1,0:T(8,128)}, u32[]{:S(2)}, u32[]{:S(2)}) collective-permute-start(f32[48,896]{1,0:T(8,128)S(1)} %get-tuple-element.14), channel_id=1, source_target_pairs={{0,24},{1,25},{2,26},{3,27},{4,28},{5,29},{6,30},{7,31},{120,96},{... | collective-permute-start | bytes 516104 | tf_op jit(solution)/shard_map/ppermute | solution.py:69
  13.2 2.7 %collective-permute-start.6 = (f32[48,896]{1,0:T(8,128)S(1)}, f32[48,896]{1,0:T(8,128)}, u32[]{:S(2)}, u32[]{:S(2)}) collective-permute-start(f32[48,896]{1,0:T(8,128)S(1)} %get-tuple-element.12), channel_id=1, source_target_pairs={{0,16},{8,0},{16,32},{24,8},{32,48},{40,24},{48,64},{56,40},{64,80... | collective-permute-start | bytes 516104 | tf_op jit(solution)/shard_map/ppermute | solution.py:68
  16.0 4.2 %collective-permute-start.2 = (f32[4,48,1152]{2,1,0:T(8,128)S(1)}, f32[4,48,1152]{2,1,0:T(8,128)}, u32[]{:S(2)}, u32[]{:S(2)}) collective-permute-start(f32[4,48,1152]{2,1,0:T(8,128)S(1)} %get-tuple-element.11.low), channel_id=1, source_target_pairs={{0,24},{1,25},{2,26},{3,27},{4,28},{5,29},{6,30},{7,31},{120,96},{... | collective-permute-start | bytes 2654216 | tf_op jit(solution)/shard_map/ppermute | solution.py:69
  20.6 4.0 %reshape.76 = bf16[384,8,144]{2,1,0:T(8,128)(2,1)} reshape(bf16[8,48,1152]{2,1,0:T(8,128)(2,1)} %param.12) | data formatting | bytes 1769472 | tf_op jit(solution)/shard_map/reshape | solution.py:345
  34.4 11.3 %collective-permute-done.6.wind_south = f32[48,896]{1,0:T(8,128)} collective-permute-done((f32[48,896]{1,0:T(8,128)S(1)}, f32[48,896]{1,0:T(8,128)}, u32[]{:S(2)}, u32[]{:S(2)}) %collective-permute-start.6) | collective-permute-done | bytes 172064 | tf_op jit(solution)/shard_map/ppermute | solution.py:68
  51.6 13.1 %collective-permute-done.south = f32[4,48,1152]{2,1,0:T(8,128)} collective-permute-done((f32[4,48,1152]{2,1,0:T(8,128)S(1)}, f32[4,48,1152]{2,1,0:T(8,128)}, u32[]{:S(2)}, u32[]{:S(2)}) %collective-permute-start) | collective-permute-done | bytes 884768 | tf_op jit(solution)/shard_map/ppermute | solution.py:68
  68.5 17.0 %collective-permute-start.5 = (f32[16,4,1152]{2,1,0:T(4,128)S(1)}, f32[16,4,1152]{2,1,0:T(4,128)S(1)}, u32[]{:S(2)}, u32[]{:S(2)}) collective-permute-start(f32[16,4,1152]{2,1,0:T(4,128)S(1)} %pad_maximum_fusion.3), channel_id=1, source_target_pairs={{1,0},{2,1},{3,2},{4,3},{5,4},{6,5},{7,6},{8,7},{9,8},{10,9},{11,1... | collective-permute-start | bytes 884744 | tf_op jit(solution)/shard_map/ppermute | solution.py:335
  85.5 2.7 %collective-permute-start.11 = (f32[14,4,288]{2,1,0:T(4,128)S(1)}, f32[14,4,288]{2,1,0:T(4,128)S(1)}, u32[]{:S(2)}, u32[]{:S(2)}) collective-permute-start(f32[14,4,288]{2,1,0:T(4,128)S(1)} %pad_maximum_fusion.5), channel_id=1, source_target_pairs={{1,0},{2,1},{3,2},{4,3},{5,4},{6,5},{7,6},{8,7},{9,8},{10,9},{11,1... | collective-permute-start | bytes 193544 | tf_op jit(solution)/shard_map/ppermute | solution.py:328
  91.5 31.0 %window.1 = (f32[8,48,1152]{2,1,0:T(8,128)}, f32[2,32,88,128]{3,2,1,0:T(8,128)}, f32[2,32,88,128]{3,2,1,0:T(8,128)}) custom-call(s32[8]{0:T(128)} %copy-done.3, s32[4]{0:T(128)} %wind_ids.1, f32[8]{0:T(128)} %add_cosine_fusion.cosine, f32[4,48,1152]{2,1,0:T(8,128)} %collective-permute-done.south, f32[4,48,1152]{2,1,0:T(8,128)} %copy-done, ...), custom_call_target="tpu_custom_call" | custom-call | flops 4294967296 | bytes 16777216 | tf_op jit(solution)/shard_map/window/pallas_call | solution.py:266
  122.5 5.5 %collective-permute-done.12 = f32[2,32,88,128]{3,2,1,0:T(8,128)S(1)} collective-permute-done((f32[2,32,88,128]{3,2,1,0:T(8,128)}, f32[2,32,88,128]{3,2,1,0:T(8,128)S(1)}, u32[]{:S(2)}, u32[]{:S(2)}) %collective-permute-start.12) | collective-permute-done | bytes 2883616 | tf_op jit(solution)/shard_map/ppermute | solution.py:358
  130.1 4.2 %collective-permute-start.22 = (f32[2,4,88,128]{3,2,1,0:T(8,128)S(1)}, f32[2,4,88,128]{3,2,1,0:T(8,128)S(1)}, u32[]{:S(2)}, u32[]{:S(2)}) collective-permute-start(f32[2,4,88,128]{3,2,1,0:T(8,128)S(1)} %bitcast.111), channel_id=1, source_target_pairs={{0,96},{1,97},{2,98},{3,99},{4,100},{5,101},{6,102},{7,103},{16,11... | collective-permute-start | bytes 1081352 | tf_op jit(solution)/shard_map/ppermute | solution.py:288
  134.5 3.6 %collective-permute-start.13 = (f32[2,4,88,128]{3,2,1,0:T(8,128)S(1)}, f32[2,4,88,128]{3,2,1,0:T(8,128)S(1)}, u32[]{:S(2)}, u32[]{:S(2)}) collective-permute-start(f32[2,4,88,128]{3,2,1,0:T(8,128)S(1)} %bitcast.108), channel_id=1, source_target_pairs={{0,6},{1,7},{2,0},{3,1},{4,2},{5,3},{6,4},{7,5},{16,22},{17,23},{1... | collective-permute-start | bytes 1081352 | tf_op jit(solution)/shard_map/ppermute | solution.py:288
  138.1 4.2 %collective-permute-done.22 = f32[2,4,88,128]{3,2,1,0:T(8,128)S(1)} collective-permute-done((f32[2,4,88,128]{3,2,1,0:T(8,128)S(1)}, f32[2,4,88,128]{3,2,1,0:T(8,128)S(1)}, u32[]{:S(2)}, u32[]{:S(2)}) %collective-permute-start.22) | collective-permute-done | bytes 360480 | tf_op jit(solution)/shard_map/ppermute | solution.py:288
  142.3 3.4 %collective-permute-done.23 = f32[2,4,88,128]{3,2,1,0:T(8,128)S(1)} collective-permute-done((f32[2,4,88,128]{3,2,1,0:T(8,128)S(1)}, f32[2,4,88,128]{3,2,1,0:T(8,128)S(1)}, u32[]{:S(2)}, u32[]{:S(2)}) %collective-permute-start.23) | collective-permute-done | bytes 360480 | tf_op jit(solution)/shard_map/ppermute | solution.py:287
  146.9 3.0 %collective-permute-start.25 = (f32[4,88,128]{2,1,0:T(8,128)S(1)}, f32[4,88,128]{2,1,0:T(8,128)S(1)}, u32[]{:S(2)}, u32[]{:S(2)}) collective-permute-start(f32[4,88,128]{2,1,0:T(8,128)S(1)} %get-tuple-element.23), channel_id=1, source_target_pairs={{0,96},{1,97},{2,98},{3,99},{4,100},{5,101},{6,102},{7,103},{16,11... | collective-permute-start | bytes 540680 | tf_op jit(solution)/shard_map/ppermute | solution.py:290
  149.9 3.0 %collective-permute-start.16 = (f32[4,88,128]{2,1,0:T(8,128)S(1)}, f32[4,88,128]{2,1,0:T(8,128)S(1)}, u32[]{:S(2)}, u32[]{:S(2)}) collective-permute-start(f32[4,88,128]{2,1,0:T(8,128)S(1)} %get-tuple-element.24), channel_id=1, source_target_pairs={{0,6},{1,7},{2,0},{3,1},{4,2},{5,3},{6,4},{7,5},{16,22},{17,23},{1... | collective-permute-start | bytes 540680 | tf_op jit(solution)/shard_map/ppermute | solution.py:290
  153.5 2.3 %collective-permute-done.16 = f32[4,88,128]{2,1,0:T(8,128)S(1)} collective-permute-done((f32[4,88,128]{2,1,0:T(8,128)S(1)}, f32[4,88,128]{2,1,0:T(8,128)S(1)}, u32[]{:S(2)}, u32[]{:S(2)}) %collective-permute-start.16) | collective-permute-done | bytes 180256 | tf_op jit(solution)/shard_map/ppermute | solution.py:290
  155.8 3.7 %collective-permute-done.15 = f32[4,88,128]{2,1,0:T(8,128)S(1)} collective-permute-done((f32[4,88,128]{2,1,0:T(8,128)S(1)}, f32[4,88,128]{2,1,0:T(8,128)S(1)}, u32[]{:S(2)}, u32[]{:S(2)}) %collective-permute-start.15) | collective-permute-done | bytes 180256 | tf_op jit(solution)/shard_map/ppermute | solution.py:289
  161.9 3.2 %collective-permute-start.17 = (f32[2,88,128]{2,1,0:T(8,128)S(1)}, f32[2,88,128]{2,1,0:T(8,128)S(1)}, u32[]{:S(2)}, u32[]{:S(2)}) collective-permute-start(f32[2,88,128]{2,1,0:T(8,128)S(1)} %get-tuple-element.49), channel_id=1, source_target_pairs={{0,96},{1,97},{2,98},{3,99},{4,100},{5,101},{6,102},{7,103},{16,11... | collective-permute-start | bytes 270344 | tf_op jit(solution)/shard_map/ppermute | solution.py:288
  168.2 3.3 %collective-permute-start.20 = (f32[88,128]{1,0:T(8,128)S(1)}, f32[88,128]{1,0:T(8,128)S(1)}, u32[]{:S(2)}, u32[]{:S(2)}) collective-permute-start(f32[88,128]{1,0:T(8,128)S(1)} %get-tuple-element.47), channel_id=1, source_target_pairs={{0,96},{1,97},{2,98},{3,99},{4,100},{5,101},{6,102},{7,103},{16,11... | collective-permute-start | bytes 135176 | tf_op jit(solution)/shard_map/ppermute | solution.py:290
  173.3 2.7 %collective-permute-start.29 = (f32[88,128]{1,0:T(8,128)S(1)}, f32[88,128]{1,0:T(8,128)S(1)}, u32[]{:S(2)}, u32[]{:S(2)}) collective-permute-start(f32[88,128]{1,0:T(8,128)S(1)} %get-tuple-element.41), channel_id=1, source_target_pairs={{0,8},{1,9},{2,10},{3,11},{4,12},{5,13},{6,14},{7,15},{16,24},{17,... | collective-permute-start | bytes 135176 | tf_op jit(solution)/shard_map/ppermute | solution.py:365
  176.0 2.8 %collective-permute-done.29 = f32[88,128]{1,0:T(8,128)S(1)} collective-permute-done((f32[88,128]{1,0:T(8,128)S(1)}, f32[88,128]{1,0:T(8,128)S(1)}, u32[]{:S(2)}, u32[]{:S(2)}) %collective-permute-start.29) | collective-permute-done | bytes 45088 | tf_op jit(solution)/shard_map/ppermute | solution.py:365
  178.8 2.5 %collective-permute-done.21 = f32[88,128]{1,0:T(8,128)S(1)} collective-permute-done((f32[88,128]{1,0:T(8,128)S(1)}, f32[88,128]{1,0:T(8,128)S(1)}, u32[]{:S(2)}, u32[]{:S(2)}) %collective-permute-start.21) | collective-permute-done | bytes 45088 | tf_op jit(solution)/shard_map/ppermute | solution.py:364
  (129 shorter events, 39.6 us)
Async XLA Ops:
  6.2 40.8 %collective-permute-start.8 = (f32[48,896]{1,0:T(8,128)S(1)}, f32[48,896]{1,0:T(8,128)}, u32[]{:S(2)}, u32[]{:S(2)}) collective-permute-start(f32[48,896]{1,0:T(8,128)S(1)} %get-tuple-element.14), channel_id=1, source_target_pairs={{0,24},{1,25},{2,26},{3,27},{4,28},{5,29},{6,30},{7,31},{120,96},{... | collective-permute-start | bytes 516104 | tf_op jit(solution)/shard_map/ppermute | solution.py:69
  11.9 36.7 %collective-permute-start.7 = (f32[48,896]{1,0:T(8,128)S(1)}, f32[48,896]{1,0:T(8,128)}, u32[]{:S(2)}, u32[]{:S(2)}) collective-permute-start(f32[48,896]{1,0:T(8,128)S(1)} %get-tuple-element.14), channel_id=1, source_target_pairs={{16,0},{32,16},{8,24},{48,32},{24,40},{64,48},{40,56},{80,64},{56,... | collective-permute-start | bytes 516104 | tf_op jit(solution)/shard_map/ppermute | solution.py:70
  13.2 32.5 %collective-permute-start.6 = (f32[48,896]{1,0:T(8,128)S(1)}, f32[48,896]{1,0:T(8,128)}, u32[]{:S(2)}, u32[]{:S(2)}) collective-permute-start(f32[48,896]{1,0:T(8,128)S(1)} %get-tuple-element.12), channel_id=1, source_target_pairs={{0,16},{8,0},{16,32},{24,8},{32,48},{40,24},{48,64},{56,40},{64,80... | collective-permute-start | bytes 516104 | tf_op jit(solution)/shard_map/ppermute | solution.py:68
  15.9 48.7 %collective-permute-start = (f32[4,48,1152]{2,1,0:T(8,128)S(1)}, f32[4,48,1152]{2,1,0:T(8,128)}, u32[]{:S(2)}, u32[]{:S(2)}) collective-permute-start(f32[4,48,1152]{2,1,0:T(8,128)S(1)} %get-tuple-element.10.high), channel_id=1, source_target_pairs={{0,16},{8,0},{16,32},{24,8},{32,48},{40,24},{48,64},{56,40},{64,80... | collective-permute-start | bytes 2654216 | tf_op jit(solution)/shard_map/ppermute | solution.py:68
  16.0 33.7 %collective-permute-start.2 = (f32[4,48,1152]{2,1,0:T(8,128)S(1)}, f32[4,48,1152]{2,1,0:T(8,128)}, u32[]{:S(2)}, u32[]{:S(2)}) collective-permute-start(f32[4,48,1152]{2,1,0:T(8,128)S(1)} %get-tuple-element.11.low), channel_id=1, source_target_pairs={{0,24},{1,25},{2,26},{3,27},{4,28},{5,29},{6,30},{7,31},{120,96},{... | collective-permute-start | bytes 2654216 | tf_op jit(solution)/shard_map/ppermute | solution.py:69
  45.7 21.3 %collective-permute-start.1 = (f32[4,48,1152]{2,1,0:T(8,128)S(1)}, f32[4,48,1152]{2,1,0:T(8,128)}, u32[]{:S(2)}, u32[]{:S(2)}) collective-permute-start(f32[4,48,1152]{2,1,0:T(8,128)S(1)} %get-tuple-element.11.low), channel_id=1, source_target_pairs={{16,0},{32,16},{8,24},{48,32},{24,40},{64,48},{40,56},{80,64},{56,... | collective-permute-start | bytes 2654216 | tf_op jit(solution)/shard_map/ppermute | solution.py:70
  49.7 17.4 %collective-permute-start.3 = (f32[4,48,1152]{2,1,0:T(8,128)}, f32[4,48,1152]{2,1,0:T(8,128)}, u32[]{:S(2)}, u32[]{:S(2)}) collective-permute-start(f32[4,48,1152]{2,1,0:T(8,128)} %collective-permute-done.2), channel_id=1, source_target_pairs={{24,8},{25,9},{26,10},{27,11},{28,12},{29,13},{30,14},{31,15},{96,... | collective-permute-start | bytes 2654216 | tf_op jit(solution)/shard_map/ppermute | solution.py:71
  51.5 37.2 %collective-permute-start.10 = (f32[14,4,288]{2,1,0:T(4,128)S(1)}, f32[14,4,288]{2,1,0:T(4,128)S(1)}, u32[]{:S(2)}, u32[]{:S(2)}) collective-permute-start(f32[14,4,288]{2,1,0:T(4,128)S(1)} %pad_maximum_fusion.4), channel_id=1, source_target_pairs={{0,1},{1,2},{2,3},{3,4},{4,5},{5,6},{6,7},{7,8},{8,9},{9,10},{10,1... | collective-permute-start | bytes 193544 | tf_op jit(solution)/shard_map/ppermute | solution.py:327
  68.3 22.3 %collective-permute-start.4 = (f32[16,4,1152]{2,1,0:T(4,128)S(1)}, f32[16,4,1152]{2,1,0:T(4,128)S(1)}, u32[]{:S(2)}, u32[]{:S(2)}) collective-permute-start(f32[16,4,1152]{2,1,0:T(4,128)S(1)} %pad_maximum_fusion.2), channel_id=1, source_target_pairs={{0,1},{1,2},{2,3},{3,4},{4,5},{5,6},{6,7},{7,8},{8,9},{9,10},{10,1... | collective-permute-start | bytes 884744 | tf_op jit(solution)/shard_map/ppermute | solution.py:334
  68.5 22.1 %collective-permute-start.5 = (f32[16,4,1152]{2,1,0:T(4,128)S(1)}, f32[16,4,1152]{2,1,0:T(4,128)S(1)}, u32[]{:S(2)}, u32[]{:S(2)}) collective-permute-start(f32[16,4,1152]{2,1,0:T(4,128)S(1)} %pad_maximum_fusion.3), channel_id=1, source_target_pairs={{1,0},{2,1},{3,2},{4,3},{5,4},{6,5},{7,6},{8,7},{9,8},{10,9},{11,1... | collective-permute-start | bytes 884744 | tf_op jit(solution)/shard_map/ppermute | solution.py:335
  130.1 12.2 %collective-permute-start.22 = (f32[2,4,88,128]{3,2,1,0:T(8,128)S(1)}, f32[2,4,88,128]{3,2,1,0:T(8,128)S(1)}, u32[]{:S(2)}, u32[]{:S(2)}) collective-permute-start(f32[2,4,88,128]{3,2,1,0:T(8,128)S(1)} %bitcast.111), channel_id=1, source_target_pairs={{0,96},{1,97},{2,98},{3,99},{4,100},{5,101},{6,102},{7,103},{16,11... | collective-permute-start | bytes 1081352 | tf_op jit(solution)/shard_map/ppermute | solution.py:288
  134.3 11.4 %collective-permute-start.23 = (f32[2,4,88,128]{3,2,1,0:T(8,128)S(1)}, f32[2,4,88,128]{3,2,1,0:T(8,128)S(1)}, u32[]{:S(2)}, u32[]{:S(2)}) collective-permute-start(f32[2,4,88,128]{3,2,1,0:T(8,128)S(1)} %bitcast.110), channel_id=1, source_target_pairs={{0,32},{1,33},{2,34},{3,35},{4,36},{5,37},{6,38},{7,39},{16,48},{1... | collective-permute-start | bytes 1081352 | tf_op jit(solution)/shard_map/ppermute | solution.py:287
  134.3 12.1 %collective-permute-start.14 = (f32[2,4,88,128]{3,2,1,0:T(8,128)S(1)}, f32[2,4,88,128]{3,2,1,0:T(8,128)S(1)}, u32[]{:S(2)}, u32[]{:S(2)}) collective-permute-start(f32[2,4,88,128]{3,2,1,0:T(8,128)S(1)} %bitcast.109), channel_id=1, source_target_pairs={{0,2},{1,3},{2,4},{3,5},{4,6},{5,7},{6,0},{7,1},{16,18},{17,19},{1... | collective-permute-start | bytes 1081352 | tf_op jit(solution)/shard_map/ppermute | solution.py:287
  134.5 12.0 %collective-permute-start.13 = (f32[2,4,88,128]{3,2,1,0:T(8,128)S(1)}, f32[2,4,88,128]{3,2,1,0:T(8,128)S(1)}, u32[]{:S(2)}, u32[]{:S(2)}) collective-permute-start(f32[2,4,88,128]{3,2,1,0:T(8,128)S(1)} %bitcast.108), channel_id=1, source_target_pairs={{0,6},{1,7},{2,0},{3,1},{4,2},{5,3},{6,4},{7,5},{16,22},{17,23},{1... | collective-permute-start | bytes 1081352 | tf_op jit(solution)/shard_map/ppermute | solution.py:288
  146.6 7.0 %collective-permute-start.24 = (f32[4,88,128]{2,1,0:T(8,128)S(1)}, f32[4,88,128]{2,1,0:T(8,128)S(1)}, u32[]{:S(2)}, u32[]{:S(2)}) collective-permute-start(f32[4,88,128]{2,1,0:T(8,128)S(1)} %get-tuple-element.22), channel_id=1, source_target_pairs={{0,32},{1,33},{2,34},{3,35},{4,36},{5,37},{6,38},{7,39},{16,48},{1... | collective-permute-start | bytes 540680 | tf_op jit(solution)/shard_map/ppermute | solution.py:289
  146.9 6.6 %collective-permute-start.25 = (f32[4,88,128]{2,1,0:T(8,128)S(1)}, f32[4,88,128]{2,1,0:T(8,128)S(1)}, u32[]{:S(2)}, u32[]{:S(2)}) collective-permute-start(f32[4,88,128]{2,1,0:T(8,128)S(1)} %get-tuple-element.23), channel_id=1, source_target_pairs={{0,96},{1,97},{2,98},{3,99},{4,100},{5,101},{6,102},{7,103},{16,11... | collective-permute-start | bytes 540680 | tf_op jit(solution)/shard_map/ppermute | solution.py:290
  149.9 6.0 %collective-permute-start.16 = (f32[4,88,128]{2,1,0:T(8,128)S(1)}, f32[4,88,128]{2,1,0:T(8,128)S(1)}, u32[]{:S(2)}, u32[]{:S(2)}) collective-permute-start(f32[4,88,128]{2,1,0:T(8,128)S(1)} %get-tuple-element.24), channel_id=1, source_target_pairs={{0,6},{1,7},{2,0},{3,1},{4,2},{5,3},{6,4},{7,5},{16,22},{17,23},{1... | collective-permute-start | bytes 540680 | tf_op jit(solution)/shard_map/ppermute | solution.py:290
  152.8 6.7 %collective-permute-start.15 = (f32[4,88,128]{2,1,0:T(8,128)S(1)}, f32[4,88,128]{2,1,0:T(8,128)S(1)}, u32[]{:S(2)}, u32[]{:S(2)}) collective-permute-start(f32[4,88,128]{2,1,0:T(8,128)S(1)} %get-tuple-element.25), channel_id=1, source_target_pairs={{0,2},{1,3},{2,4},{3,5},{4,6},{5,7},{6,0},{7,1},{16,18},{17,19},{1... | collective-permute-start | bytes 540680 | tf_op jit(solution)/shard_map/ppermute | solution.py:289
  159.8 5.8 %collective-permute-start.27 = (f32[2,88,128]{2,1,0:T(8,128)S(1)}, f32[2,88,128]{2,1,0:T(8,128)S(1)}, u32[]{:S(2)}, u32[]{:S(2)}) collective-permute-start(f32[2,88,128]{2,1,0:T(8,128)S(1)} %get-tuple-element.45), channel_id=1, source_target_pairs={{0,2},{1,3},{2,4},{3,5},{4,6},{5,7},{6,0},{7,1},{16,18},{17,19},{1... | collective-permute-start | bytes 270344 | tf_op jit(solution)/shard_map/ppermute | solution.py:287
  161.8 6.3 %collective-permute-start.18 = (f32[2,88,128]{2,1,0:T(8,128)S(1)}, f32[2,88,128]{2,1,0:T(8,128)S(1)}, u32[]{:S(2)}, u32[]{:S(2)}) collective-permute-start(f32[2,88,128]{2,1,0:T(8,128)S(1)} %get-tuple-element.48), channel_id=1, source_target_pairs={{0,32},{1,33},{2,34},{3,35},{4,36},{5,37},{6,38},{7,39},{16,48},{1... | collective-permute-start | bytes 270344 | tf_op jit(solution)/shard_map/ppermute | solution.py:287
  161.9 6.2 %collective-permute-start.17 = (f32[2,88,128]{2,1,0:T(8,128)S(1)}, f32[2,88,128]{2,1,0:T(8,128)S(1)}, u32[]{:S(2)}, u32[]{:S(2)}) collective-permute-start(f32[2,88,128]{2,1,0:T(8,128)S(1)} %get-tuple-element.49), channel_id=1, source_target_pairs={{0,96},{1,97},{2,98},{3,99},{4,100},{5,101},{6,102},{7,103},{16,11... | collective-permute-start | bytes 270344 | tf_op jit(solution)/shard_map/ppermute | solution.py:288
  165.6 5.9 %collective-permute-start.30 = (f32[88,128]{1,0:T(8,128)S(1)}, f32[88,128]{1,0:T(8,128)S(1)}, u32[]{:S(2)}, u32[]{:S(2)}) collective-permute-start(f32[88,128]{1,0:T(8,128)S(1)} %get-tuple-element.42), channel_id=1, source_target_pairs={{0,6},{1,7},{2,0},{3,1},{4,2},{5,3},{6,4},{7,5},{16,22},{17,23},{1... | collective-permute-start | bytes 135176 | tf_op jit(solution)/shard_map/ppermute | solution.py:290
  168.1 7.9 %collective-permute-start.19 = (f32[88,128]{1,0:T(8,128)S(1)}, f32[88,128]{1,0:T(8,128)S(1)}, u32[]{:S(2)}, u32[]{:S(2)}) collective-permute-start(f32[88,128]{1,0:T(8,128)S(1)} %get-tuple-element.46), channel_id=1, source_target_pairs={{0,32},{1,33},{2,34},{3,35},{4,36},{5,37},{6,38},{7,39},{16,48},{1... | collective-permute-start | bytes 135176 | tf_op jit(solution)/shard_map/ppermute | solution.py:289
  168.2 7.7 %collective-permute-start.20 = (f32[88,128]{1,0:T(8,128)S(1)}, f32[88,128]{1,0:T(8,128)S(1)}, u32[]{:S(2)}, u32[]{:S(2)}) collective-permute-start(f32[88,128]{1,0:T(8,128)S(1)} %get-tuple-element.47), channel_id=1, source_target_pairs={{0,96},{1,97},{2,98},{3,99},{4,100},{5,101},{6,102},{7,103},{16,11... | collective-permute-start | bytes 135176 | tf_op jit(solution)/shard_map/ppermute | solution.py:290
  (26 other events, 373.9 us)

commit v2 on v1

v2 whole, which is shorter than its diff:
```python
import functools
import functools
import math

import jax
import jax.numpy as jnp
import numpy as np
from jax import lax
from jax.experimental import pallas as pl
from jax.experimental.pallas import tpu as pltpu
from jax.sharding import PartitionSpec as P

LEV = 72
TR = 2
VEC = 8
POOL = 8
NSLAB = 2
STEPS = 4
DIFFUSE = 0.075
ALL = ("lat", "lon")

ROWS = 8
COLS = 48
CH = VEC * TR * LEV
GROUP = TR * LEV
WCH = NSLAB * 2 * LEV
D = STEPS
EXT = ROWS + 2 * D
PITCH = 80
FIRST = 16
SPAN = 64
WPACK = 896
PART = 640
BLOCK = 88


def place(x, y, z, core):
    return (x * 2 + y % 2) * 16 + (y // 2) * 8 + z * 2 + core


PLACES = [(x, y, z, c) for x in range(4) for y in range(4) for z in range(4) for c in range(2)]


def moved(dx=0, dy=0, dz=0, dc=0):
    return [
        (place(x, y, z, c), place((x + dx) % 4, (y + dy) % 4, (z + dz) % 4, c ^ dc))
        for x, y, z, c in PLACES
    ]


def turned(bits):
    return [(place(x, y, z, c), place(x, y ^ bits, z, c)) for x, y, z, c in PLACES]


def meridian():
    pairs = []
    for b in range(8):
        for a in range(8):
            pairs.append((a * 16 + b, (a + 1) * 16 + b if a < 7 else a * 16 + b + 8))
            pairs.append((a * 16 + b + 8, (a - 1) * 16 + b + 8 if a > 0 else a * 16 + b))
    return pairs


FORWARD = meridian()
BACKWARD = [(t, s) for s, t in FORWARD]
EASTWARD = [(b, (b + 1) % 16) for b in range(16)]
WESTWARD = [(t, s) for s, t in EASTWARD]


def edge_tile(r, m):
    i = r * (CH // 128) + m
    return slice(i // 6 * 8, i // 6 * 8 + 8), slice(WPACK + i % 6 * 128, WPACK + i % 6 * 128 + 128)


def pack_kernel(
    info, vec_ids, pool, winds, low, high, wind, edge_next, edge_last,
    next_0, next_1, last_0, last_1, chosen,
):
    lane = lax.broadcasted_iota(jnp.int32, (1, CH), 1)
    source = lane
    for k in range(VEC):
        inside = (lane >= k * GROUP) & (lane < (k + 1) * GROUP)
        source = jnp.where(inside, lane + (vec_ids[k] - k) * GROUP, source)
    for i in range(CH // 128):
        row = lax.broadcasted_iota(jnp.int32, (128, CH), 0) + i * 128
        chosen[i * 128 : (i + 1) * 128, :] = jnp.where(row == source, 1.0, 0.0).astype(jnp.bfloat16)
    for half in range(2):
        rows = pool[half * 4 : half * 4 + 4].reshape(4 * COLS, CH)
        picked = jnp.dot(rows, chosen[...], preferred_element_type=jnp.float32)
        picked = picked.reshape(4, COLS, CH)

        @pl.when(info[0] == 0)
        def _():
            (low, high)[half][...] = picked

        @pl.when(info[0] != 0)
        def _():
            for r in range(4):
                (high, low)[half][3 - r] = picked[r]

    place_in_slab = lax.rem(lax.broadcasted_iota(jnp.int32, (1, WCH), 1), 2 * LEV)
    turn = jnp.where((place_in_slab >= LEV) & (info[0] != 0), -1.0, 1.0)
    for r in range(ROWS):
        own = jnp.where(info[0] == 0, r, ROWS - 1 - r)
        line = winds[own] * turn
        wind[r] = line
        if r < 3:
            edge_last[:, r * WCH : (r + 1) * WCH] = line
        if r >= ROWS - 3:
            edge_next[:, (r - ROWS + 3) * WCH : (r - ROWS + 4) * WCH] = line
    for rows, edge, bulk_0, bulk_1 in (
        (high, edge_next, next_0, next_1),
        (low, edge_last, last_0, last_1),
    ):
        for r in range(4):
            for m in range(CH // 128):
                lanes = slice(m * 128, (m + 1) * 128)
                ends = jnp.concatenate([rows[r, :4, lanes], rows[r, COLS - 4 :, lanes]], axis=0)
                where = edge_tile(r, m)
                edge[where[0], where[1]] = ends
            bulk_0[r] = rows[r, 4 : COLS - 4, :PART]
            bulk_1[r] = rows[r, 4 : COLS - 4, PART:]


def pack(info, vec_ids, pool, winds):
    shapes = [(4, COLS, CH)] * 2 + [(ROWS, COLS, WCH)] + [(COLS, WPACK + 768)] * 2
    shapes += [(4, COLS - 8, PART), (4, COLS - 8, CH - PART)] * 2
    return pl.pallas_call(
        pack_kernel,
        out_shape=[jax.ShapeDtypeStruct(s, jnp.float32) for s in shapes],
        in_specs=[pl.BlockSpec(memory_space=pltpu.SMEM)] * 2
        + [pl.BlockSpec(memory_space=pltpu.VMEM)] * 2,
        out_specs=[pl.BlockSpec(memory_space=pltpu.VMEM)] * 9,
        scratch_shapes=[pltpu.VMEM((CH, CH), jnp.bfloat16)],
        compiler_params=pltpu.CompilerParams(vmem_limit_bytes=24 << 20),
        cost_estimate=pl.CostEstimate(flops=1 << 30, bytes_accessed=4 << 20, transcendentals=0),
        name="pack",
    )(info, vec_ids, pool, winds)


SIDE = EXT - 2


def edges_kernel(before, after, low, high, wind, *rest):
    to_east, to_west = rest[4:6]
    for first, near, target in ((COLS - 4, 4, to_east), (0, 0, to_west)):
        columns = slice(first, first + 4)
        for r in range(3):
            for m in range(CH // 128):
                lanes = slice(m * 128, (m + 1) * 128)
                where = edge_tile(r + 1, m)
                target[r, :, lanes] = before[where[0], where[1]][near : near + 4]
                where = edge_tile(r, m)
                target[11 + r, :, lanes] = after[where[0], where[1]][near : near + 4]
        for r in range(4):
            target[3 + r] = low[r, columns, :]
            target[7 + r] = high[r, columns, :]
        for r in range(SIDE):
            if r < 3:
                line = before[columns, r * WCH : (r + 1) * WCH]
            elif r < 11:
                line = wind[r - 3, columns, :]
            else:
                line = after[columns, (r - 11) * WCH : (r - 10) * WCH]
            target[SIDE + r // 4, :, r % 4 * WCH : (r % 4 + 1) * WCH] = line


def edges(arrays, bulk):
    vmem = pl.BlockSpec(memory_space=pltpu.VMEM)
    anywhere = pl.BlockSpec(memory_space=pl.ANY)
    shapes = [jax.ShapeDtypeStruct((SIDE + 4, 4, CH), jnp.float32)] * 2
    return pl.pallas_call(
        edges_kernel,
        out_shape=shapes + [jax.ShapeDtypeStruct(b.shape, b.dtype) for b in bulk],
        in_specs=[vmem] * 5 + [anywhere] * 4,
        out_specs=[vmem] * 2 + [anywhere] * 4,
        input_output_aliases={5 + i: 2 + i for i in range(4)},
        compiler_params=pltpu.CompilerParams(vmem_limit_bytes=16 << 20),
        cost_estimate=pl.CostEstimate(flops=1 << 20, bytes_accessed=4 << 20, transcendentals=0),
        name="edges",
    )(*arrays, *bulk)


def frame_kernel(info, before, after, wind, west, east, wind_ext):
    turn_west, turn_east = info[5], info[6]
    for r in range(3):
        lanes = slice(r * WCH, (r + 1) * WCH)
        wind_ext[r, 8 : 8 + COLS] = before[:, lanes]
        wind_ext[11 + r, 8 : 8 + COLS] = after[:, lanes]
    for r in range(ROWS):
        wind_ext[3 + r, 8 : 8 + COLS] = wind[r]
    lane = lax.rem(lax.broadcasted_iota(jnp.int32, (1, WCH), 1), 2 * LEV)
    for turn, payload, first in ((turn_west, west, 4), (turn_east, east, 8 + COLS)):
        sign = jnp.where((lane >= LEV) & (turn != 0), -1.0, 1.0)
        for r in range(SIDE):
            line = payload[SIDE + r // 4, :, r % 4 * WCH : (r % 4 + 1) * WCH] * sign
            wind_ext[jnp.where(turn == 0, r, SIDE - 1 - r), first : first + 4] = line


def frame_winds(info, *arrays):
    vmem = pl.BlockSpec(memory_space=pltpu.VMEM)
    return pl.pallas_call(
        frame_kernel,
        out_shape=jax.ShapeDtypeStruct((SIDE, SPAN, WCH), jnp.float32),
        in_specs=[pl.BlockSpec(memory_space=pltpu.SMEM)] + [vmem] * 5,
        out_specs=vmem,
        compiler_params=pltpu.CompilerParams(vmem_limit_bytes=16 << 20),
        cost_estimate=pl.CostEstimate(flops=1 << 20, bytes_accessed=4 << 20, transcendentals=0),
        name="frame",
    )(info, *arrays)


def window_kernel(
    part, info, wind_ids, cosine,
    before_edge, low, high, after_edge, west, east, wind_ext,
    levels, mix, basis_main, basis_rest, before_0, after_0,
    *others,
):
    before_1, after_1, earlier = others[:3] if part else (None, None, None)
    out, mine, theirs, state_a, state_b, spread, weighted, gram, rest = others[3 * part :]
    flip, mx, my, mz, mc, turn_west, turn_east = (info[i] for i in range(7))
    lanes = slice(part * 512, part * 512 + PART)
    skip = part * 64

    for r in range(4):
        state_a[4 + r, FIRST : FIRST + COLS] = low[r, :, lanes]
        state_a[8 + r, FIRST : FIRST + COLS] = high[r, :, lanes]
        for row, edge, bulk_0, bulk_1 in (
            (r, before_edge, before_0, before_1),
            (12 + r, after_edge, after_0, after_1),
        ):
            middle = slice(FIRST + 4, FIRST + COLS - 4)
            if part:
                state_a[row, middle, :128] = bulk_0[r, :, 512:]
                state_a[row, middle, 128:] = bulk_1[r]
            else:
                state_a[row, middle] = bulk_0[r]
            for m in range(PART // 128):
                tile = slice(m * 128, (m + 1) * 128)
                where = edge_tile(r, m + part * 4)
                ends = edge[where[0], where[1]]
                state_a[row, FIRST : FIRST + 4, tile] = ends[:4]
                state_a[row, FIRST + COLS - 4 : FIRST + COLS, tile] = ends[4:]
    for r in range(SIDE):
        from_west = jnp.where(turn_west == 0, r, SIDE - 1 - r)
        from_east = jnp.where(turn_east == 0, r, SIDE - 1 - r)
        state_a[1 + r, FIRST - 4 : FIRST] = west[from_west, :, lanes]
        state_a[1 + r, FIRST + COLS : FIRST + COLS + 4] = east[from_east, :, lanes]

    level = lax.broadcasted_iota(jnp.int32, (2 * LEV, PART), 0)
    level = jnp.where(level >= LEV, level - LEV, level)
    repeat = jnp.where(level == levels[:, lanes], 1.0, 0.0).astype(jnp.bfloat16)
    flat = wind_ext[...].reshape(SIDE * SPAN, WCH)
    for i in range(2 * NSLAB):
        value = flat[:, i * LEV : (i + 1) * LEV]
        coarse = value.astype(jnp.bfloat16)
        fine = (value - coarse.astype(jnp.float32)).astype(jnp.bfloat16)
        both = jnp.concatenate([coarse, fine], axis=1)
        spread[i] = jnp.dot(both, repeat, preferred_element_type=jnp.float32).reshape(
            SIDE, SPAN, PART
        )

    up, down = mix[0:1, lanes], mix[1:2, lanes]

    def updated(source, slab, r, c):
        now = source[r, pl.ds(c, 8), :]
        after = source[r + 1, pl.ds(c, 8), :]
        before = source[r - 1, pl.ds(c, 8), :]
        east_side = source[r, pl.ds(c + 1, 8), :]
        west_side = source[r, pl.ds(c - 1, 8), :]
        u = spread[2 * slab, r - 1, pl.ds(c - FIRST + 8, 8), :]
        v = spread[2 * slab + 1, r - 1, pl.ds(c - FIRST + 8, 8), :]
        gain_east = jnp.maximum(u, 0.0) + DIFFUSE
        gain_after = jnp.maximum(v, 0.0) + DIFFUSE
        change = gain_east * (east_side - now) + (gain_east - u) * (west_side - now)
        change += gain_after * (after - now) + (gain_after - v) * (before - now)
        above, below = pltpu.roll(now, PART - 1, 1), pltpu.roll(now, 1, 1)
        change += up * (above - now) - down * (now - below)
        return now + change

    buffers = (state_a, state_b)
    for step in range(STEPS - 1):
        source, target = buffers[step % 2], buffers[(step + 1) % 2]
        slab = wind_ids[step]

        def body(r, carry):
            for c in range(FIRST - 8, FIRST - 8 + SPAN, 8):
                target[r, c : c + 8, :] = updated(source, slab, r, c)
            return carry

        lax.fori_loop(1 + step, EXT - 1 - step, body, 0)

    source = buffers[(STEPS - 1) % 2]
    slab = wind_ids[STEPS - 1]
    own_lanes = lax.broadcasted_iota(jnp.int32, (16, 128), 1) >= skip

    def last(r, carry):
        own = jnp.where(flip == 0, r - D, ROWS - 1 - (r - D))
        share = cosine[own]
        for c in range(0, COLS, 16):
            first = updated(source, slab, r, FIRST + c)
            second = updated(source, slab, r, FIRST + c + 8)
            both = jnp.concatenate([first, second], axis=0)
            if part:
                there = slice(c, c + 16)
                out[own, there, :512] = earlier[own, there, :512]
                out[own, there, 512:640] = jnp.where(
                    own_lanes, both[:, :128], earlier[own, there, 512:]
                )
                out[own, there, 640:] = both[:, 128:]
            else:
                out[own, c : c + 16, :] = both
            weighted[own, c : c + 16, :] = (both * share).astype(jnp.bfloat16)
        return carry

    lax.fori_loop(D, D + ROWS, last, 0)

    flat_weighted = weighted[...].reshape(ROWS * COLS, PART)
    across = (((0,), (0,)), ((), ()))
    for i in range(PART // 128):
        gram[i * 128 : (i + 1) * 128, :] = lax.dot_general(
            flat_weighted[:, i * 128 : (i + 1) * 128],
            basis_main[...],
            across,
            preferred_element_type=jnp.float32,
        )
    tail = lax.dot_general(
        basis_rest[...], flat_weighted, across, preferred_element_type=jnp.float32
    )
    for g in range(8):
        rest[g, :, :LEV] = tail[:, skip + g * LEV : skip + (g + 1) * LEV]

    def place_blocks(i, carry):
        rz, rx, ry = i // 8, (i // 2) % 4, i % 2
        z, x = (mz + rz) % 4, (mx + rx) % 4
        outer, inner = (rx, rz) if part else (rz, rx)
        at = outer * 8 + inner * 2 + ry
        a = x * 2 + (my ^ ry)
        for dc, target in ((0, mine), (1, theirs)):
            g = z * 2 + (mc ^ dc)
            target[at, :LEV] = gram[
                pl.ds(pl.multiple_of(skip + g * LEV, 8), LEV),
                pl.ds(pl.multiple_of(a * 128, 128), 128),
            ]
            target[at, LEV:] = rest[g, pl.ds(pl.multiple_of(a * 16, 16), 16), :]
        return carry

    lax.fori_loop(0, 32, place_blocks, 0, unroll=4)


def window(part, scalars, arrays):
    blocks = jax.ShapeDtypeStruct((32, BLOCK, 128), jnp.float32)
    vmem = pl.BlockSpec(memory_space=pltpu.VMEM)
    return pl.pallas_call(
        functools.partial(window_kernel, part),
        out_shape=[
            jax.ShapeDtypeStruct((ROWS, COLS, CH if part else PART), jnp.float32),
            blocks,
            blocks,
        ],
        in_specs=[pl.BlockSpec(memory_space=pltpu.SMEM)] * len(scalars) + [vmem] * len(arrays),
        out_specs=[vmem] * 3,
        scratch_shapes=[
            pltpu.VMEM((EXT, PITCH, PART), jnp.float32),
            pltpu.VMEM((EXT, PITCH, PART), jnp.float32),
            pltpu.VMEM((2 * NSLAB, SIDE, SPAN, PART), jnp.float32),
            pltpu.VMEM((ROWS, COLS, PART), jnp.bfloat16),
            pltpu.VMEM((PART, 1024), jnp.float32),
            pltpu.VMEM((8, 128, 128), jnp.float32),
        ],
        compiler_params=pltpu.CompilerParams(vmem_limit_bytes=40 << 20),
        cost_estimate=pl.CostEstimate(flops=8 << 30, bytes_accessed=16 << 20, transcendentals=0),
        name=f"window_{part}",
    )(*scalars, *arrays)


def line_sum(parts, **axis):
    (name,) = axis
    sent = [lax.ppermute(parts[k], ALL, moved(**{name: k})) for k in (1, 2, 3)]
    return (parts[0] + sent[0]) + (sent[1] + sent[2])


def shards(pool, vec_ids, winds, wind_ids, mixing, basis):
    lat_index = lax.axis_index("lat").astype(jnp.int32)
    lon_index = lax.axis_index("lon").astype(jnp.int32)
    flip = lon_index // 8
    info = jnp.stack(
        [
            flip,
            lat_index // 2,
            lat_index % 2,
            (lon_index // 2) % 4,
            lon_index % 2,
            (lon_index % 8 == 0).astype(jnp.int32),
            (lon_index % 8 == 7).astype(jnp.int32),
        ]
    )
    low, high, wind, edge_next, edge_last, *bulk = pack(info, vec_ids, pool, winds)

    before_edge = lax.ppermute(edge_next, ALL, FORWARD)
    after_edge = lax.ppermute(edge_last, ALL, BACKWARD)
    to_east, to_west, *bulk = edges((before_edge, after_edge, low, high, wind), bulk)
    west = lax.ppermute(to_east, "lon", EASTWARD)
    east = lax.ppermute(to_west, "lon", WESTWARD)
    before_0, after_0 = lax.ppermute(bulk[0], ALL, FORWARD), lax.ppermute(bulk[2], ALL, BACKWARD)
    before_1, after_1 = lax.ppermute(bulk[1], ALL, FORWARD), lax.ppermute(bulk[3], ALL, BACKWARD)
    wind_ext = frame_winds(info, before_edge, after_edge, wind, west, east)

    level_mix = jnp.concatenate(
        [mixing.reshape(TR, LEV - 1), jnp.zeros((TR, 1), mixing.dtype)], axis=1
    )
    upper = jnp.tile(level_mix.reshape(GROUP), VEC)
    mix = jnp.stack([upper, jnp.roll(upper, 1)])
    rows = (jnp.arange(ROWS, dtype=jnp.int32) + lat_index * ROWS).astype(jnp.float32)
    cosine = jnp.cos((rows + 0.5) * (math.pi / (ROWS * 8)) - math.pi / 2)
    grouped = basis.reshape(ROWS * COLS, 8, 144)
    basis_main = grouped[:, :, :128].reshape(ROWS * COLS, 1024)
    basis_rest = grouped[:, :, 128:].reshape(ROWS * COLS, 128)

    levels = jnp.asarray(np.arange(CH, dtype=np.int32)[None] % LEV)
    scalars = (info, wind_ids, cosine)
    arrays = (
        before_edge, low, high, after_edge, west, east, wind_ext,
        levels, mix, basis_main, basis_rest, before_0, after_0,
    )
    half, mine, theirs = window(0, scalars, arrays)
    first = mine + lax.ppermute(theirs, ALL, moved(dc=1))
    sensitivity, mine, theirs = window(1, scalars, (*arrays, before_1, after_1, half))
    second = mine + lax.ppermute(theirs, ALL, moved(dc=1))

    first = line_sum(first.reshape(4, 8, BLOCK, 128), dz=1)
    second = line_sum(second.reshape(4, 8, BLOCK, 128), dx=1)
    first = line_sum(first.reshape(4, 2, BLOCK, 128), dx=1)
    second = line_sum(second.reshape(4, 2, BLOCK, 128), dz=1)
    near = jnp.where(flip == 0, first, second)
    far = jnp.where(flip == 0, second, first)
    block = near[0] + lax.ppermute(near[1], ALL, turned(1))
    block += lax.ppermute(far[0], ALL, turned(2)) + lax.ppermute(far[1], ALL, turned(3))
    ritz = jnp.concatenate([block[:LEV].T, block[LEV:, :LEV]], axis=0)
    return sensitivity, ritz * (1.0 / math.sqrt(ROWS * COLS * 128))


def solution(mesh):
    in_specs = (P("lat", "lon", None), P(), P("lat", "lon", None), P(), P(), P("lat", "lon", None))
    out_specs = (P("lat", "lon", None), P("lat", "lon"))
    return jax.shard_map(shards, mesh=mesh, in_specs=in_specs, out_specs=out_specs, check_vma=False)
```

time: 183 us -> 155 us (0.85)
  starting transfers between devices: 66.7 us -> 27.4 us
  waiting for transfers between devices: 54.5 us -> 70.6 us
  other arithmetic: 7.24 us -> 1.29 us
    ppermute x32 -> x25, starting transfers between devices: 66.7 us -> 27.4 us  [the longest x12 8.74 us: line_sum(): sent = [lax.ppermute(parts[k], ALL, moved(**{name: k})) for k in (1, 2, 3)]]
    ppermute x32 -> x25, waiting for transfers between devices: 54.5 us -> 70.6 us  [the longest x1 32 us: shards(): west = lax.ppermute(to_east, 'lon', EASTWARD)]
    slice x3 -> x2, local copies, waits for them, and re-layouts: 1.11 us -> 4.29 us  [shards(): basis_rest = grouped[:, :, 128:].reshape(ROWS * COLS, 128)]
    unnamed x35 -> x32, local copies, waits for them, and re-layouts: 5.94 us -> 9.11 us
    slice x8 -> x4, local copies, waits for them, and re-layouts: 2.67 us -> 0.18 us  [line_sum(): sent = [lax.ppermute(parts[k], ALL, moved(**{name: k})) for k in (1, 2, 3)]]
    slice x1 -> x2, local copies, waits for them, and re-layouts: 2.14 us -> 0.01 us  [shards(): basis_main = grouped[:, :, :128].reshape(ROWS * COLS, 1024)]
    select_n x2, other arithmetic: 2.18 us -> 0.06 us  [the longest x1 0.05 us: shards(): far = jnp.where(flip == 0, second, first)]
    pallas_call x1 -> x4, Pallas kernels: 31 us -> 30.3 us  [the longest x2 29.3 us: window(): pl.pallas_call(functools.partial(window_kernel, part), out_shape=[jax.Sha...]
  transfers between devices with their start and end apart: 32 -> 25, of which waited for: 16 -> 14; matrix products, arithmetic and copies ran while one was open for 11% -> 8% of each run, Pallas kernels for 0% -> 20%
where the time goes in v2:
time: 155 us; the launch traced here: 154 us
  waiting for transfers between devices  70.6 us (46%)
  Pallas kernels  33.7 us (22%)
  starting transfers between devices  27.4 us (18%)
  local copies, waits for them, and re-layouts  19.8 us (13%)
    ppermute x1, waiting for transfers between devices, shards(): west = lax.ppermute(to_east, 'lon', EASTWARD)  32 us
    pallas_call x2, Pallas kernels, window(): pl.pallas_call(functools.partial(window_kernel, part), out_shape=[jax.Sha...  29.3 us
    ppermute x12, waiting for transfers between devices, line_sum(): sent = [lax.ppermute(parts[k], ALL, moved(**{name: k})) for k in (1, 2, 3)]  22.4 us
    unnamed x32, local copies, waits for them, and re-layouts  9.11 us
    ppermute x12, starting transfers between devices, line_sum(): sent = [lax.ppermute(parts[k], ALL, moved(**{name: k})) for k in (1, 2, 3)]  8.74 us
    ppermute x1, waiting for transfers between devices, shards(): before_edge = lax.ppermute(edge_next, ALL, FORWARD)  8.28 us
    ppermute x1, starting transfers between devices, shards(): east = lax.ppermute(to_west, 'lon', WESTWARD)  5.35 us
    slice x2, local copies, waits for them, and re-layouts, shards(): basis_rest = grouped[:, :, 128:].reshape(ROWS * COLS, 128)  4.29 us
  transfers between devices with their start and end apart: 25, of which 14 were waited for; matrix products, arithmetic and copies ran while one was open for 8% of the time, Pallas kernels for 20%

profile of v2, /device:TPU:0, one launch (start us, length us, event | category | flops | bytes accessed | tf_op | source)
XLA Modules:
  0.0 153.8 jit_solution(8112037198521562779)
XLA Ops:
  3.7 3.4 %pack.1 = (f32[4,48,1152]{2,1,0:T(8,128)S(1)}, f32[4,48,1152]{2,1,0:T(8,128)S(1)}, f32[8,48,288]{2,1,0:T(8,128)S(1)}, f32[48,1664]{1,0:T(8,128)}, f32[48,1664]{1...) custom-call(s32[7]{0:T(128)S(1)} %stack.45.info, ...), custom_call_target="tpu_custom_call" | custom-call | flops 1073741824 | bytes 4194304 | tf_op jit(solution)/shard_map/pack/pallas_call | solution.py:128
  8.6 1.7 %collective-permute-start = (f32[48,1664]{1,0:T(8,128)}, f32[48,1664]{1,0:T(8,128)S(1)}, u32[]{:S(2)}, u32[]{:S(2)}) collective-permute-start(f32[48,1664]{1,0:T(8,128)} %get-tuple-element.23), channel_id=1, source_target_pairs={{0,16},{8,0},{16,32},{24,8},{32,48},{40,24},{48,64},{56,40},{64,80... | collective-permute-start | bytes 958472 | tf_op jit(solution)/shard_map/ppermute | solution.py:400
  10.2 1.9 %collective-permute-start.1 = (f32[48,1664]{1,0:T(8,128)}, f32[48,1664]{1,0:T(8,128)S(1)}, u32[]{:S(2)}, u32[]{:S(2)}) collective-permute-start(f32[48,1664]{1,0:T(8,128)} %get-tuple-element.26), channel_id=1, source_target_pairs={{16,0},{0,8},{32,16},{8,24},{48,32},{24,40},{64,48},{40,56},{80,64... | collective-permute-start | bytes 958472 | tf_op jit(solution)/shard_map/ppermute | solution.py:401
  12.4 4.0 %reshape.54 = bf16[384,8,144]{2,1,0:T(8,128)(2,1)} reshape(bf16[8,48,1152]{2,1,0:T(8,128)(2,1)} %param.12) | data formatting | bytes 1769472 | tf_op jit(solution)/shard_map/reshape | solution.py:416
  16.5 2.1 %slice.125 = bf16[384,8,16]{2,1,0:T(8,128)(2,1)} slice(bf16[384,8,144]{2,1,0:T(8,128)(2,1)} %reshape.54), slice={[0:384], [0:8], [128:144]} | slice | bytes 196608 | tf_op jit(solution)/shard_map/slice | solution.py:418
  19.2 8.3 %collective-permute-done.before.before_edge = f32[48,1664]{1,0:T(8,128)S(1)} collective-permute-done((f32[48,1664]{1,0:T(8,128)}, f32[48,1664]{1,0:T(8,128)S(1)}, u32[]{:S(2)}, u32[]{:S(2)}) %collective-permute-start) | collective-permute-done | bytes 319520 | tf_op jit(solution)/shard_map/ppermute | solution.py:400
  27.5 3.5 %collective-permute-done.1.after.after_edge = f32[48,1664]{1,0:T(8,128)S(1)} collective-permute-done((f32[48,1664]{1,0:T(8,128)}, f32[48,1664]{1,0:T(8,128)S(1)}, u32[]{:S(2)}, u32[]{:S(2)}) %collective-permute-start.1) | collective-permute-done | bytes 319520 | tf_op jit(solution)/shard_map/ppermute | solution.py:401
  34.1 3.9 %collective-permute-start.5 = (f32[4,40,640]{2,1,0:T(8,128)}, f32[4,40,640]{2,1,0:T(8,128)}, u32[]{:S(2)}, u32[]{:S(2)}) collective-permute-start(f32[4,40,640]{2,1,0:T(8,128)} %get-tuple-element.35), channel_id=1, source_target_pairs={{16,0},{0,8},{32,16},{8,24},{48,32},{24,40},{64,48},{40,56},{80,64... | collective-permute-start | bytes 1228808 | tf_op jit(solution)/shard_map/ppermute | solution.py:405
  39.7 2.2 %copy.15 = bf16[384,8,16]{0,2,1:T(8,128)(2,1)} copy(bf16[384,8,16]{2,1,0:T(8,128)(2,1)} %slice.125) | data formatting | bytes 196608 | tf_op jit(solution)/shard_map/slice | solution.py:418
  43.0 5.3 %collective-permute-start.3 = (f32[18,4,1152]{2,1,0:T(4,128)}, f32[18,4,1152]{2,1,0:T(4,128)S(1)}, u32[]{:S(2)}, u32[]{:S(2)}) collective-permute-start(f32[18,4,1152]{2,1,0:T(4,128)} %copy-done.9), channel_id=1, source_target_pairs={{1,0},{2,1},{3,2},{4,3},{5,4},{6,5},{7,6},{8,7},{9,8},{10,9},{11,1... | collective-permute-start | bytes 995336 | tf_op jit(solution)/shard_map/ppermute | solution.py:404
  48.5 32.0 %collective-permute-done.2.west = f32[18,4,1152]{2,1,0:T(4,128)S(1)} collective-permute-done((f32[18,4,1152]{2,1,0:T(4,128)}, f32[18,4,1152]{2,1,0:T(4,128)S(1)}, u32[]{:S(2)}, u32[]{:S(2)}) %collective-permute-start.2) | collective-permute-done | bytes 331808 | tf_op jit(solution)/shard_map/ppermute | solution.py:403
  81.6 14.0 %window_0.1 = (f32[8,48,640]{2,1,0:T(8,128)S(1)}, f32[32,88,128]{2,1,0:T(8,128)S(1)}, f32[32,88,128]{2,1,0:T(8,128)S(1)}) custom-call(s32[7]{0:T(128)S(1)} %stack.45.info, s32[4]{0:T(128)S(1)} %copy-done.12, f32[8]{0:T(128)S(1)} %add_cosine_fusion.cosine, f32[48,1664]{1,0:T(8,128)S(1)} %collective-permute-done.before.before_edge, ...), custom_call_target="tpu_custom_call" | custom-call | flops 8589934592 | bytes 16777216 | tf_op jit(solution)/shard_map/window_0/pallas_call | solution.py:354
  95.9 15.3 %window_1.1 = (f32[8,48,1152]{2,1,0:T(8,128)}, f32[32,88,128]{2,1,0:T(8,128)S(1)}, f32[32,88,128]{2,1,0:T(8,128)S(1)}) custom-call(s32[7]{0:T(128)S(1)} %stack.45.info, s32[4]{0:T(128)S(1)} %copy-done.12, f32[8]{0:T(128)S(1)} %add_cosine_fusion.cosine, f32[48,1664]{1,0:T(8,128)S(1)} %collective-permute-done.before.before_edge, ...), custom_call_target="tpu_custom_call" | custom-call | flops 8589934592 | bytes 16777216 | tf_op jit(solution)/shard_map/window_1/pallas_call | solution.py:354
  114.9 9.9 %collective-permute-done.10 = f32[8,88,128]{2,1,0:T(8,128)S(1)} collective-permute-done((f32[8,88,128]{2,1,0:T(8,128)S(1)}, f32[8,88,128]{2,1,0:T(8,128)S(1)}, u32[]{:S(2)}, u32[]{:S(2)}) %collective-permute-start.10) | collective-permute-done | bytes 360480 | tf_op jit(solution)/shard_map/ppermute | solution.py:379
  124.8 5.4 %collective-permute-done.11 = f32[8,88,128]{2,1,0:T(8,128)S(1)} collective-permute-done((f32[8,88,128]{2,1,0:T(8,128)S(1)}, f32[8,88,128]{2,1,0:T(8,128)S(1)}, u32[]{:S(2)}, u32[]{:S(2)}) %collective-permute-start.11) | collective-permute-done | bytes 360480 | tf_op jit(solution)/shard_map/ppermute | solution.py:379
  130.2 1.3 collective-permute-done.9
  131.9 2.6 %collective-permute-done.16 = f32[8,88,128]{2,1,0:T(8,128)S(1)} collective-permute-done((f32[8,88,128]{2,1,0:T(8,128)S(1)}, f32[8,88,128]{2,1,0:T(8,128)S(1)}, u32[]{:S(2)}, u32[]{:S(2)}) %collective-permute-start.16) | collective-permute-done | bytes 360480 | tf_op jit(solution)/shard_map/ppermute | solution.py:379
  135.2 2.2 %collective-permute-start.19 = (f32[2,88,128]{2,1,0:T(8,128)S(1)}, f32[2,88,128]{2,1,0:T(8,128)S(1)}, u32[]{:S(2)}, u32[]{:S(2)}) collective-permute-start(f32[2,88,128]{2,1,0:T(8,128)S(1)} %get-tuple-element.60), channel_id=1, source_target_pairs={{0,2},{1,3},{2,4},{3,5},{4,6},{5,7},{6,0},{7,1},{16,18},{17,19},{1... | collective-permute-start | bytes 270344 | tf_op jit(solution)/shard_map/ppermute | solution.py:379
  137.4 1.5 collective-permute-start.20
  139.5 2.0 %collective-permute-start.21 = (f32[2,88,128]{2,1,0:T(8,128)S(1)}, f32[2,88,128]{2,1,0:T(8,128)S(1)}, u32[]{:S(2)}, u32[]{:S(2)}) collective-permute-start(f32[2,88,128]{2,1,0:T(8,128)S(1)} %get-tuple-element.61), channel_id=1, source_target_pairs={{0,6},{1,7},{2,0},{3,1},{4,2},{5,3},{6,4},{7,5},{16,22},{17,23},{1... | collective-permute-start | bytes 270344 | tf_op jit(solution)/shard_map/ppermute | solution.py:379
  141.4 2.0 %collective-permute-done.20 = f32[2,88,128]{2,1,0:T(8,128)S(1)} collective-permute-done((f32[2,88,128]{2,1,0:T(8,128)S(1)}, f32[2,88,128]{2,1,0:T(8,128)S(1)}, u32[]{:S(2)}, u32[]{:S(2)}) %collective-permute-start.20) | collective-permute-done | bytes 90144 | tf_op jit(solution)/shard_map/ppermute | solution.py:379
  144.1 1.9 %collective-permute-start.22 = (f32[88,128]{1,0:T(8,128)S(1)}, f32[88,128]{1,0:T(8,128)S(1)}, u32[]{:S(2)}, u32[]{:S(2)}) collective-permute-start(f32[88,128]{1,0:T(8,128)S(1)} %slice_bitcast_fusion.2), channel_id=1, source_target_pairs={{0,16},{1,17},{2,18},{3,19},{4,20},{5,21},{6,22},{7,23},{16,0},{17... | collective-permute-start | bytes 135176 | tf_op jit(solution)/shard_map/ppermute | solution.py:437
  146.0 1.6 %collective-permute-start.23 = (f32[88,128]{1,0:T(8,128)S(1)}, f32[88,128]{1,0:T(8,128)S(1)}, u32[]{:S(2)}, u32[]{:S(2)}) collective-permute-start(f32[88,128]{1,0:T(8,128)S(1)} %get-tuple-element.64), channel_id=1, source_target_pairs={{0,8},{1,9},{2,10},{3,11},{4,12},{5,13},{6,14},{7,15},{16,24},{17,... | collective-permute-start | bytes 135176 | tf_op jit(solution)/shard_map/ppermute | solution.py:438
  148.9 2.6 %collective-permute-done.23 = f32[88,128]{1,0:T(8,128)S(1)} collective-permute-done((f32[88,128]{1,0:T(8,128)S(1)}, f32[88,128]{1,0:T(8,128)S(1)}, u32[]{:S(2)}, u32[]{:S(2)}) %collective-permute-start.23) | collective-permute-done | bytes 45088 | tf_op jit(solution)/shard_map/ppermute | solution.py:438
  (98 shorter events, 22.2 us)
Async XLA Ops:
  8.6 19.0 %collective-permute-start = (f32[48,1664]{1,0:T(8,128)}, f32[48,1664]{1,0:T(8,128)S(1)}, u32[]{:S(2)}, u32[]{:S(2)}) collective-permute-start(f32[48,1664]{1,0:T(8,128)} %get-tuple-element.23), channel_id=1, source_target_pairs={{0,16},{8,0},{16,32},{24,8},{32,48},{40,24},{48,64},{56,40},{64,80... | collective-permute-start | bytes 958472 | tf_op jit(solution)/shard_map/ppermute | solution.py:400
  10.2 20.8 %collective-permute-start.1 = (f32[48,1664]{1,0:T(8,128)}, f32[48,1664]{1,0:T(8,128)S(1)}, u32[]{:S(2)}, u32[]{:S(2)}) collective-permute-start(f32[48,1664]{1,0:T(8,128)} %get-tuple-element.26), channel_id=1, source_target_pairs={{16,0},{0,8},{32,16},{8,24},{48,32},{24,40},{64,48},{40,56},{80,64... | collective-permute-start | bytes 958472 | tf_op jit(solution)/shard_map/ppermute | solution.py:401
  34.1 47.5 %collective-permute-start.4 = (f32[4,40,640]{2,1,0:T(8,128)S(1)}, f32[4,40,640]{2,1,0:T(8,128)}, u32[]{:S(2)}, u32[]{:S(2)}) collective-permute-start(f32[4,40,640]{2,1,0:T(8,128)S(1)} %get-tuple-element.34), channel_id=1, source_target_pairs={{0,16},{8,0},{16,32},{24,8},{32,48},{40,24},{48,64},{56,40},{64,80... | collective-permute-start | bytes 1228808 | tf_op jit(solution)/shard_map/ppermute | solution.py:405
  34.1 47.5 %collective-permute-start.5 = (f32[4,40,640]{2,1,0:T(8,128)}, f32[4,40,640]{2,1,0:T(8,128)}, u32[]{:S(2)}, u32[]{:S(2)}) collective-permute-start(f32[4,40,640]{2,1,0:T(8,128)} %get-tuple-element.35), channel_id=1, source_target_pairs={{16,0},{0,8},{32,16},{8,24},{48,32},{24,40},{64,48},{40,56},{80,64... | collective-permute-start | bytes 1228808 | tf_op jit(solution)/shard_map/ppermute | solution.py:405
  42.9 37.6 %collective-permute-start.2 = (f32[18,4,1152]{2,1,0:T(4,128)}, f32[18,4,1152]{2,1,0:T(4,128)S(1)}, u32[]{:S(2)}, u32[]{:S(2)}) collective-permute-start(f32[18,4,1152]{2,1,0:T(4,128)} %copy-done.10), channel_id=1, source_target_pairs={{0,1},{1,2},{2,3},{3,4},{4,5},{5,6},{6,7},{7,8},{8,9},{9,10},{10,1... | collective-permute-start | bytes 995336 | tf_op jit(solution)/shard_map/ppermute | solution.py:403
  43.0 37.7 %collective-permute-start.3 = (f32[18,4,1152]{2,1,0:T(4,128)}, f32[18,4,1152]{2,1,0:T(4,128)S(1)}, u32[]{:S(2)}, u32[]{:S(2)}) collective-permute-start(f32[18,4,1152]{2,1,0:T(4,128)} %copy-done.9), channel_id=1, source_target_pairs={{1,0},{2,1},{3,2},{4,3},{5,4},{6,5},{7,6},{8,7},{9,8},{10,9},{11,1... | collective-permute-start | bytes 995336 | tf_op jit(solution)/shard_map/ppermute | solution.py:404
  48.4 47.5 %collective-permute-start.6 = (f32[4,40,512]{2,1,0:T(8,128)}, f32[4,40,512]{2,1,0:T(8,128)S(1)}, u32[]{:S(2)}, u32[]{:S(2)}) collective-permute-start(f32[4,40,512]{2,1,0:T(8,128)} %copy-done.3), channel_id=1, source_target_pairs={{0,16},{8,0},{16,32},{24,8},{32,48},{40,24},{48,64},{56,40},{64,80... | collective-permute-start | bytes 983048 | tf_op jit(solution)/shard_map/ppermute | solution.py:406
  80.5 15.4 %collective-permute-start.7 = (f32[4,40,512]{2,1,0:T(8,128)}, f32[4,40,512]{2,1,0:T(8,128)S(1)}, u32[]{:S(2)}, u32[]{:S(2)}) collective-permute-start(f32[4,40,512]{2,1,0:T(8,128)} %copy-done.6), channel_id=1, source_target_pairs={{16,0},{0,8},{32,16},{8,24},{48,32},{24,40},{64,48},{40,56},{80,64... | collective-permute-start | bytes 983048 | tf_op jit(solution)/shard_map/ppermute | solution.py:406
  95.6 16.1 %collective-permute-start.8 = (f32[32,88,128]{2,1,0:T(8,128)S(1)}, f32[32,88,128]{2,1,0:T(8,128)S(1)}, u32[]{:S(2)}, u32[]{:S(2)}) collective-permute-start(f32[32,88,128]{2,1,0:T(8,128)S(1)} %get-tuple-element.41), channel_id=1, source_target_pairs={{0,1},{1,0},{2,3},{3,2},{4,5},{5,4},{6,7},{7,6},{16,17},{17,16},{1... | collective-permute-start | bytes 4325384 | tf_op jit(solution)/shard_map/ppermute | solution.py:427
  111.9 12.9 %collective-permute-start.10 = (f32[8,88,128]{2,1,0:T(8,128)S(1)}, f32[8,88,128]{2,1,0:T(8,128)S(1)}, u32[]{:S(2)}, u32[]{:S(2)}) collective-permute-start(f32[8,88,128]{2,1,0:T(8,128)S(1)} %get-tuple-element.52), channel_id=1, source_target_pairs={{0,4},{1,5},{2,6},{3,7},{4,0},{5,1},{6,2},{7,3},{16,20},{17,21},{1... | collective-permute-start | bytes 1081352 | tf_op jit(solution)/shard_map/ppermute | solution.py:379
  112.0 18.2 %collective-permute-start.11 = (f32[8,88,128]{2,1,0:T(8,128)S(1)}, f32[8,88,128]{2,1,0:T(8,128)S(1)}, u32[]{:S(2)}, u32[]{:S(2)}) collective-permute-start(f32[8,88,128]{2,1,0:T(8,128)S(1)} %get-tuple-element.51), channel_id=1, source_target_pairs={{0,6},{1,7},{2,0},{3,1},{4,2},{5,3},{6,4},{7,5},{16,22},{17,23},{1... | collective-permute-start | bytes 1081352 | tf_op jit(solution)/shard_map/ppermute | solution.py:379
  112.9 18.6 %collective-permute-start.9 = (f32[8,88,128]{2,1,0:T(8,128)S(1)}, f32[8,88,128]{2,1,0:T(8,128)S(1)}, u32[]{:S(2)}, u32[]{:S(2)}) collective-permute-start(f32[8,88,128]{2,1,0:T(8,128)S(1)} %get-tuple-element.53), channel_id=1, source_target_pairs={{0,2},{1,3},{2,4},{3,5},{4,6},{5,7},{6,0},{7,1},{16,18},{17,19},{1... | collective-permute-start | bytes 1081352 | tf_op jit(solution)/shard_map/ppermute | solution.py:379
  114.7 19.7 %collective-permute-start.16 = (f32[8,88,128]{2,1,0:T(8,128)S(1)}, f32[8,88,128]{2,1,0:T(8,128)S(1)}, u32[]{:S(2)}, u32[]{:S(2)}) collective-permute-start(f32[8,88,128]{2,1,0:T(8,128)S(1)} %get-tuple-element.56), channel_id=1, source_target_pairs={{0,32},{1,33},{2,34},{3,35},{4,36},{5,37},{6,38},{7,39},{16,48},{1... | collective-permute-start | bytes 1081352 | tf_op jit(solution)/shard_map/ppermute | solution.py:379
  114.8 20.2 %collective-permute-start.17 = (f32[8,88,128]{2,1,0:T(8,128)S(1)}, f32[8,88,128]{2,1,0:T(8,128)S(1)}, u32[]{:S(2)}, u32[]{:S(2)}) collective-permute-start(f32[8,88,128]{2,1,0:T(8,128)S(1)} %get-tuple-element.55), channel_id=1, source_target_pairs={{0,64},{1,65},{2,66},{3,67},{4,68},{5,69},{6,70},{7,71},{16,80},{1... | collective-permute-start | bytes 1081352 | tf_op jit(solution)/shard_map/ppermute | solution.py:379
  124.8 10.3 %collective-permute-start.18 = (f32[8,88,128]{2,1,0:T(8,128)S(1)}, f32[8,88,128]{2,1,0:T(8,128)S(1)}, u32[]{:S(2)}, u32[]{:S(2)}) collective-permute-start(f32[8,88,128]{2,1,0:T(8,128)S(1)} %get-tuple-element.54), channel_id=1, source_target_pairs={{0,96},{1,97},{2,98},{3,99},{4,100},{5,101},{6,102},{7,103},{16,11... | collective-permute-start | bytes 1081352 | tf_op jit(solution)/shard_map/ppermute | solution.py:379
  131.7 7.8 %collective-permute-start.12 = (f32[2,88,128]{2,1,0:T(8,128)S(1)}, f32[2,88,128]{2,1,0:T(8,128)S(1)}, u32[]{:S(2)}, u32[]{:S(2)}) collective-permute-start(f32[2,88,128]{2,1,0:T(8,128)S(1)} %get-tuple-element.57), channel_id=1, source_target_pairs={{0,32},{1,33},{2,34},{3,35},{4,36},{5,37},{6,38},{7,39},{16,48},{1... | collective-permute-start | bytes 270344 | tf_op jit(solution)/shard_map/ppermute | solution.py:379
  131.8 9.7 %collective-permute-start.13 = (f32[2,88,128]{2,1,0:T(8,128)S(1)}, f32[2,88,128]{2,1,0:T(8,128)S(1)}, u32[]{:S(2)}, u32[]{:S(2)}) collective-permute-start(f32[2,88,128]{2,1,0:T(8,128)S(1)} %get-tuple-element.59), channel_id=1, source_target_pairs={{0,64},{1,65},{2,66},{3,67},{4,68},{5,69},{6,70},{7,71},{16,80},{1... | collective-permute-start | bytes 270344 | tf_op jit(solution)/shard_map/ppermute | solution.py:379
  134.4 7.0 %collective-permute-start.14 = (f32[2,88,128]{2,1,0:T(8,128)S(1)}, f32[2,88,128]{2,1,0:T(8,128)S(1)}, u32[]{:S(2)}, u32[]{:S(2)}) collective-permute-start(f32[2,88,128]{2,1,0:T(8,128)S(1)} %get-tuple-element.58), channel_id=1, source_target_pairs={{0,96},{1,97},{2,98},{3,99},{4,100},{5,101},{6,102},{7,103},{16,11... | collective-permute-start | bytes 270344 | tf_op jit(solution)/shard_map/ppermute | solution.py:379
  135.2 6.3 %collective-permute-start.19 = (f32[2,88,128]{2,1,0:T(8,128)S(1)}, f32[2,88,128]{2,1,0:T(8,128)S(1)}, u32[]{:S(2)}, u32[]{:S(2)}) collective-permute-start(f32[2,88,128]{2,1,0:T(8,128)S(1)} %get-tuple-element.60), channel_id=1, source_target_pairs={{0,2},{1,3},{2,4},{3,5},{4,6},{5,7},{6,0},{7,1},{16,18},{17,19},{1... | collective-permute-start | bytes 270344 | tf_op jit(solution)/shard_map/ppermute | solution.py:379
  137.4 6.0 %collective-permute-start.20 = (f32[2,88,128]{2,1,0:T(8,128)S(1)}, f32[2,88,128]{2,1,0:T(8,128)S(1)}, u32[]{:S(2)}, u32[]{:S(2)}) collective-permute-start(f32[2,88,128]{2,1,0:T(8,128)S(1)} %get-tuple-element.62), channel_id=1, source_target_pairs={{0,4},{1,5},{2,6},{3,7},{4,0},{5,1},{6,2},{7,3},{16,20},{17,21},{1... | collective-permute-start | bytes 270344 | tf_op jit(solution)/shard_map/ppermute | solution.py:379
  139.5 4.5 %collective-permute-start.21 = (f32[2,88,128]{2,1,0:T(8,128)S(1)}, f32[2,88,128]{2,1,0:T(8,128)S(1)}, u32[]{:S(2)}, u32[]{:S(2)}) collective-permute-start(f32[2,88,128]{2,1,0:T(8,128)S(1)} %get-tuple-element.61), channel_id=1, source_target_pairs={{0,6},{1,7},{2,0},{3,1},{4,2},{5,3},{6,4},{7,5},{16,22},{17,23},{1... | collective-permute-start | bytes 270344 | tf_op jit(solution)/shard_map/ppermute | solution.py:379
  144.1 4.8 %collective-permute-start.22 = (f32[88,128]{1,0:T(8,128)S(1)}, f32[88,128]{1,0:T(8,128)S(1)}, u32[]{:S(2)}, u32[]{:S(2)}) collective-permute-start(f32[88,128]{1,0:T(8,128)S(1)} %slice_bitcast_fusion.2), channel_id=1, source_target_pairs={{0,16},{1,17},{2,18},{3,19},{4,20},{5,21},{6,22},{7,23},{16,0},{17... | collective-permute-start | bytes 135176 | tf_op jit(solution)/shard_map/ppermute | solution.py:437
  146.0 5.6 %collective-permute-start.23 = (f32[88,128]{1,0:T(8,128)S(1)}, f32[88,128]{1,0:T(8,128)S(1)}, u32[]{:S(2)}, u32[]{:S(2)}) collective-permute-start(f32[88,128]{1,0:T(8,128)S(1)} %get-tuple-element.64), channel_id=1, source_target_pairs={{0,8},{1,9},{2,10},{3,11},{4,12},{5,13},{6,14},{7,15},{16,24},{17,... | collective-permute-start | bytes 135176 | tf_op jit(solution)/shard_map/ppermute | solution.py:438
  147.6 5.3 %collective-permute-start.24 = (f32[88,128]{1,0:T(8,128)S(1)}, f32[88,128]{1,0:T(8,128)S(1)}, u32[]{:S(2)}, u32[]{:S(2)}) collective-permute-start(f32[88,128]{1,0:T(8,128)S(1)} %get-tuple-element.63), channel_id=1, source_target_pairs={{0,24},{1,25},{2,26},{3,27},{4,28},{5,29},{6,30},{7,31},{16,8},{17... | collective-permute-start | bytes 135176 | tf_op jit(solution)/shard_map/ppermute | solution.py:438
  (17 other events, 59.1 us)

commit v3 on v2

--- a/solution.py
+++ b/solution.py
@@ -72,10 +72,7 @@
     return slice(i // 6 * 8, i // 6 * 8 + 8), slice(WPACK + i % 6 * 128, WPACK + i % 6 * 128 + 128)
 
 
-def pack_kernel(
-    info, vec_ids, pool, winds, low, high, wind, edge_next, edge_last,
-    next_0, next_1, last_0, last_1, chosen,
-):
+def choose(vec_ids, chosen):
     lane = lax.broadcasted_iota(jnp.int32, (1, CH), 1)
     source = lane
     for k in range(VEC):
@@ -84,6 +81,72 @@
     for i in range(CH // 128):
         row = lax.broadcasted_iota(jnp.int32, (128, CH), 0) + i * 128
         chosen[i * 128 : (i + 1) * 128, :] = jnp.where(row == source, 1.0, 0.0).astype(jnp.bfloat16)
+
+
+def turned_wind(winds, info, r):
+    place_in_slab = lax.rem(lax.broadcasted_iota(jnp.int32, (1, WCH), 1), 2 * LEV)
+    turn = jnp.where((place_in_slab >= LEV) & (info[0] != 0), -1.0, 1.0)
+    return winds[jnp.where(info[0] == 0, r, ROWS - 1 - r)] * turn
+
+
+def lead_kernel(
+    info, vec_ids, pool, winds, edge_next, edge_last, chosen, ends, held_winds, made, sems
+):
+    fetch = [
+        pltpu.make_async_copy(pool.at[:, :16, :], ends.at[0], sems.at[0]),
+        pltpu.make_async_copy(pool.at[:, COLS - 16 :, :], ends.at[1], sems.at[1]),
+        pltpu.make_async_copy(winds, held_winds, sems.at[2]),
+    ]
+    for copy in fetch:
+        copy.start()
+    choose(vec_ids, chosen)
+    for copy in fetch:
+        copy.wait()
+    for i in range(2):
+        rows = ends[i].reshape(ROWS * 16, CH)
+        picked = jnp.dot(rows, chosen[...], preferred_element_type=jnp.float32)
+        made[i] = picked.reshape(ROWS, 16, CH)
+    for r in range(4):
+        for edge, row in ((edge_last, r), (edge_next, 4 + r)):
+            own = jnp.where(info[0] == 0, row, ROWS - 1 - row)
+            for m in range(CH // 128):
+                lanes = slice(m * 128, (m + 1) * 128)
+                where = edge_tile(r, m)
+                edge[where[0], where[1]] = jnp.concatenate(
+                    [made[0, own, :4, lanes], made[1, own, 12:, lanes]], axis=0
+                )
+    for r in range(3):
+        lanes = slice(r * WCH, (r + 1) * WCH)
+        edge_last[:, lanes] = turned_wind(held_winds, info, r)
+        edge_next[:, lanes] = turned_wind(held_winds, info, ROWS - 3 + r)
+
+
+def lead(info, vec_ids, pool, winds):
+    vmem = pl.BlockSpec(memory_space=pltpu.VMEM)
+    return pl.pallas_call(
+        lead_kernel,
+        out_shape=[jax.ShapeDtypeStruct((COLS, WPACK + 768), jnp.float32)] * 2,
+        in_specs=[pl.BlockSpec(memory_space=pltpu.SMEM)] * 2
+        + [pl.BlockSpec(memory_space=pltpu.HBM)] * 2,
+        out_specs=[vmem] * 2,
+        scratch_shapes=[
+            pltpu.VMEM((CH, CH), jnp.bfloat16),
+            pltpu.VMEM((2, ROWS, 16, CH), jnp.bfloat16),
+            pltpu.VMEM((ROWS, COLS, WCH), jnp.float32),
+            pltpu.VMEM((2, ROWS, 16, CH), jnp.float32),
+            pltpu.SemaphoreType.DMA((3,)),
+        ],
+        compiler_params=pltpu.CompilerParams(vmem_limit_bytes=60 << 20),
+        cost_estimate=pl.CostEstimate(flops=1 << 30, bytes_accessed=4 << 20, transcendentals=0),
+        name="lead",
+    )(info, vec_ids, pool, winds)
+
+
+def pack_kernel(
+    info, vec_ids, pool, winds, basis,
+    low, high, wind, next_0, next_1, last_0, last_1, basis_main, basis_rest, chosen,
+):
+    choose(vec_ids, chosen)
     for half in range(2):
         rows = pool[half * 4 : half * 4 + 4].reshape(4 * COLS, CH)
         picked = jnp.dot(rows, chosen[...], preferred_element_type=jnp.float32)
@@ -98,44 +161,34 @@
             for r in range(4):
                 (high, low)[half][3 - r] = picked[r]
 
-    place_in_slab = lax.rem(lax.broadcasted_iota(jnp.int32, (1, WCH), 1), 2 * LEV)
-    turn = jnp.where((place_in_slab >= LEV) & (info[0] != 0), -1.0, 1.0)
-    for r in range(ROWS):
-        own = jnp.where(info[0] == 0, r, ROWS - 1 - r)
-        line = winds[own] * turn
-        wind[r] = line
-        if r < 3:
-            edge_last[:, r * WCH : (r + 1) * WCH] = line
-        if r >= ROWS - 3:
-            edge_next[:, (r - ROWS + 3) * WCH : (r - ROWS + 4) * WCH] = line
-    for rows, edge, bulk_0, bulk_1 in (
-        (high, edge_next, next_0, next_1),
-        (low, edge_last, last_0, last_1),
-    ):
+    for rows, bulk_0, bulk_1 in ((high, next_0, next_1), (low, last_0, last_1)):
         for r in range(4):
-            for m in range(CH // 128):
-                lanes = slice(m * 128, (m + 1) * 128)
-                ends = jnp.concatenate([rows[r, :4, lanes], rows[r, COLS - 4 :, lanes]], axis=0)
-                where = edge_tile(r, m)
-                edge[where[0], where[1]] = ends
             bulk_0[r] = rows[r, 4 : COLS - 4, :PART]
             bulk_1[r] = rows[r, 4 : COLS - 4, PART:]
-
-
-def pack(info, vec_ids, pool, winds):
-    shapes = [(4, COLS, CH)] * 2 + [(ROWS, COLS, WCH)] + [(COLS, WPACK + 768)] * 2
+    for r in range(ROWS):
+        wind[r] = turned_wind(winds, info, r)
+    flat = basis[...].reshape(ROWS * COLS, CH)
+    for a in range(8):
+        basis_main[:, a * 128 : (a + 1) * 128] = flat[:, a * 144 : a * 144 + 128]
+        basis_rest[:, a * 16 : (a + 1) * 16] = flat[:, a * 144 + 128 : (a + 1) * 144]
+
+
+def pack(info, vec_ids, pool, winds, basis):
+    shapes = [(4, COLS, CH)] * 2 + [(ROWS, COLS, WCH)]
     shapes += [(4, COLS - 8, PART), (4, COLS - 8, CH - PART)] * 2
+    outs = [jax.ShapeDtypeStruct(s, jnp.float32) for s in shapes]
+    outs += [jax.ShapeDtypeStruct((ROWS * COLS, n), jnp.bfloat16) for n in (1024, 128)]
+    vmem = pl.BlockSpec(memory_space=pltpu.VMEM)
     return pl.pallas_call(
         pack_kernel,
-        out_shape=[jax.ShapeDtypeStruct(s, jnp.float32) for s in shapes],
-        in_specs=[pl.BlockSpec(memory_space=pltpu.SMEM)] * 2
-        + [pl.BlockSpec(memory_space=pltpu.VMEM)] * 2,
-        out_specs=[pl.BlockSpec(memory_space=pltpu.VMEM)] * 9,
+        out_shape=outs,
+        in_specs=[pl.BlockSpec(memory_space=pltpu.SMEM)] * 2 + [vmem] * 3,
+        out_specs=[vmem] * 9,
         scratch_shapes=[pltpu.VMEM((CH, CH), jnp.bfloat16)],
         compiler_params=pltpu.CompilerParams(vmem_limit_bytes=24 << 20),
         cost_estimate=pl.CostEstimate(flops=1 << 30, bytes_accessed=4 << 20, transcendentals=0),
         name="pack",
-    )(info, vec_ids, pool, winds)
+    )(info, vec_ids, pool, winds, basis)
 
 
 SIDE = EXT - 2
@@ -205,7 +258,7 @@
         in_specs=[pl.BlockSpec(memory_space=pltpu.SMEM)] + [vmem] * 5,
         out_specs=vmem,
         compiler_params=pltpu.CompilerParams(vmem_limit_bytes=16 << 20),
-        cost_estimate=pl.CostEstimate(flops=1 << 20, bytes_accessed=4 << 20, transcendentals=0),
+        cost_estimate=pl.CostEstimate(flops=16 << 30, bytes_accessed=4 << 20, transcendentals=0),
         name="frame",
     )(info, *arrays)
 
@@ -395,15 +448,19 @@
             (lon_index % 8 == 7).astype(jnp.int32),
         ]
     )
-    low, high, wind, edge_next, edge_last, *bulk = pack(info, vec_ids, pool, winds)
-
+    edge_next, edge_last = lead(info, vec_ids, pool, winds)
     before_edge = lax.ppermute(edge_next, ALL, FORWARD)
     after_edge = lax.ppermute(edge_last, ALL, BACKWARD)
-    to_east, to_west, *bulk = edges((before_edge, after_edge, low, high, wind), bulk)
+    low, high, wind, next_0, next_1, last_0, last_1, basis_main, basis_rest = pack(
+        info, vec_ids, pool, winds, basis
+    )
+    to_east, to_west, *bulk = edges(
+        (before_edge, after_edge, low, high, wind), (next_0, last_0, next_1, last_1)
+    )
     west = lax.ppermute(to_east, "lon", EASTWARD)
     east = lax.ppermute(to_west, "lon", WESTWARD)
-    before_0, after_0 = lax.ppermute(bulk[0], ALL, FORWARD), lax.ppermute(bulk[2], ALL, BACKWARD)
-    before_1, after_1 = lax.ppermute(bulk[1], ALL, FORWARD), lax.ppermute(bulk[3], ALL, BACKWARD)
+    before_0, after_0 = lax.ppermute(bulk[0], ALL, FORWARD), lax.ppermute(bulk[1], ALL, BACKWARD)
+    before_1, after_1 = lax.ppermute(bulk[2], ALL, FORWARD), lax.ppermute(bulk[3], ALL, BACKWARD)
     wind_ext = frame_winds(info, before_edge, after_edge, wind, west, east)
 
     level_mix = jnp.concatenate(
@@ -413,10 +470,6 @@
     mix = jnp.stack([upper, jnp.roll(upper, 1)])
     rows = (jnp.arange(ROWS, dtype=jnp.int32) + lat_index * ROWS).astype(jnp.float32)
     cosine = jnp.cos((rows + 0.5) * (math.pi / (ROWS * 8)) - math.pi / 2)
-    grouped = basis.reshape(ROWS * COLS, 8, 144)
-    basis_main = grouped[:, :, :128].reshape(ROWS * COLS, 1024)
-    basis_rest = grouped[:, :, 128:].reshape(ROWS * COLS, 128)
-
     levels = jnp.asarray(np.arange(CH, dtype=np.int32)[None] % LEV)
     scalars = (info, wind_ids, cosine)
     arrays = (

time: 155 us -> 147 us (0.948)
  starting transfers between devices: 27.4 us -> 58.5 us
  waiting for transfers between devices: 70.6 us -> 46.5 us
  local copies, waits for them, and re-layouts: 19.8 us -> 2.68 us
  Pallas kernels: 33.7 us -> 36.2 us
    ppermute x12, starting transfers between devices: 8.74 us -> 34.8 us  [line_sum(): sent = [lax.ppermute(parts[k], ALL, moved(**{name: k})) for k in (1, 2, 3)]]
    ppermute x12, waiting for transfers between devices: 22.4 us -> 3.33 us  [line_sum(): sent = [lax.ppermute(parts[k], ALL, moved(**{name: k})) for k in (1, 2, 3)]]
    ppermute x1, waiting for transfers between devices: 32 us -> 17.4 us  [shards(): west = lax.ppermute(to_east, 'lon', EASTWARD)]
    unnamed x32 -> x17, local copies, waits for them, and re-layouts: 9.11 us -> 0.77 us
    ppermute x1, waiting for transfers between devices: 0.01 us -> 6.86 us  [shards(): lax.ppermute(bulk[0], ALL, FORWARD)]
    reshape x2 -> x0, local copies, waits for them, and re-layouts: 5.05 us -> none  [the longest x1 4.04 us: shards(): grouped = basis.reshape(ROWS * COLS, 8, 144)]
    ppermute x1, starting transfers between devices: 0.19 us -> 4.95 us  [shards(): lax.ppermute(bulk[3], ALL, BACKWARD)]
    slice x4 -> x0, local copies, waits for them, and re-layouts: 4.3 us -> none  [the longest x2 4.29 us: shards(): basis_rest = grouped[:, :, 128:].reshape(ROWS * COLS, 128)]
  transfers between devices with their start and end apart: 25 -> 25, of which waited for: 14 -> 9; matrix products, arithmetic and copies ran while one was open for 8% -> 2% of each run, Pallas kernels for 20% -> 22%
where the time goes in v3:
time: 147 us; the launch traced here: 146 us
  starting transfers between devices  58.5 us (40%)
  waiting for transfers between devices  46.5 us (32%)
  Pallas kernels  36.2 us (25%)
  local copies, waits for them, and re-layouts  2.68 us (2%)
    ppermute x12, starting transfers between devices, line_sum(): sent = [lax.ppermute(parts[k], ALL, moved(**{name: k})) for k in (1, 2, 3)]  34.8 us
    pallas_call x2, Pallas kernels, window(): pl.pallas_call(functools.partial(window_kernel, part), out_shape=[jax.Sha...  28.1 us
    ppermute x1, waiting for transfers between devices, shards(): west = lax.ppermute(to_east, 'lon', EASTWARD)  17.4 us
    ppermute x1, waiting for transfers between devices, shards(): before_edge = lax.ppermute(edge_next, ALL, FORWARD)  10.7 us
    ppermute x1, waiting for transfers between devices, shards(): lax.ppermute(bulk[0], ALL, FORWARD)  6.86 us
    ppermute x1, starting transfers between devices, shards(): east = lax.ppermute(to_west, 'lon', WESTWARD)  5.98 us
    ppermute x1, starting transfers between devices, shards(): lax.ppermute(bulk[3], ALL, BACKWARD)  4.95 us
    pallas_call x1, Pallas kernels, lead(): pl.pallas_call(lead_kernel, out_shape=[jax.ShapeDtypeStruct((COLS, WPACK...  4.01 us
  transfers between devices with their start and end apart: 25, of which 9 were waited for; matrix products, arithmetic and copies ran while one was open for 2% of the time, Pallas kernels for 22%

profile of v3, /device:TPU:0, one launch (start us, length us, event | category | flops | bytes accessed | tf_op | source)
XLA Modules:
  0.0 146.3 jit_solution(969637774488557929)
XLA Ops:
  1.4 4.0 %lead.1 = (f32[48,1664]{1,0:T(8,128)}, f32[48,1664]{1,0:T(8,128)}) custom-call(s32[7]{0:T(128)} %stack.45.info, s32[8]{0:T(128)} %vec_ids.3, bf16[8,48,1152]{2,1,0:T(8,128)(2,1)} %pool.3, f32[8,48,288]{2,1,0:T(8,128)} %winds.3), custom_call_target="tpu_custom_call" | custom-call | flops 1073741824 | bytes 4194304 | tf_op jit(solution)/shard_map/lead/pallas_call | solution.py:126
  5.4 1.7 %collective-permute-start = (f32[48,1664]{1,0:T(8,128)}, f32[48,1664]{1,0:T(8,128)S(1)}, u32[]{:S(2)}, u32[]{:S(2)}) collective-permute-start(f32[48,1664]{1,0:T(8,128)} %get-tuple-element.25), channel_id=1, source_target_pairs={{0,16},{8,0},{16,32},{24,8},{32,48},{40,24},{48,64},{56,40},{64,80... | collective-permute-start | bytes 958472 | tf_op jit(solution)/shard_map/ppermute | solution.py:452
  7.2 1.9 %collective-permute-start.1 = (f32[48,1664]{1,0:T(8,128)}, f32[48,1664]{1,0:T(8,128)S(1)}, u32[]{:S(2)}, u32[]{:S(2)}) collective-permute-start(f32[48,1664]{1,0:T(8,128)} %get-tuple-element.28), channel_id=1, source_target_pairs={{16,0},{0,8},{32,16},{8,24},{48,32},{24,40},{64,48},{40,56},{80,64... | collective-permute-start | bytes 958472 | tf_op jit(solution)/shard_map/ppermute | solution.py:453
  10.7 3.1 %pack.1 = (f32[4,48,1152]{2,1,0:T(8,128)S(1)}, f32[4,48,1152]{2,1,0:T(8,128)S(1)}, f32[8,48,288]{2,1,0:T(8,128)S(1)}, f32[4,40,640]{2,1,0:T(8,128)S(1)}, f32[4,4...) custom-call(s32[7]{0:T(128)S(1)} %copy-done, ...), custom_call_target="tpu_custom_call" | custom-call | flops 1073741824 | bytes 4194304 | tf_op jit(solution)/shard_map/pack/pallas_call | solution.py:182
  13.8 10.7 %collective-permute-done.before.before_edge = f32[48,1664]{1,0:T(8,128)S(1)} collective-permute-done((f32[48,1664]{1,0:T(8,128)}, f32[48,1664]{1,0:T(8,128)S(1)}, u32[]{:S(2)}, u32[]{:S(2)}) %collective-permute-start) | collective-permute-done | bytes 319520 | tf_op jit(solution)/shard_map/ppermute | solution.py:452
  24.5 3.5 %collective-permute-done.1.after.after_edge = f32[48,1664]{1,0:T(8,128)S(1)} collective-permute-done((f32[48,1664]{1,0:T(8,128)}, f32[48,1664]{1,0:T(8,128)S(1)}, u32[]{:S(2)}, u32[]{:S(2)}) %collective-permute-start.1) | collective-permute-done | bytes 319520 | tf_op jit(solution)/shard_map/ppermute | solution.py:453
  28.2 6.0 %collective-permute-start.3 = (f32[18,4,1152]{2,1,0:T(4,128)S(1)}, f32[18,4,1152]{2,1,0:T(4,128)S(1)}, u32[]{:S(2)}, u32[]{:S(2)}) collective-permute-start(f32[18,4,1152]{2,1,0:T(4,128)S(1)} %get-tuple-element.35), channel_id=1, source_target_pairs={{1,0},{2,1},{3,2},{4,3},{5,4},{6,5},{7,6},{8,7},{9,8},{10,9},{11,1... | collective-permute-start | bytes 995336 | tf_op jit(solution)/shard_map/ppermute | solution.py:461
  34.3 3.5 %collective-permute-start.5 = (f32[4,40,640]{2,1,0:T(8,128)S(1)}, f32[4,40,640]{2,1,0:T(8,128)S(1)}, u32[]{:S(2)}, u32[]{:S(2)}) collective-permute-start(f32[4,40,640]{2,1,0:T(8,128)S(1)} %get-tuple-element.39), channel_id=1, source_target_pairs={{16,0},{0,8},{32,16},{8,24},{48,32},{24,40},{64,48},{40,56},{80,64... | collective-permute-start | bytes 1228808 | tf_op jit(solution)/shard_map/ppermute | solution.py:462
  37.8 17.4 %collective-permute-done.2.west = f32[18,4,1152]{2,1,0:T(4,128)S(1)} collective-permute-done((f32[18,4,1152]{2,1,0:T(4,128)S(1)}, f32[18,4,1152]{2,1,0:T(4,128)S(1)}, u32[]{:S(2)}, u32[]{:S(2)}) %collective-permute-start.2) | collective-permute-done | bytes 331808 | tf_op jit(solution)/shard_map/ppermute | solution.py:460
  55.2 5.0 %collective-permute-start.7 = (f32[4,40,512]{2,1,0:T(8,128)S(1)}, f32[4,40,512]{2,1,0:T(8,128)S(1)}, u32[]{:S(2)}, u32[]{:S(2)}) collective-permute-start(f32[4,40,512]{2,1,0:T(8,128)S(1)} %get-tuple-element.41), channel_id=1, source_target_pairs={{16,0},{0,8},{32,16},{8,24},{48,32},{24,40},{64,48},{40,56},{80,64... | collective-permute-start | bytes 983048 | tf_op jit(solution)/shard_map/ppermute | solution.py:463
  61.1 6.9 %collective-permute-done.4.before_0 = f32[4,40,640]{2,1,0:T(8,128)S(1)} collective-permute-done((f32[4,40,640]{2,1,0:T(8,128)S(1)}, f32[4,40,640]{2,1,0:T(8,128)S(1)}, u32[]{:S(2)}, u32[]{:S(2)}) %collective-permute-start.4) | collective-permute-done | bytes 409632 | tf_op jit(solution)/shard_map/ppermute | solution.py:462
  68.0 1.5 collective-permute-done.5.after_0
  69.4 13.4 %window_0.1 = (f32[8,48,640]{2,1,0:T(8,128)S(1)}, f32[32,88,128]{2,1,0:T(8,128)S(1)}, f32[32,88,128]{2,1,0:T(8,128)S(1)}) custom-call(s32[7]{0:T(128)S(1)} %copy-done, s32[4]{0:T(128)S(1)} %copy-done.5, f32[8]{0:T(128)S(1)} %add_cosine_fusion.cosine, f32[48,1664]{1,0:T(8,128)S(1)} %collective-permute-done.before.before_edge, ...), custom_call_target="tpu_custom_call" | custom-call | flops 8589934592 | bytes 16777216 | tf_op jit(solution)/shard_map/window_0/pallas_call | solution.py:407
  83.1 14.7 %window_1.1 = (f32[8,48,1152]{2,1,0:T(8,128)}, f32[32,88,128]{2,1,0:T(8,128)S(1)}, f32[32,88,128]{2,1,0:T(8,128)S(1)}) custom-call(s32[7]{0:T(128)S(1)} %copy-done, s32[4]{0:T(128)S(1)} %copy-done.5, f32[8]{0:T(128)S(1)} %add_cosine_fusion.cosine, f32[48,1664]{1,0:T(8,128)S(1)} %collective-permute-done.before.before_edge, ...), custom_call_target="tpu_custom_call" | custom-call | flops 8589934592 | bytes 16777216 | tf_op jit(solution)/shard_map/window_1/pallas_call | solution.py:407
  98.6 4.6 %collective-permute-start.11 = (f32[8,88,128]{2,1,0:T(8,128)S(1)}, f32[8,88,128]{2,1,0:T(8,128)S(1)}, u32[]{:S(2)}, u32[]{:S(2)}) collective-permute-start(f32[8,88,128]{2,1,0:T(8,128)S(1)} %get-tuple-element.53), channel_id=1, source_target_pairs={{0,6},{1,7},{2,0},{3,1},{4,2},{5,3},{6,4},{7,5},{16,22},{17,23},{1... | collective-permute-start | bytes 1081352 | tf_op jit(solution)/shard_map/ppermute | solution.py:432
  104.4 8.0 %collective-permute-start.17 = (f32[8,88,128]{2,1,0:T(8,128)S(1)}, f32[8,88,128]{2,1,0:T(8,128)S(1)}, u32[]{:S(2)}, u32[]{:S(2)}) collective-permute-start(f32[8,88,128]{2,1,0:T(8,128)S(1)} %get-tuple-element.57), channel_id=1, source_target_pairs={{0,64},{1,65},{2,66},{3,67},{4,68},{5,69},{6,70},{7,71},{16,80},{1... | collective-permute-start | bytes 1081352 | tf_op jit(solution)/shard_map/ppermute | solution.py:432
  112.4 8.5 %collective-permute-start.18 = (f32[8,88,128]{2,1,0:T(8,128)S(1)}, f32[8,88,128]{2,1,0:T(8,128)S(1)}, u32[]{:S(2)}, u32[]{:S(2)}) collective-permute-start(f32[8,88,128]{2,1,0:T(8,128)S(1)} %get-tuple-element.56), channel_id=1, source_target_pairs={{0,96},{1,97},{2,98},{3,99},{4,100},{5,101},{6,102},{7,103},{16,11... | collective-permute-start | bytes 1081352 | tf_op jit(solution)/shard_map/ppermute | solution.py:432
  121.1 8.2 %collective-permute-start.13 = (f32[2,88,128]{2,1,0:T(8,128)S(1)}, f32[2,88,128]{2,1,0:T(8,128)S(1)}, u32[]{:S(2)}, u32[]{:S(2)}) collective-permute-start(f32[2,88,128]{2,1,0:T(8,128)S(1)} %get-tuple-element.61), channel_id=1, source_target_pairs={{0,64},{1,65},{2,66},{3,67},{4,68},{5,69},{6,70},{7,71},{16,80},{1... | collective-permute-start | bytes 270344 | tf_op jit(solution)/shard_map/ppermute | solution.py:432
  129.7 1.9 %collective-permute-start.20 = (f32[2,88,128]{2,1,0:T(8,128)S(1)}, f32[2,88,128]{2,1,0:T(8,128)S(1)}, u32[]{:S(2)}, u32[]{:S(2)}) collective-permute-start(f32[2,88,128]{2,1,0:T(8,128)S(1)} %get-tuple-element.64), channel_id=1, source_target_pairs={{0,4},{1,5},{2,6},{3,7},{4,0},{5,1},{6,2},{7,3},{16,20},{17,21},{1... | collective-permute-start | bytes 270344 | tf_op jit(solution)/shard_map/ppermute | solution.py:432
  131.6 2.3 %collective-permute-start.21 = (f32[2,88,128]{2,1,0:T(8,128)S(1)}, f32[2,88,128]{2,1,0:T(8,128)S(1)}, u32[]{:S(2)}, u32[]{:S(2)}) collective-permute-start(f32[2,88,128]{2,1,0:T(8,128)S(1)} %get-tuple-element.63), channel_id=1, source_target_pairs={{0,6},{1,7},{2,0},{3,1},{4,2},{5,3},{6,4},{7,5},{16,22},{17,23},{1... | collective-permute-start | bytes 270344 | tf_op jit(solution)/shard_map/ppermute | solution.py:432
  134.0 2.7 %collective-permute-done.19 = f32[2,88,128]{2,1,0:T(8,128)S(1)} collective-permute-done((f32[2,88,128]{2,1,0:T(8,128)S(1)}, f32[2,88,128]{2,1,0:T(8,128)S(1)}, u32[]{:S(2)}, u32[]{:S(2)}) %collective-permute-start.19) | collective-permute-done | bytes 90144 | tf_op jit(solution)/shard_map/ppermute | solution.py:432
  137.5 2.7 %collective-permute-start.23 = (f32[88,128]{1,0:T(8,128)S(1)}, f32[88,128]{1,0:T(8,128)S(1)}, u32[]{:S(2)}, u32[]{:S(2)}) collective-permute-start(f32[88,128]{1,0:T(8,128)S(1)} %get-tuple-element.66), channel_id=1, source_target_pairs={{0,8},{1,9},{2,10},{3,11},{4,12},{5,13},{6,14},{7,15},{16,24},{17,... | collective-permute-start | bytes 135176 | tf_op jit(solution)/shard_map/ppermute | solution.py:491
  140.1 2.0 %collective-permute-start.24 = (f32[88,128]{1,0:T(8,128)S(1)}, f32[88,128]{1,0:T(8,128)S(1)}, u32[]{:S(2)}, u32[]{:S(2)}) collective-permute-start(f32[88,128]{1,0:T(8,128)S(1)} %get-tuple-element.65), channel_id=1, source_target_pairs={{0,24},{1,25},{2,26},{3,27},{4,28},{5,29},{6,30},{7,31},{16,8},{17... | collective-permute-start | bytes 135176 | tf_op jit(solution)/shard_map/ppermute | solution.py:491
  143.1 2.3 %collective-permute-done.24 = f32[88,128]{1,0:T(8,128)S(1)} collective-permute-done((f32[88,128]{1,0:T(8,128)S(1)}, f32[88,128]{1,0:T(8,128)S(1)}, u32[]{:S(2)}, u32[]{:S(2)}) %collective-permute-start.24) | collective-permute-done | bytes 45088 | tf_op jit(solution)/shard_map/ppermute | solution.py:491
  (78 shorter events, 8.8 us)
Async XLA Ops:
  5.4 19.0 %collective-permute-start = (f32[48,1664]{1,0:T(8,128)}, f32[48,1664]{1,0:T(8,128)S(1)}, u32[]{:S(2)}, u32[]{:S(2)}) collective-permute-start(f32[48,1664]{1,0:T(8,128)} %get-tuple-element.25), channel_id=1, source_target_pairs={{0,16},{8,0},{16,32},{24,8},{32,48},{40,24},{48,64},{56,40},{64,80... | collective-permute-start | bytes 958472 | tf_op jit(solution)/shard_map/ppermute | solution.py:452
  7.2 20.8 %collective-permute-start.1 = (f32[48,1664]{1,0:T(8,128)}, f32[48,1664]{1,0:T(8,128)S(1)}, u32[]{:S(2)}, u32[]{:S(2)}) collective-permute-start(f32[48,1664]{1,0:T(8,128)} %get-tuple-element.28), channel_id=1, source_target_pairs={{16,0},{0,8},{32,16},{8,24},{48,32},{24,40},{64,48},{40,56},{80,64... | collective-permute-start | bytes 958472 | tf_op jit(solution)/shard_map/ppermute | solution.py:453
  28.1 27.2 %collective-permute-start.2 = (f32[18,4,1152]{2,1,0:T(4,128)S(1)}, f32[18,4,1152]{2,1,0:T(4,128)S(1)}, u32[]{:S(2)}, u32[]{:S(2)}) collective-permute-start(f32[18,4,1152]{2,1,0:T(4,128)S(1)} %get-tuple-element.34), channel_id=1, source_target_pairs={{0,1},{1,2},{2,3},{3,4},{4,5},{5,6},{6,7},{7,8},{8,9},{9,10},{10,1... | collective-permute-start | bytes 995336 | tf_op jit(solution)/shard_map/ppermute | solution.py:460
  28.2 32.0 %collective-permute-start.3 = (f32[18,4,1152]{2,1,0:T(4,128)S(1)}, f32[18,4,1152]{2,1,0:T(4,128)S(1)}, u32[]{:S(2)}, u32[]{:S(2)}) collective-permute-start(f32[18,4,1152]{2,1,0:T(4,128)S(1)} %get-tuple-element.35), channel_id=1, source_target_pairs={{1,0},{2,1},{3,2},{4,3},{5,4},{6,5},{7,6},{8,7},{9,8},{10,9},{11,1... | collective-permute-start | bytes 995336 | tf_op jit(solution)/shard_map/ppermute | solution.py:461
  34.2 33.7 %collective-permute-start.4 = (f32[4,40,640]{2,1,0:T(8,128)S(1)}, f32[4,40,640]{2,1,0:T(8,128)S(1)}, u32[]{:S(2)}, u32[]{:S(2)}) collective-permute-start(f32[4,40,640]{2,1,0:T(8,128)S(1)} %get-tuple-element.38), channel_id=1, source_target_pairs={{0,16},{8,0},{16,32},{24,8},{32,48},{40,24},{48,64},{56,40},{64,80... | collective-permute-start | bytes 1228808 | tf_op jit(solution)/shard_map/ppermute | solution.py:462
  34.3 35.1 %collective-permute-start.5 = (f32[4,40,640]{2,1,0:T(8,128)S(1)}, f32[4,40,640]{2,1,0:T(8,128)S(1)}, u32[]{:S(2)}, u32[]{:S(2)}) collective-permute-start(f32[4,40,640]{2,1,0:T(8,128)S(1)} %get-tuple-element.39), channel_id=1, source_target_pairs={{16,0},{0,8},{32,16},{8,24},{48,32},{24,40},{64,48},{40,56},{80,64... | collective-permute-start | bytes 1228808 | tf_op jit(solution)/shard_map/ppermute | solution.py:462
  37.8 45.2 %collective-permute-start.6 = (f32[4,40,512]{2,1,0:T(8,128)S(1)}, f32[4,40,512]{2,1,0:T(8,128)S(1)}, u32[]{:S(2)}, u32[]{:S(2)}) collective-permute-start(f32[4,40,512]{2,1,0:T(8,128)S(1)} %get-tuple-element.40), channel_id=1, source_target_pairs={{0,16},{8,0},{16,32},{24,8},{32,48},{40,24},{48,64},{56,40},{64,80... | collective-permute-start | bytes 983048 | tf_op jit(solution)/shard_map/ppermute | solution.py:463
  55.2 27.8 %collective-permute-start.7 = (f32[4,40,512]{2,1,0:T(8,128)S(1)}, f32[4,40,512]{2,1,0:T(8,128)S(1)}, u32[]{:S(2)}, u32[]{:S(2)}) collective-permute-start(f32[4,40,512]{2,1,0:T(8,128)S(1)} %get-tuple-element.41), channel_id=1, source_target_pairs={{16,0},{0,8},{32,16},{8,24},{48,32},{24,40},{64,48},{40,56},{80,64... | collective-permute-start | bytes 983048 | tf_op jit(solution)/shard_map/ppermute | solution.py:463
  82.8 15.5 %collective-permute-start.8 = (f32[32,88,128]{2,1,0:T(8,128)S(1)}, f32[32,88,128]{2,1,0:T(8,128)S(1)}, u32[]{:S(2)}, u32[]{:S(2)}) collective-permute-start(f32[32,88,128]{2,1,0:T(8,128)S(1)} %get-tuple-element.45), channel_id=1, source_target_pairs={{0,1},{1,0},{2,3},{3,2},{4,5},{5,4},{6,7},{7,6},{16,17},{17,16},{1... | collective-permute-start | bytes 4325384 | tf_op jit(solution)/shard_map/ppermute | solution.py:480
  97.8 6.3 %collective-permute-start.15 = (f32[32,88,128]{2,1,0:T(8,128)S(1)}, f32[32,88,128]{2,1,0:T(8,128)S(1)}, u32[]{:S(2)}, u32[]{:S(2)}) collective-permute-start(f32[32,88,128]{2,1,0:T(8,128)S(1)} %get-tuple-element.47), channel_id=1, source_target_pairs={{0,1},{1,0},{2,3},{3,2},{4,5},{5,4},{6,7},{7,6},{16,17},{17,16},{1... | collective-permute-start | bytes 4325384 | tf_op jit(solution)/shard_map/ppermute | solution.py:482
  98.5 13.9 %collective-permute-start.10 = (f32[8,88,128]{2,1,0:T(8,128)S(1)}, f32[8,88,128]{2,1,0:T(8,128)S(1)}, u32[]{:S(2)}, u32[]{:S(2)}) collective-permute-start(f32[8,88,128]{2,1,0:T(8,128)S(1)} %get-tuple-element.54), channel_id=1, source_target_pairs={{0,4},{1,5},{2,6},{3,7},{4,0},{5,1},{6,2},{7,3},{16,20},{17,21},{1... | collective-permute-start | bytes 1081352 | tf_op jit(solution)/shard_map/ppermute | solution.py:432
  98.6 22.3 %collective-permute-start.11 = (f32[8,88,128]{2,1,0:T(8,128)S(1)}, f32[8,88,128]{2,1,0:T(8,128)S(1)}, u32[]{:S(2)}, u32[]{:S(2)}) collective-permute-start(f32[8,88,128]{2,1,0:T(8,128)S(1)} %get-tuple-element.53), channel_id=1, source_target_pairs={{0,6},{1,7},{2,0},{3,1},{4,2},{5,3},{6,4},{7,5},{16,22},{17,23},{1... | collective-permute-start | bytes 1081352 | tf_op jit(solution)/shard_map/ppermute | solution.py:432
  103.3 17.7 %collective-permute-start.9 = (f32[8,88,128]{2,1,0:T(8,128)S(1)}, f32[8,88,128]{2,1,0:T(8,128)S(1)}, u32[]{:S(2)}, u32[]{:S(2)}) collective-permute-start(f32[8,88,128]{2,1,0:T(8,128)S(1)} %get-tuple-element.55), channel_id=1, source_target_pairs={{0,2},{1,3},{2,4},{3,5},{4,6},{5,7},{6,0},{7,1},{16,18},{17,19},{1... | collective-permute-start | bytes 1081352 | tf_op jit(solution)/shard_map/ppermute | solution.py:432
  104.3 25.0 %collective-permute-start.16 = (f32[8,88,128]{2,1,0:T(8,128)S(1)}, f32[8,88,128]{2,1,0:T(8,128)S(1)}, u32[]{:S(2)}, u32[]{:S(2)}) collective-permute-start(f32[8,88,128]{2,1,0:T(8,128)S(1)} %get-tuple-element.58), channel_id=1, source_target_pairs={{0,32},{1,33},{2,34},{3,35},{4,36},{5,37},{6,38},{7,39},{16,48},{1... | collective-permute-start | bytes 1081352 | tf_op jit(solution)/shard_map/ppermute | solution.py:432
  104.4 24.9 %collective-permute-start.17 = (f32[8,88,128]{2,1,0:T(8,128)S(1)}, f32[8,88,128]{2,1,0:T(8,128)S(1)}, u32[]{:S(2)}, u32[]{:S(2)}) collective-permute-start(f32[8,88,128]{2,1,0:T(8,128)S(1)} %get-tuple-element.57), channel_id=1, source_target_pairs={{0,64},{1,65},{2,66},{3,67},{4,68},{5,69},{6,70},{7,71},{16,80},{1... | collective-permute-start | bytes 1081352 | tf_op jit(solution)/shard_map/ppermute | solution.py:432
  112.4 16.9 %collective-permute-start.18 = (f32[8,88,128]{2,1,0:T(8,128)S(1)}, f32[8,88,128]{2,1,0:T(8,128)S(1)}, u32[]{:S(2)}, u32[]{:S(2)}) collective-permute-start(f32[8,88,128]{2,1,0:T(8,128)S(1)} %get-tuple-element.56), channel_id=1, source_target_pairs={{0,96},{1,97},{2,98},{3,99},{4,100},{5,101},{6,102},{7,103},{16,11... | collective-permute-start | bytes 1081352 | tf_op jit(solution)/shard_map/ppermute | solution.py:432
  121.1 10.6 %collective-permute-start.12 = (f32[2,88,128]{2,1,0:T(8,128)S(1)}, f32[2,88,128]{2,1,0:T(8,128)S(1)}, u32[]{:S(2)}, u32[]{:S(2)}) collective-permute-start(f32[2,88,128]{2,1,0:T(8,128)S(1)} %get-tuple-element.59), channel_id=1, source_target_pairs={{0,32},{1,33},{2,34},{3,35},{4,36},{5,37},{6,38},{7,39},{16,48},{1... | collective-permute-start | bytes 270344 | tf_op jit(solution)/shard_map/ppermute | solution.py:432
  121.1 12.8 %collective-permute-start.13 = (f32[2,88,128]{2,1,0:T(8,128)S(1)}, f32[2,88,128]{2,1,0:T(8,128)S(1)}, u32[]{:S(2)}, u32[]{:S(2)}) collective-permute-start(f32[2,88,128]{2,1,0:T(8,128)S(1)} %get-tuple-element.61), channel_id=1, source_target_pairs={{0,64},{1,65},{2,66},{3,67},{4,68},{5,69},{6,70},{7,71},{16,80},{1... | collective-permute-start | bytes 270344 | tf_op jit(solution)/shard_map/ppermute | solution.py:432
  129.5 7.2 %collective-permute-start.19 = (f32[2,88,128]{2,1,0:T(8,128)S(1)}, f32[2,88,128]{2,1,0:T(8,128)S(1)}, u32[]{:S(2)}, u32[]{:S(2)}) collective-permute-start(f32[2,88,128]{2,1,0:T(8,128)S(1)} %get-tuple-element.62), channel_id=1, source_target_pairs={{0,2},{1,3},{2,4},{3,5},{4,6},{5,7},{6,0},{7,1},{16,18},{17,19},{1... | collective-permute-start | bytes 270344 | tf_op jit(solution)/shard_map/ppermute | solution.py:432
  129.7 7.0 %collective-permute-start.20 = (f32[2,88,128]{2,1,0:T(8,128)S(1)}, f32[2,88,128]{2,1,0:T(8,128)S(1)}, u32[]{:S(2)}, u32[]{:S(2)}) collective-permute-start(f32[2,88,128]{2,1,0:T(8,128)S(1)} %get-tuple-element.64), channel_id=1, source_target_pairs={{0,4},{1,5},{2,6},{3,7},{4,0},{5,1},{6,2},{7,3},{16,20},{17,21},{1... | collective-permute-start | bytes 270344 | tf_op jit(solution)/shard_map/ppermute | solution.py:432
  131.6 5.6 %collective-permute-start.21 = (f32[2,88,128]{2,1,0:T(8,128)S(1)}, f32[2,88,128]{2,1,0:T(8,128)S(1)}, u32[]{:S(2)}, u32[]{:S(2)}) collective-permute-start(f32[2,88,128]{2,1,0:T(8,128)S(1)} %get-tuple-element.63), channel_id=1, source_target_pairs={{0,6},{1,7},{2,0},{3,1},{4,2},{5,3},{6,4},{7,5},{16,22},{17,23},{1... | collective-permute-start | bytes 270344 | tf_op jit(solution)/shard_map/ppermute | solution.py:432
  137.3 4.8 %collective-permute-start.22 = (f32[88,128]{1,0:T(8,128)S(1)}, f32[88,128]{1,0:T(8,128)S(1)}, u32[]{:S(2)}, u32[]{:S(2)}) collective-permute-start(f32[88,128]{1,0:T(8,128)S(1)} %slice_bitcast_fusion.2), channel_id=1, source_target_pairs={{0,16},{1,17},{2,18},{3,19},{4,20},{5,21},{6,22},{7,23},{16,0},{17... | collective-permute-start | bytes 135176 | tf_op jit(solution)/shard_map/ppermute | solution.py:490
  137.5 5.6 %collective-permute-start.23 = (f32[88,128]{1,0:T(8,128)S(1)}, f32[88,128]{1,0:T(8,128)S(1)}, u32[]{:S(2)}, u32[]{:S(2)}) collective-permute-start(f32[88,128]{1,0:T(8,128)S(1)} %get-tuple-element.66), channel_id=1, source_target_pairs={{0,8},{1,9},{2,10},{3,11},{4,12},{5,13},{6,14},{7,15},{16,24},{17,... | collective-permute-start | bytes 135176 | tf_op jit(solution)/shard_map/ppermute | solution.py:491
  140.1 5.3 %collective-permute-start.24 = (f32[88,128]{1,0:T(8,128)S(1)}, f32[88,128]{1,0:T(8,128)S(1)}, u32[]{:S(2)}, u32[]{:S(2)}) collective-permute-start(f32[88,128]{1,0:T(8,128)S(1)} %get-tuple-element.65), channel_id=1, source_target_pairs={{0,24},{1,25},{2,26},{3,27},{4,28},{5,29},{6,30},{7,31},{16,8},{17... | collective-permute-start | bytes 135176 | tf_op jit(solution)/shard_map/ppermute | solution.py:491
  (9 other events, 86.8 us)

commit v4 on v3

--- a/solution.py
+++ b/solution.py
@@ -234,7 +234,22 @@
     )(*arrays, *bulk)
 
 
-def frame_kernel(info, before, after, wind, west, east, wind_ext):
+def repeat_winds(wind_ext, levels, lanes, spread):
+    level = lax.broadcasted_iota(jnp.int32, (2 * LEV, PART), 0)
+    level = jnp.where(level >= LEV, level - LEV, level)
+    repeat = jnp.where(level == levels[:, lanes], 1.0, 0.0).astype(jnp.bfloat16)
+    flat = wind_ext[...].reshape(SIDE * SPAN, WCH)
+    for i in range(2 * NSLAB):
+        value = flat[:, i * LEV : (i + 1) * LEV]
+        coarse = value.astype(jnp.bfloat16)
+        fine = (value - coarse.astype(jnp.float32)).astype(jnp.bfloat16)
+        both = jnp.concatenate([coarse, fine], axis=1)
+        spread[i] = jnp.dot(both, repeat, preferred_element_type=jnp.float32).reshape(
+            SIDE, SPAN, PART
+        )
+
+
+def frame_kernel(info, before, after, wind, west, east, levels, wind_ext, spread):
     turn_west, turn_east = info[5], info[6]
     for r in range(3):
         lanes = slice(r * WCH, (r + 1) * WCH)
@@ -248,16 +263,20 @@
         for r in range(SIDE):
             line = payload[SIDE + r // 4, :, r % 4 * WCH : (r % 4 + 1) * WCH] * sign
             wind_ext[jnp.where(turn == 0, r, SIDE - 1 - r), first : first + 4] = line
+    repeat_winds(wind_ext, levels, slice(512, 512 + PART), spread)
 
 
 def frame_winds(info, *arrays):
     vmem = pl.BlockSpec(memory_space=pltpu.VMEM)
     return pl.pallas_call(
         frame_kernel,
-        out_shape=jax.ShapeDtypeStruct((SIDE, SPAN, WCH), jnp.float32),
-        in_specs=[pl.BlockSpec(memory_space=pltpu.SMEM)] + [vmem] * 5,
-        out_specs=vmem,
-        compiler_params=pltpu.CompilerParams(vmem_limit_bytes=16 << 20),
+        out_shape=[
+            jax.ShapeDtypeStruct((SIDE, SPAN, WCH), jnp.float32),
+            jax.ShapeDtypeStruct((2 * NSLAB, SIDE, SPAN, PART), jnp.float32),
+        ],
+        in_specs=[pl.BlockSpec(memory_space=pltpu.SMEM)] + [vmem] * 6,
+        out_specs=[vmem] * 2,
+        compiler_params=pltpu.CompilerParams(vmem_limit_bytes=24 << 20),
         cost_estimate=pl.CostEstimate(flops=16 << 30, bytes_accessed=4 << 20, transcendentals=0),
         name="frame",
     )(info, *arrays)
@@ -270,7 +289,8 @@
     *others,
 ):
     before_1, after_1, earlier = others[:3] if part else (None, None, None)
-    out, mine, theirs, state_a, state_b, spread, weighted, gram, rest = others[3 * part :]
+    out, mine, theirs, state_a, state_b, weighted, gram, rest, *spread = others[3 * part :]
+    spread = spread[0] if spread else None
     flip, mx, my, mz, mc, turn_west, turn_east = (info[i] for i in range(7))
     lanes = slice(part * 512, part * 512 + PART)
     skip = part * 64
@@ -300,18 +320,10 @@
         state_a[1 + r, FIRST - 4 : FIRST] = west[from_west, :, lanes]
         state_a[1 + r, FIRST + COLS : FIRST + COLS + 4] = east[from_east, :, lanes]
 
-    level = lax.broadcasted_iota(jnp.int32, (2 * LEV, PART), 0)
-    level = jnp.where(level >= LEV, level - LEV, level)
-    repeat = jnp.where(level == levels[:, lanes], 1.0, 0.0).astype(jnp.bfloat16)
-    flat = wind_ext[...].reshape(SIDE * SPAN, WCH)
-    for i in range(2 * NSLAB):
-        value = flat[:, i * LEV : (i + 1) * LEV]
-        coarse = value.astype(jnp.bfloat16)
-        fine = (value - coarse.astype(jnp.float32)).astype(jnp.bfloat16)
-        both = jnp.concatenate([coarse, fine], axis=1)
-        spread[i] = jnp.dot(both, repeat, preferred_element_type=jnp.float32).reshape(
-            SIDE, SPAN, PART
-        )
+    if part:
+        spread = wind_ext
+    else:
+        repeat_winds(wind_ext, levels, lanes, spread)
 
     up, down = mix[0:1, lanes], mix[1:2, lanes]
 
@@ -398,7 +410,7 @@
             target[at, LEV:] = rest[g, pl.ds(pl.multiple_of(a * 16, 16), 16), :]
         return carry
 
-    lax.fori_loop(0, 32, place_blocks, 0, unroll=4)
+    lax.fori_loop(0, 32, place_blocks, 0, unroll=8)
 
 
 def window(part, scalars, arrays):
@@ -416,12 +428,12 @@
         scratch_shapes=[
             pltpu.VMEM((EXT, PITCH, PART), jnp.float32),
             pltpu.VMEM((EXT, PITCH, PART), jnp.float32),
-            pltpu.VMEM((2 * NSLAB, SIDE, SPAN, PART), jnp.float32),
             pltpu.VMEM((ROWS, COLS, PART), jnp.bfloat16),
             pltpu.VMEM((PART, 1024), jnp.float32),
             pltpu.VMEM((8, 128, 128), jnp.float32),
-        ],
-        compiler_params=pltpu.CompilerParams(vmem_limit_bytes=40 << 20),
+        ]
+        + [pltpu.VMEM((2 * NSLAB, SIDE, SPAN, PART), jnp.float32)] * (1 - part),
+        compiler_params=pltpu.CompilerParams(vmem_limit_bytes=(24 if part else 32) << 20),
         cost_estimate=pl.CostEstimate(flops=8 << 30, bytes_accessed=16 << 20, transcendentals=0),
         name=f"window_{part}",
     )(*scalars, *arrays)
@@ -461,7 +473,8 @@
     east = lax.ppermute(to_west, "lon", WESTWARD)
     before_0, after_0 = lax.ppermute(bulk[0], ALL, FORWARD), lax.ppermute(bulk[1], ALL, BACKWARD)
     before_1, after_1 = lax.ppermute(bulk[2], ALL, FORWARD), lax.ppermute(bulk[3], ALL, BACKWARD)
-    wind_ext = frame_winds(info, before_edge, after_edge, wind, west, east)
+    levels = jnp.asarray(np.arange(CH, dtype=np.int32)[None] % LEV)
+    wind_ext, spread = frame_winds(info, before_edge, after_edge, wind, west, east, levels)
 
     level_mix = jnp.concatenate(
         [mixing.reshape(TR, LEV - 1), jnp.zeros((TR, 1), mixing.dtype)], axis=1
@@ -470,15 +483,14 @@
     mix = jnp.stack([upper, jnp.roll(upper, 1)])
     rows = (jnp.arange(ROWS, dtype=jnp.int32) + lat_index * ROWS).astype(jnp.float32)
     cosine = jnp.cos((rows + 0.5) * (math.pi / (ROWS * 8)) - math.pi / 2)
-    levels = jnp.asarray(np.arange(CH, dtype=np.int32)[None] % LEV)
     scalars = (info, wind_ids, cosine)
-    arrays = (
-        before_edge, low, high, after_edge, west, east, wind_ext,
-        levels, mix, basis_main, basis_rest, before_0, after_0,
+    tile = (before_edge, low, high, after_edge, west, east)
+    arrays = (levels, mix, basis_main, basis_rest, before_0, after_0)
+    half, mine, theirs = window(0, scalars, (*tile, wind_ext, *arrays))
+    first = mine + lax.ppermute(theirs, ALL, moved(dc=1))
+    sensitivity, mine, theirs = window(
+        1, scalars, (*tile, spread, *arrays, before_1, after_1, half)
     )
-    half, mine, theirs = window(0, scalars, arrays)
-    first = mine + lax.ppermute(theirs, ALL, moved(dc=1))
-    sensitivity, mine, theirs = window(1, scalars, (*arrays, before_1, after_1, half))
     second = mine + lax.ppermute(theirs, ALL, moved(dc=1))
 
     first = line_sum(first.reshape(4, 8, BLOCK, 128), dz=1)

time: 147 us -> 145 us (0.986)
  waiting for transfers between devices: 46.5 us -> 45 us
    pallas_call x1, Pallas kernels: 0.9 us -> 2.57 us  [frame_winds(): pl.pallas_call(frame_kernel, out_shape=[jax.ShapeDtypeStruct((SIDE, SPAN,...]
    ppermute x1, waiting for transfers between devices: 6.86 us -> 5.2 us  [shards(): lax.ppermute(bulk[0], ALL, FORWARD)]
  transfers between devices with their start and end apart: 25 -> 25, of which waited for: 9 -> 10; matrix products, arithmetic and copies ran while one was open for 2% -> 2% of each run, Pallas kernels for 22% -> 22%
where the time goes in v4:
time: 145 us
  starting transfers between devices  58.1 us (40%)
  waiting for transfers between devices  45 us (31%)
  Pallas kernels  36.6 us (25%)
  local copies, waits for them, and re-layouts  2.63 us (2%)
    ppermute x12, starting transfers between devices, line_sum(): sent = [lax.ppermute(parts[k], ALL, moved(**{name: k})) for k in (1, 2, 3)]  34.6 us
    pallas_call x2, Pallas kernels, window(): pl.pallas_call(functools.partial(window_kernel, part), out_shape=[jax.Sha...  26.8 us
    ppermute x1, waiting for transfers between devices, shards(): west = lax.ppermute(to_east, 'lon', EASTWARD)  17.4 us
    ppermute x1, waiting for transfers between devices, shards(): before_edge = lax.ppermute(edge_next, ALL, FORWARD)  10.6 us
    ppermute x1, starting transfers between devices, shards(): east = lax.ppermute(to_west, 'lon', WESTWARD)  6 us
    ppermute x1, waiting for transfers between devices, shards(): lax.ppermute(bulk[0], ALL, FORWARD)  5.2 us
    ppermute x1, starting transfers between devices, shards(): lax.ppermute(bulk[3], ALL, BACKWARD)  4.93 us
    pallas_call x1, Pallas kernels, lead(): pl.pallas_call(lead_kernel, out_shape=[jax.ShapeDtypeStruct((COLS, WPACK...  4.01 us
  transfers between devices with their start and end apart: 25, of which 10 were waited for; matrix products, arithmetic and copies ran while one was open for 2% of the time, Pallas kernels for 22%

profile of v4, /device:TPU:0, one launch (start us, length us, event | category | flops | bytes accessed | tf_op | source)
XLA Modules:
  0.0 144.7 jit_solution(15759916075432924647)
XLA Ops:
  1.3 4.0 %lead.1 = (f32[48,1664]{1,0:T(8,128)}, f32[48,1664]{1,0:T(8,128)}) custom-call(s32[7]{0:T(128)} %stack.45.info, s32[8]{0:T(128)} %vec_ids.3, bf16[8,48,1152]{2,1,0:T(8,128)(2,1)} %pool.3, f32[8,48,288]{2,1,0:T(8,128)} %winds.3), custom_call_target="tpu_custom_call" | custom-call | flops 1073741824 | bytes 4194304 | tf_op jit(solution)/shard_map/lead/pallas_call | solution.py:126
  5.4 1.7 %collective-permute-start = (f32[48,1664]{1,0:T(8,128)}, f32[48,1664]{1,0:T(8,128)S(1)}, u32[]{:S(2)}, u32[]{:S(2)}) collective-permute-start(f32[48,1664]{1,0:T(8,128)} %get-tuple-element.27), channel_id=1, source_target_pairs={{0,16},{8,0},{16,32},{24,8},{32,48},{40,24},{48,64},{56,40},{64,80... | collective-permute-start | bytes 958472 | tf_op jit(solution)/shard_map/ppermute | solution.py:464
  7.1 1.9 %collective-permute-start.1 = (f32[48,1664]{1,0:T(8,128)}, f32[48,1664]{1,0:T(8,128)S(1)}, u32[]{:S(2)}, u32[]{:S(2)}) collective-permute-start(f32[48,1664]{1,0:T(8,128)} %get-tuple-element.30), channel_id=1, source_target_pairs={{16,0},{0,8},{32,16},{8,24},{48,32},{24,40},{64,48},{40,56},{80,64... | collective-permute-start | bytes 958472 | tf_op jit(solution)/shard_map/ppermute | solution.py:465
  10.7 3.1 %pack.1 = (f32[4,48,1152]{2,1,0:T(8,128)S(1)}, f32[4,48,1152]{2,1,0:T(8,128)S(1)}, f32[8,48,288]{2,1,0:T(8,128)S(1)}, f32[4,40,640]{2,1,0:T(8,128)S(1)}, f32[4,4...) custom-call(s32[7]{0:T(128)S(1)} %copy-done, ...), custom_call_target="tpu_custom_call" | custom-call | flops 1073741824 | bytes 4194304 | tf_op jit(solution)/shard_map/pack/pallas_call | solution.py:182
  13.8 10.6 %collective-permute-done.before.before_edge = f32[48,1664]{1,0:T(8,128)S(1)} collective-permute-done((f32[48,1664]{1,0:T(8,128)}, f32[48,1664]{1,0:T(8,128)S(1)}, u32[]{:S(2)}, u32[]{:S(2)}) %collective-permute-start) | collective-permute-done | bytes 319520 | tf_op jit(solution)/shard_map/ppermute | solution.py:464
  24.4 3.5 %collective-permute-done.1.after.after_edge = f32[48,1664]{1,0:T(8,128)S(1)} collective-permute-done((f32[48,1664]{1,0:T(8,128)}, f32[48,1664]{1,0:T(8,128)S(1)}, u32[]{:S(2)}, u32[]{:S(2)}) %collective-permute-start.1) | collective-permute-done | bytes 319520 | tf_op jit(solution)/shard_map/ppermute | solution.py:465
  28.1 6.0 %collective-permute-start.3 = (f32[18,4,1152]{2,1,0:T(4,128)S(1)}, f32[18,4,1152]{2,1,0:T(4,128)S(1)}, u32[]{:S(2)}, u32[]{:S(2)}) collective-permute-start(f32[18,4,1152]{2,1,0:T(4,128)S(1)} %get-tuple-element.37), channel_id=1, source_target_pairs={{1,0},{2,1},{3,2},{4,3},{5,4},{6,5},{7,6},{8,7},{9,8},{10,9},{11,1... | collective-permute-start | bytes 995336 | tf_op jit(solution)/shard_map/ppermute | solution.py:473
  34.2 3.5 %collective-permute-start.5 = (f32[4,40,640]{2,1,0:T(8,128)S(1)}, f32[4,40,640]{2,1,0:T(8,128)S(1)}, u32[]{:S(2)}, u32[]{:S(2)}) collective-permute-start(f32[4,40,640]{2,1,0:T(8,128)S(1)} %get-tuple-element.42), channel_id=1, source_target_pairs={{16,0},{0,8},{32,16},{8,24},{48,32},{24,40},{64,48},{40,56},{80,64... | collective-permute-start | bytes 1228808 | tf_op jit(solution)/shard_map/ppermute | solution.py:474
  37.8 17.4 %collective-permute-done.2.west = f32[18,4,1152]{2,1,0:T(4,128)S(1)} collective-permute-done((f32[18,4,1152]{2,1,0:T(4,128)S(1)}, f32[18,4,1152]{2,1,0:T(4,128)S(1)}, u32[]{:S(2)}, u32[]{:S(2)}) %collective-permute-start.2) | collective-permute-done | bytes 331808 | tf_op jit(solution)/shard_map/ppermute | solution.py:472
  55.2 4.9 %collective-permute-start.7 = (f32[4,40,512]{2,1,0:T(8,128)S(1)}, f32[4,40,512]{2,1,0:T(8,128)S(1)}, u32[]{:S(2)}, u32[]{:S(2)}) collective-permute-start(f32[4,40,512]{2,1,0:T(8,128)S(1)} %get-tuple-element.44), channel_id=1, source_target_pairs={{16,0},{0,8},{32,16},{8,24},{48,32},{24,40},{64,48},{40,56},{80,64... | collective-permute-start | bytes 983048 | tf_op jit(solution)/shard_map/ppermute | solution.py:475
  60.1 2.6 %frame.1 = (f32[14,64,288]{2,1,0:T(8,128)S(1)}, f32[4,14,64,640]{3,2,1,0:T(8,128)S(1)}) custom-call(s32[7]{0:T(128)S(1)} %copy-done, f32[48,1664]{1,0:T(8,128)S(1)} %collective-permute-done.before.before_edge, f32[48,1664]{1,0:T(8,128)S(1)} %collective-permute-done.1.after.after_edge, f32[8,48,288]{2,1,0:T(8,128)S(1)} %get-tuple-element.31.wind, ...), custom_call_target="tpu_custom_call" | custom-call | flops 17179869184 | bytes 4194304 | tf_op jit(solution)/shard_map/frame/pallas_call | solution.py:271
  62.7 5.2 %collective-permute-done.4.before_0 = f32[4,40,640]{2,1,0:T(8,128)S(1)} collective-permute-done((f32[4,40,640]{2,1,0:T(8,128)S(1)}, f32[4,40,640]{2,1,0:T(8,128)S(1)}, u32[]{:S(2)}, u32[]{:S(2)}) %collective-permute-start.4) | collective-permute-done | bytes 409632 | tf_op jit(solution)/shard_map/ppermute | solution.py:474
  69.5 13.4 %window_0.1 = (f32[8,48,640]{2,1,0:T(8,128)S(1)}, f32[32,88,128]{2,1,0:T(8,128)S(1)}, f32[32,88,128]{2,1,0:T(8,128)S(1)}) custom-call(s32[7]{0:T(128)S(1)} %copy-done, s32[4]{0:T(128)S(1)} %copy-done.5, f32[8]{0:T(128)S(1)} %add_cosine_fusion.cosine, f32[48,1664]{1,0:T(8,128)S(1)} %collective-permute-done.before.before_edge, ...), custom_call_target="tpu_custom_call" | custom-call | flops 8589934592 | bytes 16777216 | tf_op jit(solution)/shard_map/window_0/pallas_call | solution.py:419
  83.0 13.3 %window_1.1 = (f32[8,48,1152]{2,1,0:T(8,128)}, f32[32,88,128]{2,1,0:T(8,128)S(1)}, f32[32,88,128]{2,1,0:T(8,128)S(1)}) custom-call(s32[7]{0:T(128)S(1)} %copy-done, s32[4]{0:T(128)S(1)} %copy-done.5, f32[8]{0:T(128)S(1)} %add_cosine_fusion.cosine, f32[48,1664]{1,0:T(8,128)S(1)} %collective-permute-done.before.before_edge, ...), custom_call_target="tpu_custom_call" | custom-call | flops 8589934592 | bytes 16777216 | tf_op jit(solution)/shard_map/window_1/pallas_call | solution.py:419
  97.2 4.5 %collective-permute-start.11 = (f32[8,88,128]{2,1,0:T(8,128)S(1)}, f32[8,88,128]{2,1,0:T(8,128)S(1)}, u32[]{:S(2)}, u32[]{:S(2)}) collective-permute-start(f32[8,88,128]{2,1,0:T(8,128)S(1)} %get-tuple-element.57), channel_id=1, source_target_pairs={{0,6},{1,7},{2,0},{3,1},{4,2},{5,3},{6,4},{7,5},{16,22},{17,23},{1... | collective-permute-start | bytes 1081352 | tf_op jit(solution)/shard_map/ppermute | solution.py:444
  102.8 8.0 %collective-permute-start.17 = (f32[8,88,128]{2,1,0:T(8,128)S(1)}, f32[8,88,128]{2,1,0:T(8,128)S(1)}, u32[]{:S(2)}, u32[]{:S(2)}) collective-permute-start(f32[8,88,128]{2,1,0:T(8,128)S(1)} %get-tuple-element.61), channel_id=1, source_target_pairs={{0,64},{1,65},{2,66},{3,67},{4,68},{5,69},{6,70},{7,71},{16,80},{1... | collective-permute-start | bytes 1081352 | tf_op jit(solution)/shard_map/ppermute | solution.py:444
  110.8 8.5 %collective-permute-start.18 = (f32[8,88,128]{2,1,0:T(8,128)S(1)}, f32[8,88,128]{2,1,0:T(8,128)S(1)}, u32[]{:S(2)}, u32[]{:S(2)}) collective-permute-start(f32[8,88,128]{2,1,0:T(8,128)S(1)} %get-tuple-element.60), channel_id=1, source_target_pairs={{0,96},{1,97},{2,98},{3,99},{4,100},{5,101},{6,102},{7,103},{16,11... | collective-permute-start | bytes 1081352 | tf_op jit(solution)/shard_map/ppermute | solution.py:444
  119.6 8.2 %collective-permute-start.13 = (f32[2,88,128]{2,1,0:T(8,128)S(1)}, f32[2,88,128]{2,1,0:T(8,128)S(1)}, u32[]{:S(2)}, u32[]{:S(2)}) collective-permute-start(f32[2,88,128]{2,1,0:T(8,128)S(1)} %get-tuple-element.65), channel_id=1, source_target_pairs={{0,64},{1,65},{2,66},{3,67},{4,68},{5,69},{6,70},{7,71},{16,80},{1... | collective-permute-start | bytes 270344 | tf_op jit(solution)/shard_map/ppermute | solution.py:444
  128.0 2.0 %collective-permute-start.20 = (f32[2,88,128]{2,1,0:T(8,128)S(1)}, f32[2,88,128]{2,1,0:T(8,128)S(1)}, u32[]{:S(2)}, u32[]{:S(2)}) collective-permute-start(f32[2,88,128]{2,1,0:T(8,128)S(1)} %get-tuple-element.68), channel_id=1, source_target_pairs={{0,4},{1,5},{2,6},{3,7},{4,0},{5,1},{6,2},{7,3},{16,20},{17,21},{1... | collective-permute-start | bytes 270344 | tf_op jit(solution)/shard_map/ppermute | solution.py:444
  130.0 2.2 %collective-permute-start.21 = (f32[2,88,128]{2,1,0:T(8,128)S(1)}, f32[2,88,128]{2,1,0:T(8,128)S(1)}, u32[]{:S(2)}, u32[]{:S(2)}) collective-permute-start(f32[2,88,128]{2,1,0:T(8,128)S(1)} %get-tuple-element.67), channel_id=1, source_target_pairs={{0,6},{1,7},{2,0},{3,1},{4,2},{5,3},{6,4},{7,5},{16,22},{17,23},{1... | collective-permute-start | bytes 270344 | tf_op jit(solution)/shard_map/ppermute | solution.py:444
  132.3 2.8 %collective-permute-done.19 = f32[2,88,128]{2,1,0:T(8,128)S(1)} collective-permute-done((f32[2,88,128]{2,1,0:T(8,128)S(1)}, f32[2,88,128]{2,1,0:T(8,128)S(1)}, u32[]{:S(2)}, u32[]{:S(2)}) %collective-permute-start.19) | collective-permute-done | bytes 90144 | tf_op jit(solution)/shard_map/ppermute | solution.py:444
  135.9 2.7 %collective-permute-start.23 = (f32[88,128]{1,0:T(8,128)S(1)}, f32[88,128]{1,0:T(8,128)S(1)}, u32[]{:S(2)}, u32[]{:S(2)}) collective-permute-start(f32[88,128]{1,0:T(8,128)S(1)} %get-tuple-element.70), channel_id=1, source_target_pairs={{0,8},{1,9},{2,10},{3,11},{4,12},{5,13},{6,14},{7,15},{16,24},{17,... | collective-permute-start | bytes 135176 | tf_op jit(solution)/shard_map/ppermute | solution.py:503
  138.6 2.0 %collective-permute-start.24 = (f32[88,128]{1,0:T(8,128)S(1)}, f32[88,128]{1,0:T(8,128)S(1)}, u32[]{:S(2)}, u32[]{:S(2)}) collective-permute-start(f32[88,128]{1,0:T(8,128)S(1)} %get-tuple-element.69), channel_id=1, source_target_pairs={{0,24},{1,25},{2,26},{3,27},{4,28},{5,29},{6,30},{7,31},{16,8},{17... | collective-permute-start | bytes 135176 | tf_op jit(solution)/shard_map/ppermute | solution.py:503
  141.5 2.3 %collective-permute-done.24 = f32[88,128]{1,0:T(8,128)S(1)} collective-permute-done((f32[88,128]{1,0:T(8,128)S(1)}, f32[88,128]{1,0:T(8,128)S(1)}, u32[]{:S(2)}, u32[]{:S(2)}) %collective-permute-start.24) | collective-permute-done | bytes 45088 | tf_op jit(solution)/shard_map/ppermute | solution.py:503
  (78 shorter events, 9.2 us)
Async XLA Ops:
  5.4 19.0 %collective-permute-start = (f32[48,1664]{1,0:T(8,128)}, f32[48,1664]{1,0:T(8,128)S(1)}, u32[]{:S(2)}, u32[]{:S(2)}) collective-permute-start(f32[48,1664]{1,0:T(8,128)} %get-tuple-element.27), channel_id=1, source_target_pairs={{0,16},{8,0},{16,32},{24,8},{32,48},{40,24},{48,64},{56,40},{64,80... | collective-permute-start | bytes 958472 | tf_op jit(solution)/shard_map/ppermute | solution.py:464
  7.1 20.8 %collective-permute-start.1 = (f32[48,1664]{1,0:T(8,128)}, f32[48,1664]{1,0:T(8,128)S(1)}, u32[]{:S(2)}, u32[]{:S(2)}) collective-permute-start(f32[48,1664]{1,0:T(8,128)} %get-tuple-element.30), channel_id=1, source_target_pairs={{16,0},{0,8},{32,16},{8,24},{48,32},{24,40},{64,48},{40,56},{80,64... | collective-permute-start | bytes 958472 | tf_op jit(solution)/shard_map/ppermute | solution.py:465
  28.0 27.2 %collective-permute-start.2 = (f32[18,4,1152]{2,1,0:T(4,128)S(1)}, f32[18,4,1152]{2,1,0:T(4,128)S(1)}, u32[]{:S(2)}, u32[]{:S(2)}) collective-permute-start(f32[18,4,1152]{2,1,0:T(4,128)S(1)} %get-tuple-element.36), channel_id=1, source_target_pairs={{0,1},{1,2},{2,3},{3,4},{4,5},{5,6},{6,7},{7,8},{8,9},{9,10},{10,1... | collective-permute-start | bytes 995336 | tf_op jit(solution)/shard_map/ppermute | solution.py:472
  28.1 32.0 %collective-permute-start.3 = (f32[18,4,1152]{2,1,0:T(4,128)S(1)}, f32[18,4,1152]{2,1,0:T(4,128)S(1)}, u32[]{:S(2)}, u32[]{:S(2)}) collective-permute-start(f32[18,4,1152]{2,1,0:T(4,128)S(1)} %get-tuple-element.37), channel_id=1, source_target_pairs={{1,0},{2,1},{3,2},{4,3},{5,4},{6,5},{7,6},{8,7},{9,8},{10,9},{11,1... | collective-permute-start | bytes 995336 | tf_op jit(solution)/shard_map/ppermute | solution.py:473
  34.2 33.7 %collective-permute-start.4 = (f32[4,40,640]{2,1,0:T(8,128)S(1)}, f32[4,40,640]{2,1,0:T(8,128)S(1)}, u32[]{:S(2)}, u32[]{:S(2)}) collective-permute-start(f32[4,40,640]{2,1,0:T(8,128)S(1)} %get-tuple-element.41), channel_id=1, source_target_pairs={{0,16},{8,0},{16,32},{24,8},{32,48},{40,24},{48,64},{56,40},{64,80... | collective-permute-start | bytes 1228808 | tf_op jit(solution)/shard_map/ppermute | solution.py:474
  34.2 35.2 %collective-permute-start.5 = (f32[4,40,640]{2,1,0:T(8,128)S(1)}, f32[4,40,640]{2,1,0:T(8,128)S(1)}, u32[]{:S(2)}, u32[]{:S(2)}) collective-permute-start(f32[4,40,640]{2,1,0:T(8,128)S(1)} %get-tuple-element.42), channel_id=1, source_target_pairs={{16,0},{0,8},{32,16},{8,24},{48,32},{24,40},{64,48},{40,56},{80,64... | collective-permute-start | bytes 1228808 | tf_op jit(solution)/shard_map/ppermute | solution.py:474
  37.8 45.3 %collective-permute-start.6 = (f32[4,40,512]{2,1,0:T(8,128)S(1)}, f32[4,40,512]{2,1,0:T(8,128)S(1)}, u32[]{:S(2)}, u32[]{:S(2)}) collective-permute-start(f32[4,40,512]{2,1,0:T(8,128)S(1)} %get-tuple-element.43), channel_id=1, source_target_pairs={{0,16},{8,0},{16,32},{24,8},{32,48},{40,24},{48,64},{56,40},{64,80... | collective-permute-start | bytes 983048 | tf_op jit(solution)/shard_map/ppermute | solution.py:475
  55.2 27.8 %collective-permute-start.7 = (f32[4,40,512]{2,1,0:T(8,128)S(1)}, f32[4,40,512]{2,1,0:T(8,128)S(1)}, u32[]{:S(2)}, u32[]{:S(2)}) collective-permute-start(f32[4,40,512]{2,1,0:T(8,128)S(1)} %get-tuple-element.44), channel_id=1, source_target_pairs={{16,0},{0,8},{32,16},{8,24},{48,32},{24,40},{64,48},{40,56},{80,64... | collective-permute-start | bytes 983048 | tf_op jit(solution)/shard_map/ppermute | solution.py:475
  82.9 13.9 %collective-permute-start.8 = (f32[32,88,128]{2,1,0:T(8,128)S(1)}, f32[32,88,128]{2,1,0:T(8,128)S(1)}, u32[]{:S(2)}, u32[]{:S(2)}) collective-permute-start(f32[32,88,128]{2,1,0:T(8,128)S(1)} %get-tuple-element.49), channel_id=1, source_target_pairs={{0,1},{1,0},{2,3},{3,2},{4,5},{5,4},{6,7},{7,6},{16,17},{17,16},{1... | collective-permute-start | bytes 4325384 | tf_op jit(solution)/shard_map/ppermute | solution.py:490
  96.4 6.1 %collective-permute-start.15 = (f32[32,88,128]{2,1,0:T(8,128)S(1)}, f32[32,88,128]{2,1,0:T(8,128)S(1)}, u32[]{:S(2)}, u32[]{:S(2)}) collective-permute-start(f32[32,88,128]{2,1,0:T(8,128)S(1)} %get-tuple-element.51), channel_id=1, source_target_pairs={{0,1},{1,0},{2,3},{3,2},{4,5},{5,4},{6,7},{7,6},{16,17},{17,16},{1... | collective-permute-start | bytes 4325384 | tf_op jit(solution)/shard_map/ppermute | solution.py:494
  97.1 13.7 %collective-permute-start.10 = (f32[8,88,128]{2,1,0:T(8,128)S(1)}, f32[8,88,128]{2,1,0:T(8,128)S(1)}, u32[]{:S(2)}, u32[]{:S(2)}) collective-permute-start(f32[8,88,128]{2,1,0:T(8,128)S(1)} %get-tuple-element.58), channel_id=1, source_target_pairs={{0,4},{1,5},{2,6},{3,7},{4,0},{5,1},{6,2},{7,3},{16,20},{17,21},{1... | collective-permute-start | bytes 1081352 | tf_op jit(solution)/shard_map/ppermute | solution.py:444
  97.2 22.2 %collective-permute-start.11 = (f32[8,88,128]{2,1,0:T(8,128)S(1)}, f32[8,88,128]{2,1,0:T(8,128)S(1)}, u32[]{:S(2)}, u32[]{:S(2)}) collective-permute-start(f32[8,88,128]{2,1,0:T(8,128)S(1)} %get-tuple-element.57), channel_id=1, source_target_pairs={{0,6},{1,7},{2,0},{3,1},{4,2},{5,3},{6,4},{7,5},{16,22},{17,23},{1... | collective-permute-start | bytes 1081352 | tf_op jit(solution)/shard_map/ppermute | solution.py:444
  101.7 17.7 %collective-permute-start.9 = (f32[8,88,128]{2,1,0:T(8,128)S(1)}, f32[8,88,128]{2,1,0:T(8,128)S(1)}, u32[]{:S(2)}, u32[]{:S(2)}) collective-permute-start(f32[8,88,128]{2,1,0:T(8,128)S(1)} %get-tuple-element.59), channel_id=1, source_target_pairs={{0,2},{1,3},{2,4},{3,5},{4,6},{5,7},{6,0},{7,1},{16,18},{17,19},{1... | collective-permute-start | bytes 1081352 | tf_op jit(solution)/shard_map/ppermute | solution.py:444
  102.7 25.1 %collective-permute-start.16 = (f32[8,88,128]{2,1,0:T(8,128)S(1)}, f32[8,88,128]{2,1,0:T(8,128)S(1)}, u32[]{:S(2)}, u32[]{:S(2)}) collective-permute-start(f32[8,88,128]{2,1,0:T(8,128)S(1)} %get-tuple-element.62), channel_id=1, source_target_pairs={{0,32},{1,33},{2,34},{3,35},{4,36},{5,37},{6,38},{7,39},{16,48},{1... | collective-permute-start | bytes 1081352 | tf_op jit(solution)/shard_map/ppermute | solution.py:444
  102.8 25.0 %collective-permute-start.17 = (f32[8,88,128]{2,1,0:T(8,128)S(1)}, f32[8,88,128]{2,1,0:T(8,128)S(1)}, u32[]{:S(2)}, u32[]{:S(2)}) collective-permute-start(f32[8,88,128]{2,1,0:T(8,128)S(1)} %get-tuple-element.61), channel_id=1, source_target_pairs={{0,64},{1,65},{2,66},{3,67},{4,68},{5,69},{6,70},{7,71},{16,80},{1... | collective-permute-start | bytes 1081352 | tf_op jit(solution)/shard_map/ppermute | solution.py:444
  110.8 17.0 %collective-permute-start.18 = (f32[8,88,128]{2,1,0:T(8,128)S(1)}, f32[8,88,128]{2,1,0:T(8,128)S(1)}, u32[]{:S(2)}, u32[]{:S(2)}) collective-permute-start(f32[8,88,128]{2,1,0:T(8,128)S(1)} %get-tuple-element.60), channel_id=1, source_target_pairs={{0,96},{1,97},{2,98},{3,99},{4,100},{5,101},{6,102},{7,103},{16,11... | collective-permute-start | bytes 1081352 | tf_op jit(solution)/shard_map/ppermute | solution.py:444
  119.5 10.6 %collective-permute-start.12 = (f32[2,88,128]{2,1,0:T(8,128)S(1)}, f32[2,88,128]{2,1,0:T(8,128)S(1)}, u32[]{:S(2)}, u32[]{:S(2)}) collective-permute-start(f32[2,88,128]{2,1,0:T(8,128)S(1)} %get-tuple-element.63), channel_id=1, source_target_pairs={{0,32},{1,33},{2,34},{3,35},{4,36},{5,37},{6,38},{7,39},{16,48},{1... | collective-permute-start | bytes 270344 | tf_op jit(solution)/shard_map/ppermute | solution.py:444
  119.6 12.7 %collective-permute-start.13 = (f32[2,88,128]{2,1,0:T(8,128)S(1)}, f32[2,88,128]{2,1,0:T(8,128)S(1)}, u32[]{:S(2)}, u32[]{:S(2)}) collective-permute-start(f32[2,88,128]{2,1,0:T(8,128)S(1)} %get-tuple-element.65), channel_id=1, source_target_pairs={{0,64},{1,65},{2,66},{3,67},{4,68},{5,69},{6,70},{7,71},{16,80},{1... | collective-permute-start | bytes 270344 | tf_op jit(solution)/shard_map/ppermute | solution.py:444
  127.9 7.2 %collective-permute-start.19 = (f32[2,88,128]{2,1,0:T(8,128)S(1)}, f32[2,88,128]{2,1,0:T(8,128)S(1)}, u32[]{:S(2)}, u32[]{:S(2)}) collective-permute-start(f32[2,88,128]{2,1,0:T(8,128)S(1)} %get-tuple-element.66), channel_id=1, source_target_pairs={{0,2},{1,3},{2,4},{3,5},{4,6},{5,7},{6,0},{7,1},{16,18},{17,19},{1... | collective-permute-start | bytes 270344 | tf_op jit(solution)/shard_map/ppermute | solution.py:444
  128.0 7.1 %collective-permute-start.20 = (f32[2,88,128]{2,1,0:T(8,128)S(1)}, f32[2,88,128]{2,1,0:T(8,128)S(1)}, u32[]{:S(2)}, u32[]{:S(2)}) collective-permute-start(f32[2,88,128]{2,1,0:T(8,128)S(1)} %get-tuple-element.68), channel_id=1, source_target_pairs={{0,4},{1,5},{2,6},{3,7},{4,0},{5,1},{6,2},{7,3},{16,20},{17,21},{1... | collective-permute-start | bytes 270344 | tf_op jit(solution)/shard_map/ppermute | solution.py:444
  130.0 5.6 %collective-permute-start.21 = (f32[2,88,128]{2,1,0:T(8,128)S(1)}, f32[2,88,128]{2,1,0:T(8,128)S(1)}, u32[]{:S(2)}, u32[]{:S(2)}) collective-permute-start(f32[2,88,128]{2,1,0:T(8,128)S(1)} %get-tuple-element.67), channel_id=1, source_target_pairs={{0,6},{1,7},{2,0},{3,1},{4,2},{5,3},{6,4},{7,5},{16,22},{17,23},{1... | collective-permute-start | bytes 270344 | tf_op jit(solution)/shard_map/ppermute | solution.py:444
  135.8 4.8 %collective-permute-start.22 = (f32[88,128]{1,0:T(8,128)S(1)}, f32[88,128]{1,0:T(8,128)S(1)}, u32[]{:S(2)}, u32[]{:S(2)}) collective-permute-start(f32[88,128]{1,0:T(8,128)S(1)} %slice_bitcast_fusion.2), channel_id=1, source_target_pairs={{0,16},{1,17},{2,18},{3,19},{4,20},{5,21},{6,22},{7,23},{16,0},{17... | collective-permute-start | bytes 135176 | tf_op jit(solution)/shard_map/ppermute | solution.py:502
  135.9 5.6 %collective-permute-start.23 = (f32[88,128]{1,0:T(8,128)S(1)}, f32[88,128]{1,0:T(8,128)S(1)}, u32[]{:S(2)}, u32[]{:S(2)}) collective-permute-start(f32[88,128]{1,0:T(8,128)S(1)} %get-tuple-element.70), channel_id=1, source_target_pairs={{0,8},{1,9},{2,10},{3,11},{4,12},{5,13},{6,14},{7,15},{16,24},{17,... | collective-permute-start | bytes 135176 | tf_op jit(solution)/shard_map/ppermute | solution.py:503
  138.6 5.3 %collective-permute-start.24 = (f32[88,128]{1,0:T(8,128)S(1)}, f32[88,128]{1,0:T(8,128)S(1)}, u32[]{:S(2)}, u32[]{:S(2)}) collective-permute-start(f32[88,128]{1,0:T(8,128)S(1)} %get-tuple-element.69), channel_id=1, source_target_pairs={{0,24},{1,25},{2,26},{3,27},{4,28},{5,29},{6,30},{7,31},{16,8},{17... | collective-permute-start | bytes 135176 | tf_op jit(solution)/shard_map/ppermute | solution.py:503
  (9 other events, 105.4 us)

commit v5 on v4

--- a/solution.py
+++ b/solution.py
@@ -445,6 +445,18 @@
     return (parts[0] + sent[0]) + (sent[1] + sent[2])
 
 
+def ring_sum(parts, **axis):
+    (name,) = axis
+    up, down = moved(**{name: 1}), moved(**{name: -1})
+    from_below = lax.ppermute(parts[3:5], ALL, up)
+    from_above = lax.ppermute(parts[5:7], ALL, down)
+    last_below = lax.ppermute(parts[2] + from_below[1], ALL, up)
+    last_above = lax.ppermute(parts[7] + from_above[0], ALL, down)
+    return jnp.stack(
+        [parts[0] + from_above[1] + last_below, parts[1] + from_below[0] + last_above]
+    )
+
+
 def shards(pool, vec_ids, winds, wind_ids, mixing, basis):
     lat_index = lax.axis_index("lat").astype(jnp.int32)
     lon_index = lax.axis_index("lon").astype(jnp.int32)
@@ -493,7 +505,7 @@
     )
     second = mine + lax.ppermute(theirs, ALL, moved(dc=1))
 
-    first = line_sum(first.reshape(4, 8, BLOCK, 128), dz=1)
+    first = ring_sum(first.reshape(8, 4, BLOCK, 128), dz=1)
     second = line_sum(second.reshape(4, 8, BLOCK, 128), dx=1)
     first = line_sum(first.reshape(4, 2, BLOCK, 128), dx=1)
     second = line_sum(second.reshape(4, 2, BLOCK, 128), dz=1)

time: 145 us -> 152 us (1.048)
  waiting for transfers between devices: 45 us -> 65.1 us
  starting transfers between devices: 58.1 us -> 45.3 us
    ppermute x12 -> x9, waiting for transfers between devices: 3.45 us -> 18.8 us  [line_sum(): sent = [lax.ppermute(parts[k], ALL, moved(**{name: k})) for k in (1, 2, 3)]]
    ppermute x12 -> x9, starting transfers between devices: 34.6 us -> 19.5 us  [line_sum(): sent = [lax.ppermute(parts[k], ALL, moved(**{name: k})) for k in (1, 2, 3)]]
    ppermute x1, waiting for transfers between devices: 0.01 us -> 2.55 us  [shards(): second = mine + lax.ppermute(theirs, ALL, moved(dc=1))]
    ppermute x0 -> x4, waiting for transfers between devices: none -> 2.38 us  [the longest x1 2.37 us: ring_sum(): last_above = lax.ppermute(parts[7] + from_above[0], ALL, down)]
    ppermute x0 -> x4, starting transfers between devices: none -> 2.31 us  [the longest x1 1.43 us: ring_sum(): last_below = lax.ppermute(parts[2] + from_below[1], ALL, up)]
  transfers between devices with their start and end apart: 25 -> 26, of which waited for: 10 -> 14; matrix products, arithmetic and copies ran while one was open for 2% -> 1% of each run, Pallas kernels for 22% -> 21%
where the time goes in v5:
time: 152 us
  waiting for transfers between devices  65.1 us (43%)
  starting transfers between devices  45.3 us (30%)
  Pallas kernels  36.6 us (24%)
  local copies, waits for them, and re-layouts  2.61 us (2%)
    pallas_call x2, Pallas kernels, window(): pl.pallas_call(functools.partial(window_kernel, part), out_shape=[jax.Sha...  26.8 us
    ppermute x9, starting transfers between devices, line_sum(): sent = [lax.ppermute(parts[k], ALL, moved(**{name: k})) for k in (1, 2, 3)]  19.5 us
    ppermute x9, waiting for transfers between devices, line_sum(): sent = [lax.ppermute(parts[k], ALL, moved(**{name: k})) for k in (1, 2, 3)]  18.8 us
    ppermute x1, waiting for transfers between devices, shards(): west = lax.ppermute(to_east, 'lon', EASTWARD)  17.4 us
    ppermute x1, waiting for transfers between devices, shards(): before_edge = lax.ppermute(edge_next, ALL, FORWARD)  10.7 us
    ppermute x1, starting transfers between devices, shards(): east = lax.ppermute(to_west, 'lon', WESTWARD)  6 us
    ppermute x1, waiting for transfers between devices, shards(): lax.ppermute(bulk[0], ALL, FORWARD)  5.2 us
    ppermute x1, starting transfers between devices, shards(): lax.ppermute(bulk[3], ALL, BACKWARD)  4.94 us
  transfers between devices with their start and end apart: 26, of which 14 were waited for; matrix products, arithmetic and copies ran while one was open for 1% of the time, Pallas kernels for 21%

profile of v5, /device:TPU:0, one launch (start us, length us, event | category | flops | bytes accessed | tf_op | source)
XLA Modules:
  0.0 152.0 jit_solution(9522570602446714680)
XLA Ops:
  1.4 4.0 %lead.1 = (f32[48,1664]{1,0:T(8,128)}, f32[48,1664]{1,0:T(8,128)}) custom-call(s32[7]{0:T(128)} %stack.54.info, s32[8]{0:T(128)} %vec_ids.3, bf16[8,48,1152]{2,1,0:T(8,128)(2,1)} %pool.3, f32[8,48,288]{2,1,0:T(8,128)} %winds.3), custom_call_target="tpu_custom_call" | custom-call | flops 1073741824 | bytes 4194304 | tf_op jit(solution)/shard_map/lead/pallas_call | solution.py:126
  10.6 3.1 %pack.1 = (f32[4,48,1152]{2,1,0:T(8,128)S(1)}, f32[4,48,1152]{2,1,0:T(8,128)S(1)}, f32[8,48,288]{2,1,0:T(8,128)S(1)}, f32[4,40,640]{2,1,0:T(8,128)S(1)}, f32[4,4...) custom-call(s32[7]{0:T(128)S(1)} %copy-done, ...), custom_call_target="tpu_custom_call" | custom-call | flops 1073741824 | bytes 4194304 | tf_op jit(solution)/shard_map/pack/pallas_call | solution.py:182
  13.8 10.7 %collective-permute-done.before.before_edge = f32[48,1664]{1,0:T(8,128)S(1)} collective-permute-done((f32[48,1664]{1,0:T(8,128)}, f32[48,1664]{1,0:T(8,128)S(1)}, u32[]{:S(2)}, u32[]{:S(2)}) %collective-permute-start) | collective-permute-done | bytes 319520 | tf_op jit(solution)/shard_map/ppermute | solution.py:476
  24.5 3.5 %collective-permute-done.1.after.after_edge = f32[48,1664]{1,0:T(8,128)S(1)} collective-permute-done((f32[48,1664]{1,0:T(8,128)}, f32[48,1664]{1,0:T(8,128)S(1)}, u32[]{:S(2)}, u32[]{:S(2)}) %collective-permute-start.1) | collective-permute-done | bytes 319520 | tf_op jit(solution)/shard_map/ppermute | solution.py:477
  28.1 6.0 %collective-permute-start.3 = (f32[18,4,1152]{2,1,0:T(4,128)S(1)}, f32[18,4,1152]{2,1,0:T(4,128)S(1)}, u32[]{:S(2)}, u32[]{:S(2)}) collective-permute-start(f32[18,4,1152]{2,1,0:T(4,128)S(1)} %get-tuple-element.37), channel_id=1, source_target_pairs={{1,0},{2,1},{3,2},{4,3},{5,4},{6,5},{7,6},{8,7},{9,8},{10,9},{11,1... | collective-permute-start | bytes 995336 | tf_op jit(solution)/shard_map/ppermute | solution.py:485
  34.3 3.5 %collective-permute-start.5 = (f32[4,40,640]{2,1,0:T(8,128)S(1)}, f32[4,40,640]{2,1,0:T(8,128)S(1)}, u32[]{:S(2)}, u32[]{:S(2)}) collective-permute-start(f32[4,40,640]{2,1,0:T(8,128)S(1)} %get-tuple-element.42), channel_id=1, source_target_pairs={{16,0},{0,8},{32,16},{8,24},{48,32},{24,40},{64,48},{40,56},{80,64... | collective-permute-start | bytes 1228808 | tf_op jit(solution)/shard_map/ppermute | solution.py:486
  37.8 17.4 %collective-permute-done.2.west = f32[18,4,1152]{2,1,0:T(4,128)S(1)} collective-permute-done((f32[18,4,1152]{2,1,0:T(4,128)S(1)}, f32[18,4,1152]{2,1,0:T(4,128)S(1)}, u32[]{:S(2)}, u32[]{:S(2)}) %collective-permute-start.2) | collective-permute-done | bytes 331808 | tf_op jit(solution)/shard_map/ppermute | solution.py:484
  55.2 4.9 %collective-permute-start.7 = (f32[4,40,512]{2,1,0:T(8,128)S(1)}, f32[4,40,512]{2,1,0:T(8,128)S(1)}, u32[]{:S(2)}, u32[]{:S(2)}) collective-permute-start(f32[4,40,512]{2,1,0:T(8,128)S(1)} %get-tuple-element.44), channel_id=1, source_target_pairs={{16,0},{0,8},{32,16},{8,24},{48,32},{24,40},{64,48},{40,56},{80,64... | collective-permute-start | bytes 983048 | tf_op jit(solution)/shard_map/ppermute | solution.py:487
  60.2 2.6 %frame.1 = (f32[14,64,288]{2,1,0:T(8,128)S(1)}, f32[4,14,64,640]{3,2,1,0:T(8,128)S(1)}) custom-call(s32[7]{0:T(128)S(1)} %copy-done, f32[48,1664]{1,0:T(8,128)S(1)} %collective-permute-done.before.before_edge, f32[48,1664]{1,0:T(8,128)S(1)} %collective-permute-done.1.after.after_edge, f32[8,48,288]{2,1,0:T(8,128)S(1)} %get-tuple-element.31.wind, ...), custom_call_target="tpu_custom_call" | custom-call | flops 17179869184 | bytes 4194304 | tf_op jit(solution)/shard_map/frame/pallas_call | solution.py:271
  62.8 5.2 %collective-permute-done.4.before_0 = f32[4,40,640]{2,1,0:T(8,128)S(1)} collective-permute-done((f32[4,40,640]{2,1,0:T(8,128)S(1)}, f32[4,40,640]{2,1,0:T(8,128)S(1)}, u32[]{:S(2)}, u32[]{:S(2)}) %collective-permute-start.4) | collective-permute-done | bytes 409632 | tf_op jit(solution)/shard_map/ppermute | solution.py:486
  69.5 13.4 %window_0.1 = (f32[8,48,640]{2,1,0:T(8,128)S(1)}, f32[32,88,128]{2,1,0:T(8,128)S(1)}, f32[32,88,128]{2,1,0:T(8,128)S(1)}) custom-call(s32[7]{0:T(128)S(1)} %copy-done, s32[4]{0:T(128)S(1)} %copy-done.5, f32[8]{0:T(128)S(1)} %add_cosine_fusion.cosine, f32[48,1664]{1,0:T(8,128)S(1)} %collective-permute-done.before.before_edge, ...), custom_call_target="tpu_custom_call" | custom-call | flops 8589934592 | bytes 16777216 | tf_op jit(solution)/shard_map/window_0/pallas_call | solution.py:419
  83.1 13.4 %window_1.1 = (f32[8,48,1152]{2,1,0:T(8,128)}, f32[32,88,128]{2,1,0:T(8,128)S(1)}, f32[32,88,128]{2,1,0:T(8,128)S(1)}) custom-call(s32[7]{0:T(128)S(1)} %copy-done, s32[4]{0:T(128)S(1)} %copy-done.5, f32[8]{0:T(128)S(1)} %add_cosine_fusion.cosine, f32[48,1664]{1,0:T(8,128)S(1)} %collective-permute-done.before.before_edge, ...), custom_call_target="tpu_custom_call" | custom-call | flops 8589934592 | bytes 16777216 | tf_op jit(solution)/shard_map/window_1/pallas_call | solution.py:419
  97.2 2.5 %collective-permute-done.16 = f32[32,88,128]{2,1,0:T(8,128)S(1)} collective-permute-done((f32[32,88,128]{2,1,0:T(8,128)S(1)}, f32[32,88,128]{2,1,0:T(8,128)S(1)}, u32[]{:S(2)}, u32[]{:S(2)}) %collective-permute-start.16) | collective-permute-done | bytes 1441824 | tf_op jit(solution)/shard_map/ppermute | solution.py:506
  100.1 10.8 %collective-permute-start.18 = (f32[8,88,128]{2,1,0:T(8,128)S(1)}, f32[8,88,128]{2,1,0:T(8,128)S(1)}, u32[]{:S(2)}, u32[]{:S(2)}) collective-permute-start(f32[8,88,128]{2,1,0:T(8,128)S(1)} %get-tuple-element.62), channel_id=1, source_target_pairs={{0,64},{1,65},{2,66},{3,67},{4,68},{5,69},{6,70},{7,71},{16,80},{1... | collective-permute-start | bytes 1081352 | tf_op jit(solution)/shard_map/ppermute | solution.py:444
  113.0 5.3 %collective-permute-done.17 = f32[8,88,128]{2,1,0:T(8,128)S(1)} collective-permute-done((f32[8,88,128]{2,1,0:T(8,128)S(1)}, f32[8,88,128]{2,1,0:T(8,128)S(1)}, u32[]{:S(2)}, u32[]{:S(2)}) %collective-permute-start.17) | collective-permute-done | bytes 360480 | tf_op jit(solution)/shard_map/ppermute | solution.py:444
  118.3 8.9 %collective-permute-done.18 = f32[8,88,128]{2,1,0:T(8,128)S(1)} collective-permute-done((f32[8,88,128]{2,1,0:T(8,128)S(1)}, f32[8,88,128]{2,1,0:T(8,128)S(1)}, u32[]{:S(2)}, u32[]{:S(2)}) %collective-permute-start.18) | collective-permute-done | bytes 360480 | tf_op jit(solution)/shard_map/ppermute | solution.py:444
  127.6 2.2 %collective-permute-start.20 = (f32[2,88,128]{2,1,0:T(8,128)S(1)}, f32[2,88,128]{2,1,0:T(8,128)S(1)}, u32[]{:S(2)}, u32[]{:S(2)}) collective-permute-start(f32[2,88,128]{2,1,0:T(8,128)S(1)} %get-tuple-element.67), channel_id=1, source_target_pairs={{0,2},{1,3},{2,4},{3,5},{4,6},{5,7},{6,0},{7,1},{16,18},{17,19},{1... | collective-permute-start | bytes 270344 | tf_op jit(solution)/shard_map/ppermute | solution.py:444
  129.8 2.8 %collective-permute-start.22 = (f32[2,88,128]{2,1,0:T(8,128)S(1)}, f32[2,88,128]{2,1,0:T(8,128)S(1)}, u32[]{:S(2)}, u32[]{:S(2)}) collective-permute-start(f32[2,88,128]{2,1,0:T(8,128)S(1)} %get-tuple-element.68), channel_id=1, source_target_pairs={{0,6},{1,7},{2,0},{3,1},{4,2},{5,3},{6,4},{7,5},{16,22},{17,23},{1... | collective-permute-start | bytes 270344 | tf_op jit(solution)/shard_map/ppermute | solution.py:444
  132.6 2.4 %collective-permute-done.12 = f32[4,88,128]{2,1,0:T(8,128)S(1)} collective-permute-done((f32[4,88,128]{2,1,0:T(8,128)S(1)}, f32[4,88,128]{2,1,0:T(8,128)S(1)}, u32[]{:S(2)}, u32[]{:S(2)}) %collective-permute-start.12) | collective-permute-done | bytes 180256 | tf_op jit(solution)/shard_map/ppermute | solution.py:454
  135.2 3.5 %collective-permute-start.14 = (f32[2,88,128]{2,1,0:T(8,128)S(1)}, f32[2,88,128]{2,1,0:T(8,128)S(1)}, u32[]{:S(2)}, u32[]{:S(2)}) collective-permute-start(f32[2,88,128]{2,1,0:T(8,128)S(1)} %get-tuple-element.66), channel_id=1, source_target_pairs={{0,64},{1,65},{2,66},{3,67},{4,68},{5,69},{6,70},{7,71},{16,80},{1... | collective-permute-start | bytes 270344 | tf_op jit(solution)/shard_map/ppermute | solution.py:444
  138.7 2.2 %collective-permute-done.13 = f32[2,88,128]{2,1,0:T(8,128)S(1)} collective-permute-done((f32[2,88,128]{2,1,0:T(8,128)S(1)}, f32[2,88,128]{2,1,0:T(8,128)S(1)}, u32[]{:S(2)}, u32[]{:S(2)}) %collective-permute-start.13) | collective-permute-done | bytes 90144 | tf_op jit(solution)/shard_map/ppermute | solution.py:444
  143.4 2.5 %collective-permute-start.24 = (f32[88,128]{1,0:T(8,128)S(1)}, f32[88,128]{1,0:T(8,128)S(1)}, u32[]{:S(2)}, u32[]{:S(2)}) collective-permute-start(f32[88,128]{1,0:T(8,128)S(1)} %get-tuple-element.71), channel_id=1, source_target_pairs={{0,8},{1,9},{2,10},{3,11},{4,12},{5,13},{6,14},{7,15},{16,24},{17,... | collective-permute-start | bytes 135176 | tf_op jit(solution)/shard_map/ppermute | solution.py:515
  145.9 2.2 %collective-permute-start.25 = (f32[88,128]{1,0:T(8,128)S(1)}, f32[88,128]{1,0:T(8,128)S(1)}, u32[]{:S(2)}, u32[]{:S(2)}) collective-permute-start(f32[88,128]{1,0:T(8,128)S(1)} %get-tuple-element.70), channel_id=1, source_target_pairs={{0,24},{1,25},{2,26},{3,27},{4,28},{5,29},{6,30},{7,31},{16,8},{17... | collective-permute-start | bytes 135176 | tf_op jit(solution)/shard_map/ppermute | solution.py:515
  149.0 2.1 %collective-permute-done.25 = f32[88,128]{1,0:T(8,128)S(1)} collective-permute-done((f32[88,128]{1,0:T(8,128)S(1)}, f32[88,128]{1,0:T(8,128)S(1)}, u32[]{:S(2)}, u32[]{:S(2)}) %collective-permute-start.25) | collective-permute-done | bytes 45088 | tf_op jit(solution)/shard_map/ppermute | solution.py:515
  (83 shorter events, 15.8 us)
Async XLA Ops:
  5.4 19.0 %collective-permute-start = (f32[48,1664]{1,0:T(8,128)}, f32[48,1664]{1,0:T(8,128)S(1)}, u32[]{:S(2)}, u32[]{:S(2)}) collective-permute-start(f32[48,1664]{1,0:T(8,128)} %get-tuple-element.27), channel_id=1, source_target_pairs={{0,16},{8,0},{16,32},{24,8},{32,48},{40,24},{48,64},{56,40},{64,80... | collective-permute-start | bytes 958472 | tf_op jit(solution)/shard_map/ppermute | solution.py:476
  7.1 20.8 %collective-permute-start.1 = (f32[48,1664]{1,0:T(8,128)}, f32[48,1664]{1,0:T(8,128)S(1)}, u32[]{:S(2)}, u32[]{:S(2)}) collective-permute-start(f32[48,1664]{1,0:T(8,128)} %get-tuple-element.30), channel_id=1, source_target_pairs={{16,0},{0,8},{32,16},{8,24},{48,32},{24,40},{64,48},{40,56},{80,64... | collective-permute-start | bytes 958472 | tf_op jit(solution)/shard_map/ppermute | solution.py:477
  28.1 27.2 %collective-permute-start.2 = (f32[18,4,1152]{2,1,0:T(4,128)S(1)}, f32[18,4,1152]{2,1,0:T(4,128)S(1)}, u32[]{:S(2)}, u32[]{:S(2)}) collective-permute-start(f32[18,4,1152]{2,1,0:T(4,128)S(1)} %get-tuple-element.36), channel_id=1, source_target_pairs={{0,1},{1,2},{2,3},{3,4},{4,5},{5,6},{6,7},{7,8},{8,9},{9,10},{10,1... | collective-permute-start | bytes 995336 | tf_op jit(solution)/shard_map/ppermute | solution.py:484
  28.1 32.0 %collective-permute-start.3 = (f32[18,4,1152]{2,1,0:T(4,128)S(1)}, f32[18,4,1152]{2,1,0:T(4,128)S(1)}, u32[]{:S(2)}, u32[]{:S(2)}) collective-permute-start(f32[18,4,1152]{2,1,0:T(4,128)S(1)} %get-tuple-element.37), channel_id=1, source_target_pairs={{1,0},{2,1},{3,2},{4,3},{5,4},{6,5},{7,6},{8,7},{9,8},{10,9},{11,1... | collective-permute-start | bytes 995336 | tf_op jit(solution)/shard_map/ppermute | solution.py:485
  34.2 33.7 %collective-permute-start.4 = (f32[4,40,640]{2,1,0:T(8,128)S(1)}, f32[4,40,640]{2,1,0:T(8,128)S(1)}, u32[]{:S(2)}, u32[]{:S(2)}) collective-permute-start(f32[4,40,640]{2,1,0:T(8,128)S(1)} %get-tuple-element.41), channel_id=1, source_target_pairs={{0,16},{8,0},{16,32},{24,8},{32,48},{40,24},{48,64},{56,40},{64,80... | collective-permute-start | bytes 1228808 | tf_op jit(solution)/shard_map/ppermute | solution.py:486
  34.3 35.2 %collective-permute-start.5 = (f32[4,40,640]{2,1,0:T(8,128)S(1)}, f32[4,40,640]{2,1,0:T(8,128)S(1)}, u32[]{:S(2)}, u32[]{:S(2)}) collective-permute-start(f32[4,40,640]{2,1,0:T(8,128)S(1)} %get-tuple-element.42), channel_id=1, source_target_pairs={{16,0},{0,8},{32,16},{8,24},{48,32},{24,40},{64,48},{40,56},{80,64... | collective-permute-start | bytes 1228808 | tf_op jit(solution)/shard_map/ppermute | solution.py:486
  37.8 45.3 %collective-permute-start.6 = (f32[4,40,512]{2,1,0:T(8,128)S(1)}, f32[4,40,512]{2,1,0:T(8,128)S(1)}, u32[]{:S(2)}, u32[]{:S(2)}) collective-permute-start(f32[4,40,512]{2,1,0:T(8,128)S(1)} %get-tuple-element.43), channel_id=1, source_target_pairs={{0,16},{8,0},{16,32},{24,8},{32,48},{40,24},{48,64},{56,40},{64,80... | collective-permute-start | bytes 983048 | tf_op jit(solution)/shard_map/ppermute | solution.py:487
  55.2 27.8 %collective-permute-start.7 = (f32[4,40,512]{2,1,0:T(8,128)S(1)}, f32[4,40,512]{2,1,0:T(8,128)S(1)}, u32[]{:S(2)}, u32[]{:S(2)}) collective-permute-start(f32[4,40,512]{2,1,0:T(8,128)S(1)} %get-tuple-element.44), channel_id=1, source_target_pairs={{16,0},{0,8},{32,16},{8,24},{48,32},{24,40},{64,48},{40,56},{80,64... | collective-permute-start | bytes 983048 | tf_op jit(solution)/shard_map/ppermute | solution.py:487
  83.0 13.9 %collective-permute-start.8 = (f32[32,88,128]{2,1,0:T(8,128)S(1)}, f32[32,88,128]{2,1,0:T(8,128)S(1)}, u32[]{:S(2)}, u32[]{:S(2)}) collective-permute-start(f32[32,88,128]{2,1,0:T(8,128)S(1)} %get-tuple-element.49), channel_id=1, source_target_pairs={{0,1},{1,0},{2,3},{3,2},{4,5},{5,4},{6,7},{7,6},{16,17},{17,16},{1... | collective-permute-start | bytes 4325384 | tf_op jit(solution)/shard_map/ppermute | solution.py:502
  97.1 14.4 %collective-permute-start.10 = (f32[2,4,88,128]{3,2,1,0:T(8,128)S(1)}, f32[2,4,88,128]{3,2,1,0:T(8,128)S(1)}, u32[]{:S(2)}, u32[]{:S(2)}) collective-permute-start(f32[2,4,88,128]{3,2,1,0:T(8,128)S(1)} %bitcast.69), channel_id=1, source_target_pairs={{0,2},{1,3},{2,4},{3,5},{4,6},{5,7},{6,0},{7,1},{16,18},{17,19},{1... | collective-permute-start | bytes 1081352 | tf_op jit(solution)/shard_map/ppermute | solution.py:451
  100.0 18.4 %collective-permute-start.17 = (f32[8,88,128]{2,1,0:T(8,128)S(1)}, f32[8,88,128]{2,1,0:T(8,128)S(1)}, u32[]{:S(2)}, u32[]{:S(2)}) collective-permute-start(f32[8,88,128]{2,1,0:T(8,128)S(1)} %get-tuple-element.63), channel_id=1, source_target_pairs={{0,32},{1,33},{2,34},{3,35},{4,36},{5,37},{6,38},{7,39},{16,48},{1... | collective-permute-start | bytes 1081352 | tf_op jit(solution)/shard_map/ppermute | solution.py:444
  100.1 27.2 %collective-permute-start.18 = (f32[8,88,128]{2,1,0:T(8,128)S(1)}, f32[8,88,128]{2,1,0:T(8,128)S(1)}, u32[]{:S(2)}, u32[]{:S(2)}) collective-permute-start(f32[8,88,128]{2,1,0:T(8,128)S(1)} %get-tuple-element.62), channel_id=1, source_target_pairs={{0,64},{1,65},{2,66},{3,67},{4,68},{5,69},{6,70},{7,71},{16,80},{1... | collective-permute-start | bytes 1081352 | tf_op jit(solution)/shard_map/ppermute | solution.py:444
  110.9 16.4 %collective-permute-start.19 = (f32[8,88,128]{2,1,0:T(8,128)S(1)}, f32[8,88,128]{2,1,0:T(8,128)S(1)}, u32[]{:S(2)}, u32[]{:S(2)}) collective-permute-start(f32[8,88,128]{2,1,0:T(8,128)S(1)} %get-tuple-element.61), channel_id=1, source_target_pairs={{0,96},{1,97},{2,98},{3,99},{4,100},{5,101},{6,102},{7,103},{16,11... | collective-permute-start | bytes 1081352 | tf_op jit(solution)/shard_map/ppermute | solution.py:444
  110.9 16.5 %collective-permute-start.9 = (f32[2,4,88,128]{3,2,1,0:T(8,128)S(1)}, f32[2,4,88,128]{3,2,1,0:T(8,128)S(1)}, u32[]{:S(2)}, u32[]{:S(2)}) collective-permute-start(f32[2,4,88,128]{3,2,1,0:T(8,128)S(1)} %bitcast.68), channel_id=1, source_target_pairs={{0,6},{1,7},{2,0},{3,1},{4,2},{5,3},{6,4},{7,5},{16,22},{17,23},{1... | collective-permute-start | bytes 1081352 | tf_op jit(solution)/shard_map/ppermute | solution.py:452
  111.6 15.8 %collective-permute-start.11 = (f32[4,88,128]{2,1,0:T(8,128)S(1)}, f32[4,88,128]{2,1,0:T(8,128)S(1)}, u32[]{:S(2)}, u32[]{:S(2)}) collective-permute-start(f32[4,88,128]{2,1,0:T(8,128)S(1)} %fusion.5), channel_id=1, source_target_pairs={{0,2},{1,3},{2,4},{3,5},{4,6},{5,7},{6,0},{7,1},{16,18},{17,19},{1... | collective-permute-start | bytes 540680 | tf_op jit(solution)/shard_map/ppermute | solution.py:453
  127.4 7.5 %collective-permute-start.12 = (f32[4,88,128]{2,1,0:T(8,128)S(1)}, f32[4,88,128]{2,1,0:T(8,128)S(1)}, u32[]{:S(2)}, u32[]{:S(2)}) collective-permute-start(f32[4,88,128]{2,1,0:T(8,128)S(1)} %get-tuple-element.58), channel_id=1, source_target_pairs={{0,6},{1,7},{2,0},{3,1},{4,2},{5,3},{6,4},{7,5},{16,22},{17,23},{1... | collective-permute-start | bytes 540680 | tf_op jit(solution)/shard_map/ppermute | solution.py:454
  127.6 11.1 %collective-permute-start.20 = (f32[2,88,128]{2,1,0:T(8,128)S(1)}, f32[2,88,128]{2,1,0:T(8,128)S(1)}, u32[]{:S(2)}, u32[]{:S(2)}) collective-permute-start(f32[2,88,128]{2,1,0:T(8,128)S(1)} %get-tuple-element.67), channel_id=1, source_target_pairs={{0,2},{1,3},{2,4},{3,5},{4,6},{5,7},{6,0},{7,1},{16,18},{17,19},{1... | collective-permute-start | bytes 270344 | tf_op jit(solution)/shard_map/ppermute | solution.py:444
  129.8 8.9 %collective-permute-start.21 = (f32[2,88,128]{2,1,0:T(8,128)S(1)}, f32[2,88,128]{2,1,0:T(8,128)S(1)}, u32[]{:S(2)}, u32[]{:S(2)}) collective-permute-start(f32[2,88,128]{2,1,0:T(8,128)S(1)} %get-tuple-element.69), channel_id=1, source_target_pairs={{0,4},{1,5},{2,6},{3,7},{4,0},{5,1},{6,2},{7,3},{16,20},{17,21},{1... | collective-permute-start | bytes 270344 | tf_op jit(solution)/shard_map/ppermute | solution.py:444
  129.8 8.9 %collective-permute-start.22 = (f32[2,88,128]{2,1,0:T(8,128)S(1)}, f32[2,88,128]{2,1,0:T(8,128)S(1)}, u32[]{:S(2)}, u32[]{:S(2)}) collective-permute-start(f32[2,88,128]{2,1,0:T(8,128)S(1)} %get-tuple-element.68), channel_id=1, source_target_pairs={{0,6},{1,7},{2,0},{3,1},{4,2},{5,3},{6,4},{7,5},{16,22},{17,23},{1... | collective-permute-start | bytes 270344 | tf_op jit(solution)/shard_map/ppermute | solution.py:444
  135.1 5.8 %collective-permute-start.13 = (f32[2,88,128]{2,1,0:T(8,128)S(1)}, f32[2,88,128]{2,1,0:T(8,128)S(1)}, u32[]{:S(2)}, u32[]{:S(2)}) collective-permute-start(f32[2,88,128]{2,1,0:T(8,128)S(1)} %get-tuple-element.64), channel_id=1, source_target_pairs={{0,32},{1,33},{2,34},{3,35},{4,36},{5,37},{6,38},{7,39},{16,48},{1... | collective-permute-start | bytes 270344 | tf_op jit(solution)/shard_map/ppermute | solution.py:444
  135.2 7.0 %collective-permute-start.14 = (f32[2,88,128]{2,1,0:T(8,128)S(1)}, f32[2,88,128]{2,1,0:T(8,128)S(1)}, u32[]{:S(2)}, u32[]{:S(2)}) collective-permute-start(f32[2,88,128]{2,1,0:T(8,128)S(1)} %get-tuple-element.66), channel_id=1, source_target_pairs={{0,64},{1,65},{2,66},{3,67},{4,68},{5,69},{6,70},{7,71},{16,80},{1... | collective-permute-start | bytes 270344 | tf_op jit(solution)/shard_map/ppermute | solution.py:444
  143.3 4.8 %collective-permute-start.23 = (f32[88,128]{1,0:T(8,128)S(1)}, f32[88,128]{1,0:T(8,128)S(1)}, u32[]{:S(2)}, u32[]{:S(2)}) collective-permute-start(f32[88,128]{1,0:T(8,128)S(1)} %slice_bitcast_fusion.10), channel_id=1, source_target_pairs={{0,16},{1,17},{2,18},{3,19},{4,20},{5,21},{6,22},{7,23},{16,0},{17... | collective-permute-start | bytes 135176 | tf_op jit(solution)/shard_map/ppermute | solution.py:514
  143.4 5.6 %collective-permute-start.24 = (f32[88,128]{1,0:T(8,128)S(1)}, f32[88,128]{1,0:T(8,128)S(1)}, u32[]{:S(2)}, u32[]{:S(2)}) collective-permute-start(f32[88,128]{1,0:T(8,128)S(1)} %get-tuple-element.71), channel_id=1, source_target_pairs={{0,8},{1,9},{2,10},{3,11},{4,12},{5,13},{6,14},{7,15},{16,24},{17,... | collective-permute-start | bytes 135176 | tf_op jit(solution)/shard_map/ppermute | solution.py:515
  145.9 5.3 %collective-permute-start.25 = (f32[88,128]{1,0:T(8,128)S(1)}, f32[88,128]{1,0:T(8,128)S(1)}, u32[]{:S(2)}, u32[]{:S(2)}) collective-permute-start(f32[88,128]{1,0:T(8,128)S(1)} %get-tuple-element.70), channel_id=1, source_target_pairs={{0,24},{1,25},{2,26},{3,27},{4,28},{5,29},{6,30},{7,31},{16,8},{17... | collective-permute-start | bytes 135176 | tf_op jit(solution)/shard_map/ppermute | solution.py:515
  (10 other events, 108.2 us)

commit v6 on v4

--- a/solution.py
+++ b/solution.py
@@ -62,7 +62,9 @@
 
 
 FORWARD = meridian()
-BACKWARD = [(t, s) for s, t in FORWARD]
+CIRCLE = FORWARD + [(t, s) for s, t in FORWARD]
+SWAP_A = [(s, t) for s, t in CIRCLE if s // 16 // 2 == t // 16 // 2 and s // 16 != t // 16]
+SWAP_B = [pair for pair in CIRCLE if pair not in SWAP_A]
 EASTWARD = [(b, (b + 1) % 16) for b in range(16)]
 WESTWARD = [(t, s) for s, t in EASTWARD]
 
@@ -90,7 +92,7 @@
 
 
 def lead_kernel(
-    info, vec_ids, pool, winds, edge_next, edge_last, chosen, ends, held_winds, made, sems
+    info, vec_ids, pool, winds, edge_a, edge_b, chosen, ends, held_winds, made, sems
 ):
     fetch = [
         pltpu.make_async_copy(pool.at[:, :16, :], ends.at[0], sems.at[0]),
@@ -107,7 +109,8 @@
         picked = jnp.dot(rows, chosen[...], preferred_element_type=jnp.float32)
         made[i] = picked.reshape(ROWS, 16, CH)
     for r in range(4):
-        for edge, row in ((edge_last, r), (edge_next, 4 + r)):
+        for edge, flag in ((edge_a, info[7]), (edge_b, 1 - info[7])):
+            row = jnp.where(flag == 0, 4 + r, r)
             own = jnp.where(info[0] == 0, row, ROWS - 1 - row)
             for m in range(CH // 128):
                 lanes = slice(m * 128, (m + 1) * 128)
@@ -117,8 +120,9 @@
                 )
     for r in range(3):
         lanes = slice(r * WCH, (r + 1) * WCH)
-        edge_last[:, lanes] = turned_wind(held_winds, info, r)
-        edge_next[:, lanes] = turned_wind(held_winds, info, ROWS - 3 + r)
+        for edge, flag in ((edge_a, info[7]), (edge_b, 1 - info[7])):
+            row = jnp.where(flag == 0, ROWS - 3 + r, r)
+            edge[:, lanes] = turned_wind(held_winds, info, row)
 
 
 def lead(info, vec_ids, pool, winds):
@@ -144,7 +148,7 @@
 
 def pack_kernel(
     info, vec_ids, pool, winds, basis,
-    low, high, wind, next_0, next_1, last_0, last_1, basis_main, basis_rest, chosen,
+    low, high, wind, a_0, a_1, b_0, b_1, basis_main, basis_rest, chosen,
 ):
     choose(vec_ids, chosen)
     for half in range(2):
@@ -161,10 +165,11 @@
             for r in range(4):
                 (high, low)[half][3 - r] = picked[r]
 
-    for rows, bulk_0, bulk_1 in ((high, next_0, next_1), (low, last_0, last_1)):
+    for flag, bulk_0, bulk_1 in ((info[7], a_0, a_1), (1 - info[7], b_0, b_1)):
         for r in range(4):
-            bulk_0[r] = rows[r, 4 : COLS - 4, :PART]
-            bulk_1[r] = rows[r, 4 : COLS - 4, PART:]
+            line = jnp.where(flag == 0, high[r, 4 : COLS - 4, :], low[r, 4 : COLS - 4, :])
+            bulk_0[r] = line[:, :PART]
+            bulk_1[r] = line[:, PART:]
     for r in range(ROWS):
         wind[r] = turned_wind(winds, info, r)
     flat = basis[...].reshape(ROWS * COLS, CH)
@@ -285,10 +290,10 @@
 def window_kernel(
     part, info, wind_ids, cosine,
     before_edge, low, high, after_edge, west, east, wind_ext,
-    levels, mix, basis_main, basis_rest, before_0, after_0,
+    levels, mix, basis_main, basis_rest, a_0, b_0,
     *others,
 ):
-    before_1, after_1, earlier = others[:3] if part else (None, None, None)
+    a_1, b_1, earlier = others[:3] if part else (None, None, None)
     out, mine, theirs, state_a, state_b, weighted, gram, rest, *spread = others[3 * part :]
     spread = spread[0] if spread else None
     flip, mx, my, mz, mc, turn_west, turn_east = (info[i] for i in range(7))
@@ -298,16 +303,13 @@
     for r in range(4):
         state_a[4 + r, FIRST : FIRST + COLS] = low[r, :, lanes]
         state_a[8 + r, FIRST : FIRST + COLS] = high[r, :, lanes]
-        for row, edge, bulk_0, bulk_1 in (
-            (r, before_edge, before_0, before_1),
-            (12 + r, after_edge, after_0, after_1),
-        ):
+        for row, edge, flag in ((r, before_edge, 1 - info[7]), (12 + r, after_edge, info[7])):
             middle = slice(FIRST + 4, FIRST + COLS - 4)
             if part:
-                state_a[row, middle, :128] = bulk_0[r, :, 512:]
-                state_a[row, middle, 128:] = bulk_1[r]
+                state_a[row, middle, :128] = jnp.where(flag == 0, a_0[r, :, 512:], b_0[r, :, 512:])
+                state_a[row, middle, 128:] = jnp.where(flag == 0, a_1[r], b_1[r])
             else:
-                state_a[row, middle] = bulk_0[r]
+                state_a[row, middle] = jnp.where(flag == 0, a_0[r], b_0[r])
             for m in range(PART // 128):
                 tile = slice(m * 128, (m + 1) * 128)
                 where = edge_tile(r, m + part * 4)
@@ -458,21 +460,23 @@
             lon_index % 2,
             (lon_index % 8 == 0).astype(jnp.int32),
             (lon_index % 8 == 7).astype(jnp.int32),
+            (lat_index + flip) % 2,
         ]
     )
-    edge_next, edge_last = lead(info, vec_ids, pool, winds)
-    before_edge = lax.ppermute(edge_next, ALL, FORWARD)
-    after_edge = lax.ppermute(edge_last, ALL, BACKWARD)
-    low, high, wind, next_0, next_1, last_0, last_1, basis_main, basis_rest = pack(
+    edge_a, edge_b = lead(info, vec_ids, pool, winds)
+    edge_a, edge_b = lax.ppermute(edge_a, ALL, SWAP_A), lax.ppermute(edge_b, ALL, SWAP_B)
+    before_edge = jnp.where(info[7] == 0, edge_b, edge_a)
+    after_edge = jnp.where(info[7] == 0, edge_a, edge_b)
+    low, high, wind, a_0, a_1, b_0, b_1, basis_main, basis_rest = pack(
         info, vec_ids, pool, winds, basis
     )
     to_east, to_west, *bulk = edges(
-        (before_edge, after_edge, low, high, wind), (next_0, last_0, next_1, last_1)
+        (before_edge, after_edge, low, high, wind), (a_0, b_0, a_1, b_1)
     )
     west = lax.ppermute(to_east, "lon", EASTWARD)
     east = lax.ppermute(to_west, "lon", WESTWARD)
-    before_0, after_0 = lax.ppermute(bulk[0], ALL, FORWARD), lax.ppermute(bulk[1], ALL, BACKWARD)
-    before_1, after_1 = lax.ppermute(bulk[2], ALL, FORWARD), lax.ppermute(bulk[3], ALL, BACKWARD)
+    a_0, b_0 = lax.ppermute(bulk[0], ALL, SWAP_A), lax.ppermute(bulk[1], ALL, SWAP_B)
+    a_1, b_1 = lax.ppermute(bulk[2], ALL, SWAP_A), lax.ppermute(bulk[3], ALL, SWAP_B)
     levels = jnp.asarray(np.arange(CH, dtype=np.int32)[None] % LEV)
     wind_ext, spread = frame_winds(info, before_edge, after_edge, wind, west, east, levels)
 
@@ -485,11 +489,11 @@
     cosine = jnp.cos((rows + 0.5) * (math.pi / (ROWS * 8)) - math.pi / 2)
     scalars = (info, wind_ids, cosine)
     tile = (before_edge, low, high, after_edge, west, east)
-    arrays = (levels, mix, basis_main, basis_rest, before_0, after_0)
+    arrays = (levels, mix, basis_main, basis_rest, a_0, b_0)
     half, mine, theirs = window(0, scalars, (*tile, wind_ext, *arrays))
     first = mine + lax.ppermute(theirs, ALL, moved(dc=1))
     sensitivity, mine, theirs = window(
-        1, scalars, (*tile, spread, *arrays, before_1, after_1, half)
+        1, scalars, (*tile, spread, *arrays, a_1, b_1, half)
     )
     second = mine + lax.ppermute(theirs, ALL, moved(dc=1))
 

time: 145 us -> 147 us (1.014)
  waiting for transfers between devices: 45 us -> 75.7 us
  starting transfers between devices: 58.1 us -> 28.8 us
    ppermute x12, starting transfers between devices: 34.6 us -> 8.75 us  [line_sum(): sent = [lax.ppermute(parts[k], ALL, moved(**{name: k})) for k in (1, 2, 3)]]
    ppermute x12, waiting for transfers between devices: 3.45 us -> 22.4 us  [line_sum(): sent = [lax.ppermute(parts[k], ALL, moved(**{name: k})) for k in (1, 2, 3)]]
    ppermute x1, waiting for transfers between devices: 17.4 us -> 0.32 us  [shards(): west = lax.ppermute(to_east, 'lon', EASTWARD)]
    ppermute x1, waiting for transfers between devices: 0.01 us -> 17 us  [shards(): east = lax.ppermute(to_west, 'lon', WESTWARD)]
    ppermute x6, waiting for transfers between devices: 20.9 us -> 31.6 us  [the longest x1 10.7 us: shards(): lax.ppermute(edge_b, ALL, SWAP_B)]
    ppermute x6, starting transfers between devices: 12.1 us -> 9.3 us  [the longest x1 3.36 us: shards(): lax.ppermute(edge_b, ALL, SWAP_B)]
    ppermute x1, starting transfers between devices: 0.09 us -> 1.58 us  [shards(): block = near[0] + lax.ppermute(near[1], ALL, turned(1))]
  transfers between devices with their start and end apart: 25 -> 25, of which waited for: 10 -> 16; matrix products, arithmetic and copies ran while one was open for 2% -> 2% of each run, Pallas kernels for 22% -> 22%
where the time goes in v6:
time: 147 us; the launch traced here: 146 us
  waiting for transfers between devices  75.7 us (51%)
  Pallas kernels  36.7 us (25%)
  starting transfers between devices  28.8 us (20%)
  local copies, waits for them, and re-layouts  2.69 us (2%)
    pallas_call x2, Pallas kernels, window(): pl.pallas_call(functools.partial(window_kernel, part), out_shape=[jax.Sha...  26.8 us
    ppermute x12, waiting for transfers between devices, line_sum(): sent = [lax.ppermute(parts[k], ALL, moved(**{name: k})) for k in (1, 2, 3)]  22.4 us
    ppermute x1, waiting for transfers between devices, shards(): east = lax.ppermute(to_west, 'lon', WESTWARD)  17 us
    ppermute x1, waiting for transfers between devices, shards(): lax.ppermute(edge_b, ALL, SWAP_B)  10.7 us
    ppermute x1, waiting for transfers between devices, shards(): lax.ppermute(bulk[1], ALL, SWAP_B)  10.3 us
    ppermute x12, starting transfers between devices, line_sum(): sent = [lax.ppermute(parts[k], ALL, moved(**{name: k})) for k in (1, 2, 3)]  8.75 us
    ppermute x1, waiting for transfers between devices, shards(): lax.ppermute(bulk[0], ALL, SWAP_A)  6.2 us
    ppermute x1, starting transfers between devices, shards(): east = lax.ppermute(to_west, 'lon', WESTWARD)  5.34 us
  transfers between devices with their start and end apart: 25, of which 16 were waited for; matrix products, arithmetic and copies ran while one was open for 2% of the time, Pallas kernels for 22%

profile of v6, /device:TPU:0, one launch (start us, length us, event | category | flops | bytes accessed | tf_op | source)
XLA Modules:
  0.0 146.3 jit_solution(6287450206596752384)
XLA Ops:
  1.4 4.0 %lead.1 = (f32[48,1664]{1,0:T(8,128)}, f32[48,1664]{1,0:T(8,128)}) custom-call(s32[8]{0:T(128)} %stack.49.info, s32[8]{0:T(128)} %vec_ids.3, bf16[8,48,1152]{2,1,0:T(8,128)(2,1)} %pool.3, f32[8,48,288]{2,1,0:T(8,128)} %winds.3), custom_call_target="tpu_custom_call" | custom-call | flops 1073741824 | bytes 4194304 | tf_op jit(solution)/shard_map/lead/pallas_call | solution.py:130
  5.4 3.4 %collective-permute-start = (f32[48,1664]{1,0:T(8,128)}, f32[48,1664]{1,0:T(8,128)S(1)}, u32[]{:S(2)}, u32[]{:S(2)}) collective-permute-start(f32[48,1664]{1,0:T(8,128)} %get-tuple-element.27), channel_id=1, source_target_pairs={{8,0},{16,32},{40,24},{48,64},{72,56},{80,96},{104,88},{112,120},{... | collective-permute-start | bytes 958472 | tf_op jit(solution)/shard_map/ppermute | solution.py:467
  10.5 3.3 %pack.1 = (f32[4,48,1152]{2,1,0:T(8,128)S(1)}, f32[4,48,1152]{2,1,0:T(8,128)S(1)}, f32[8,48,288]{2,1,0:T(8,128)S(1)}, f32[4,40,640]{2,1,0:T(8,128)S(1)}, f32[4,4...) custom-call(s32[8]{0:T(128)S(1)} %copy-done, ...), custom_call_target="tpu_custom_call" | custom-call | flops 1073741824 | bytes 4194304 | tf_op jit(solution)/shard_map/pack/pallas_call | solution.py:187
  13.8 10.7 %collective-permute-done = f32[48,1664]{1,0:T(8,128)S(1)} collective-permute-done((f32[48,1664]{1,0:T(8,128)}, f32[48,1664]{1,0:T(8,128)S(1)}, u32[]{:S(2)}, u32[]{:S(2)}) %collective-permute-start) | collective-permute-done | bytes 319520 | tf_op jit(solution)/shard_map/ppermute | solution.py:467
  24.5 4.4 %collective-permute-done.1 = f32[48,1664]{1,0:T(8,128)S(1)} collective-permute-done((f32[48,1664]{1,0:T(8,128)}, f32[48,1664]{1,0:T(8,128)S(1)}, u32[]{:S(2)}, u32[]{:S(2)}) %collective-permute-start.1) | collective-permute-done | bytes 319520 | tf_op jit(solution)/shard_map/ppermute | solution.py:467
  29.1 5.3 %collective-permute-start.3 = (f32[18,4,1152]{2,1,0:T(4,128)S(1)}, f32[18,4,1152]{2,1,0:T(4,128)S(1)}, u32[]{:S(2)}, u32[]{:S(2)}) collective-permute-start(f32[18,4,1152]{2,1,0:T(4,128)S(1)} %get-tuple-element.37), channel_id=1, source_target_pairs={{1,0},{2,1},{3,2},{4,3},{5,4},{6,5},{7,6},{8,7},{9,8},{10,9},{11,1... | collective-permute-start | bytes 995336 | tf_op jit(solution)/shard_map/ppermute | solution.py:477
  34.5 2.5 %collective-permute-start.4 = (f32[4,40,640]{2,1,0:T(8,128)S(1)}, f32[4,40,640]{2,1,0:T(8,128)S(1)}, u32[]{:S(2)}, u32[]{:S(2)}) collective-permute-start(f32[4,40,640]{2,1,0:T(8,128)S(1)} %get-tuple-element.41), channel_id=1, source_target_pairs={{0,16},{24,8},{32,48},{56,40},{64,80},{88,72},{96,112},{120,104},{... | collective-permute-start | bytes 1228808 | tf_op jit(solution)/shard_map/ppermute | solution.py:478
  37.0 2.0 %collective-permute-start.5 = (f32[4,40,640]{2,1,0:T(8,128)S(1)}, f32[4,40,640]{2,1,0:T(8,128)S(1)}, u32[]{:S(2)}, u32[]{:S(2)}) collective-permute-start(f32[4,40,640]{2,1,0:T(8,128)S(1)} %get-tuple-element.42), channel_id=1, source_target_pairs={{8,0},{16,32},{40,24},{48,64},{72,56},{80,96},{104,88},{112,120},{... | collective-permute-start | bytes 1228808 | tf_op jit(solution)/shard_map/ppermute | solution.py:478
  40.8 17.0 %collective-permute-done.3.east = f32[18,4,1152]{2,1,0:T(4,128)S(1)} collective-permute-done((f32[18,4,1152]{2,1,0:T(4,128)S(1)}, f32[18,4,1152]{2,1,0:T(4,128)S(1)}, u32[]{:S(2)}, u32[]{:S(2)}) %collective-permute-start.3) | collective-permute-done | bytes 331808 | tf_op jit(solution)/shard_map/ppermute | solution.py:477
  57.8 2.6 %frame.1 = (f32[14,64,288]{2,1,0:T(8,128)S(1)}, f32[4,14,64,640]{3,2,1,0:T(8,128)S(1)}) custom-call(s32[8]{0:T(128)S(1)} %copy-done, f32[48,1664]{1,0:T(8,128)S(1)} %get-tuple-element.64.before.before_edge, f32[48,1664]{1,0:T(8,128)S(1)} %get-tuple-element.63.after.after_edge, f32[8,48,288]{2,1,0:T(8,128)S(1)} %get-tuple-element.31.wind, ...), custom_call_target="tpu_custom_call" | custom-call | flops 17179869184 | bytes 4194304 | tf_op jit(solution)/shard_map/frame/pallas_call | solution.py:276
  60.4 6.2 %collective-permute-done.4.a_0 = f32[4,40,640]{2,1,0:T(8,128)S(1)} collective-permute-done((f32[4,40,640]{2,1,0:T(8,128)S(1)}, f32[4,40,640]{2,1,0:T(8,128)S(1)}, u32[]{:S(2)}, u32[]{:S(2)}) %collective-permute-start.4) | collective-permute-done | bytes 409632 | tf_op jit(solution)/shard_map/ppermute | solution.py:478
  66.6 10.3 %collective-permute-done.5.b_0 = f32[4,40,640]{2,1,0:T(8,128)S(1)} collective-permute-done((f32[4,40,640]{2,1,0:T(8,128)S(1)}, f32[4,40,640]{2,1,0:T(8,128)S(1)}, u32[]{:S(2)}, u32[]{:S(2)}) %collective-permute-start.5) | collective-permute-done | bytes 409632 | tf_op jit(solution)/shard_map/ppermute | solution.py:478
  76.9 13.5 %window_0.1 = (f32[8,48,640]{2,1,0:T(8,128)S(1)}, f32[32,88,128]{2,1,0:T(8,128)S(1)}, f32[32,88,128]{2,1,0:T(8,128)S(1)}) custom-call(s32[8]{0:T(128)S(1)} %copy-done, s32[4]{0:T(128)S(1)} %copy-done.5, f32[8]{0:T(128)S(1)} %add_cosine_fusion.cosine, f32[48,1664]{1,0:T(8,128)S(1)} %get-tuple-element.64.before.before_edge, ...), custom_call_target="tpu_custom_call" | custom-call | flops 8589934592 | bytes 16777216 | tf_op jit(solution)/shard_map/window_0/pallas_call | solution.py:421
  90.5 13.4 %window_1.1 = (f32[8,48,1152]{2,1,0:T(8,128)}, f32[32,88,128]{2,1,0:T(8,128)S(1)}, f32[32,88,128]{2,1,0:T(8,128)S(1)}) custom-call(s32[8]{0:T(128)S(1)} %copy-done, s32[4]{0:T(128)S(1)} %copy-done.5, f32[8]{0:T(128)S(1)} %add_cosine_fusion.cosine, f32[48,1664]{1,0:T(8,128)S(1)} %get-tuple-element.64.before.before_edge, ...), custom_call_target="tpu_custom_call" | custom-call | flops 8589934592 | bytes 16777216 | tf_op jit(solution)/shard_map/window_1/pallas_call | solution.py:421
  104.7 2.0 %collective-permute-start.9 = (f32[8,88,128]{2,1,0:T(8,128)S(1)}, f32[8,88,128]{2,1,0:T(8,128)S(1)}, u32[]{:S(2)}, u32[]{:S(2)}) collective-permute-start(f32[8,88,128]{2,1,0:T(8,128)S(1)} %get-tuple-element.59), channel_id=1, source_target_pairs={{0,2},{1,3},{2,4},{3,5},{4,6},{5,7},{6,0},{7,1},{16,18},{17,19},{1... | collective-permute-start | bytes 1081352 | tf_op jit(solution)/shard_map/ppermute | solution.py:446
  107.5 9.9 %collective-permute-done.10 = f32[8,88,128]{2,1,0:T(8,128)S(1)} collective-permute-done((f32[8,88,128]{2,1,0:T(8,128)S(1)}, f32[8,88,128]{2,1,0:T(8,128)S(1)}, u32[]{:S(2)}, u32[]{:S(2)}) %collective-permute-start.10) | collective-permute-done | bytes 360480 | tf_op jit(solution)/shard_map/ppermute | solution.py:446
  118.3 5.9 %collective-permute-done.9 = f32[8,88,128]{2,1,0:T(8,128)S(1)} collective-permute-done((f32[8,88,128]{2,1,0:T(8,128)S(1)}, f32[8,88,128]{2,1,0:T(8,128)S(1)}, u32[]{:S(2)}, u32[]{:S(2)}) %collective-permute-start.9) | collective-permute-done | bytes 360480 | tf_op jit(solution)/shard_map/ppermute | solution.py:446
  124.5 2.6 %collective-permute-done.16 = f32[8,88,128]{2,1,0:T(8,128)S(1)} collective-permute-done((f32[8,88,128]{2,1,0:T(8,128)S(1)}, f32[8,88,128]{2,1,0:T(8,128)S(1)}, u32[]{:S(2)}, u32[]{:S(2)}) %collective-permute-start.16) | collective-permute-done | bytes 360480 | tf_op jit(solution)/shard_map/ppermute | solution.py:446
  127.8 2.0 %collective-permute-start.19 = (f32[2,88,128]{2,1,0:T(8,128)S(1)}, f32[2,88,128]{2,1,0:T(8,128)S(1)}, u32[]{:S(2)}, u32[]{:S(2)}) collective-permute-start(f32[2,88,128]{2,1,0:T(8,128)S(1)} %get-tuple-element.68), channel_id=1, source_target_pairs={{0,2},{1,3},{2,4},{3,5},{4,6},{5,7},{6,0},{7,1},{16,18},{17,19},{1... | collective-permute-start | bytes 270344 | tf_op jit(solution)/shard_map/ppermute | solution.py:446
  129.8 1.7 %collective-permute-start.20 = (f32[2,88,128]{2,1,0:T(8,128)S(1)}, f32[2,88,128]{2,1,0:T(8,128)S(1)}, u32[]{:S(2)}, u32[]{:S(2)}) collective-permute-start(f32[2,88,128]{2,1,0:T(8,128)S(1)} %get-tuple-element.70), channel_id=1, source_target_pairs={{0,4},{1,5},{2,6},{3,7},{4,0},{5,1},{6,2},{7,3},{16,20},{17,21},{1... | collective-permute-start | bytes 270344 | tf_op jit(solution)/shard_map/ppermute | solution.py:446
  132.1 2.0 %collective-permute-start.21 = (f32[2,88,128]{2,1,0:T(8,128)S(1)}, f32[2,88,128]{2,1,0:T(8,128)S(1)}, u32[]{:S(2)}, u32[]{:S(2)}) collective-permute-start(f32[2,88,128]{2,1,0:T(8,128)S(1)} %get-tuple-element.69), channel_id=1, source_target_pairs={{0,6},{1,7},{2,0},{3,1},{4,2},{5,3},{6,4},{7,5},{16,22},{17,23},{1... | collective-permute-start | bytes 270344 | tf_op jit(solution)/shard_map/ppermute | solution.py:446
  134.1 1.8 %collective-permute-done.20 = f32[2,88,128]{2,1,0:T(8,128)S(1)} collective-permute-done((f32[2,88,128]{2,1,0:T(8,128)S(1)}, f32[2,88,128]{2,1,0:T(8,128)S(1)}, u32[]{:S(2)}, u32[]{:S(2)}) %collective-permute-start.20) | collective-permute-done | bytes 90144 | tf_op jit(solution)/shard_map/ppermute | solution.py:446
  138.3 1.9 %collective-permute-start.23 = (f32[88,128]{1,0:T(8,128)S(1)}, f32[88,128]{1,0:T(8,128)S(1)}, u32[]{:S(2)}, u32[]{:S(2)}) collective-permute-start(f32[88,128]{1,0:T(8,128)S(1)} %get-tuple-element.72), channel_id=1, source_target_pairs={{0,8},{1,9},{2,10},{3,11},{4,12},{5,13},{6,14},{7,15},{16,24},{17,... | collective-permute-start | bytes 135176 | tf_op jit(solution)/shard_map/ppermute | solution.py:507
  141.5 2.3 %collective-permute-done.23 = f32[88,128]{1,0:T(8,128)S(1)} collective-permute-done((f32[88,128]{1,0:T(8,128)S(1)}, f32[88,128]{1,0:T(8,128)S(1)}, u32[]{:S(2)}, u32[]{:S(2)}) %collective-permute-start.23) | collective-permute-done | bytes 45088 | tf_op jit(solution)/shard_map/ppermute | solution.py:507
  (79 shorter events, 14.9 us)
Async XLA Ops:
  5.4 19.1 %collective-permute-start = (f32[48,1664]{1,0:T(8,128)}, f32[48,1664]{1,0:T(8,128)S(1)}, u32[]{:S(2)}, u32[]{:S(2)}) collective-permute-start(f32[48,1664]{1,0:T(8,128)} %get-tuple-element.27), channel_id=1, source_target_pairs={{8,0},{16,32},{40,24},{48,64},{72,56},{80,96},{104,88},{112,120},{... | collective-permute-start | bytes 958472 | tf_op jit(solution)/shard_map/ppermute | solution.py:467
  8.8 20.1 %collective-permute-start.1 = (f32[48,1664]{1,0:T(8,128)}, f32[48,1664]{1,0:T(8,128)S(1)}, u32[]{:S(2)}, u32[]{:S(2)}) collective-permute-start(f32[48,1664]{1,0:T(8,128)} %get-tuple-element.28), channel_id=1, source_target_pairs={{0,16},{24,8},{32,48},{56,40},{64,80},{88,72},{96,112},{120,104},{... | collective-permute-start | bytes 958472 | tf_op jit(solution)/shard_map/ppermute | solution.py:467
  29.0 10.2 %collective-permute-start.2 = (f32[18,4,1152]{2,1,0:T(4,128)S(1)}, f32[18,4,1152]{2,1,0:T(4,128)S(1)}, u32[]{:S(2)}, u32[]{:S(2)}) collective-permute-start(f32[18,4,1152]{2,1,0:T(4,128)S(1)} %get-tuple-element.36), channel_id=1, source_target_pairs={{0,1},{1,2},{2,3},{3,4},{4,5},{5,6},{6,7},{7,8},{8,9},{9,10},{10,1... | collective-permute-start | bytes 995336 | tf_op jit(solution)/shard_map/ppermute | solution.py:476
  29.1 28.7 %collective-permute-start.3 = (f32[18,4,1152]{2,1,0:T(4,128)S(1)}, f32[18,4,1152]{2,1,0:T(4,128)S(1)}, u32[]{:S(2)}, u32[]{:S(2)}) collective-permute-start(f32[18,4,1152]{2,1,0:T(4,128)S(1)} %get-tuple-element.37), channel_id=1, source_target_pairs={{1,0},{2,1},{3,2},{4,3},{5,4},{6,5},{7,6},{8,7},{9,8},{10,9},{11,1... | collective-permute-start | bytes 995336 | tf_op jit(solution)/shard_map/ppermute | solution.py:477
  34.5 32.1 %collective-permute-start.4 = (f32[4,40,640]{2,1,0:T(8,128)S(1)}, f32[4,40,640]{2,1,0:T(8,128)S(1)}, u32[]{:S(2)}, u32[]{:S(2)}) collective-permute-start(f32[4,40,640]{2,1,0:T(8,128)S(1)} %get-tuple-element.41), channel_id=1, source_target_pairs={{0,16},{24,8},{32,48},{56,40},{64,80},{88,72},{96,112},{120,104},{... | collective-permute-start | bytes 1228808 | tf_op jit(solution)/shard_map/ppermute | solution.py:478
  37.0 39.9 %collective-permute-start.5 = (f32[4,40,640]{2,1,0:T(8,128)S(1)}, f32[4,40,640]{2,1,0:T(8,128)S(1)}, u32[]{:S(2)}, u32[]{:S(2)}) collective-permute-start(f32[4,40,640]{2,1,0:T(8,128)S(1)} %get-tuple-element.42), channel_id=1, source_target_pairs={{8,0},{16,32},{40,24},{48,64},{72,56},{80,96},{104,88},{112,120},{... | collective-permute-start | bytes 1228808 | tf_op jit(solution)/shard_map/ppermute | solution.py:478
  38.9 51.5 %collective-permute-start.6 = (f32[4,40,512]{2,1,0:T(8,128)S(1)}, f32[4,40,512]{2,1,0:T(8,128)S(1)}, u32[]{:S(2)}, u32[]{:S(2)}) collective-permute-start(f32[4,40,512]{2,1,0:T(8,128)S(1)} %get-tuple-element.43), channel_id=1, source_target_pairs={{0,16},{24,8},{32,48},{56,40},{64,80},{88,72},{96,112},{120,104},{... | collective-permute-start | bytes 983048 | tf_op jit(solution)/shard_map/ppermute | solution.py:479
  39.3 51.2 %collective-permute-start.7 = (f32[4,40,512]{2,1,0:T(8,128)S(1)}, f32[4,40,512]{2,1,0:T(8,128)S(1)}, u32[]{:S(2)}, u32[]{:S(2)}) collective-permute-start(f32[4,40,512]{2,1,0:T(8,128)S(1)} %get-tuple-element.44), channel_id=1, source_target_pairs={{8,0},{16,32},{40,24},{48,64},{72,56},{80,96},{104,88},{112,120},{... | collective-permute-start | bytes 983048 | tf_op jit(solution)/shard_map/ppermute | solution.py:479
  90.4 13.9 %collective-permute-start.8 = (f32[32,88,128]{2,1,0:T(8,128)S(1)}, f32[32,88,128]{2,1,0:T(8,128)S(1)}, u32[]{:S(2)}, u32[]{:S(2)}) collective-permute-start(f32[32,88,128]{2,1,0:T(8,128)S(1)} %get-tuple-element.49), channel_id=1, source_target_pairs={{0,1},{1,0},{2,3},{3,2},{4,5},{5,4},{6,7},{7,6},{16,17},{17,16},{1... | collective-permute-start | bytes 4325384 | tf_op jit(solution)/shard_map/ppermute | solution.py:494
  104.5 12.9 %collective-permute-start.10 = (f32[8,88,128]{2,1,0:T(8,128)S(1)}, f32[8,88,128]{2,1,0:T(8,128)S(1)}, u32[]{:S(2)}, u32[]{:S(2)}) collective-permute-start(f32[8,88,128]{2,1,0:T(8,128)S(1)} %get-tuple-element.58), channel_id=1, source_target_pairs={{0,4},{1,5},{2,6},{3,7},{4,0},{5,1},{6,2},{7,3},{16,20},{17,21},{1... | collective-permute-start | bytes 1081352 | tf_op jit(solution)/shard_map/ppermute | solution.py:446
  104.6 13.7 %collective-permute-start.11 = (f32[8,88,128]{2,1,0:T(8,128)S(1)}, f32[8,88,128]{2,1,0:T(8,128)S(1)}, u32[]{:S(2)}, u32[]{:S(2)}) collective-permute-start(f32[8,88,128]{2,1,0:T(8,128)S(1)} %get-tuple-element.57), channel_id=1, source_target_pairs={{0,6},{1,7},{2,0},{3,1},{4,2},{5,3},{6,4},{7,5},{16,22},{17,23},{1... | collective-permute-start | bytes 1081352 | tf_op jit(solution)/shard_map/ppermute | solution.py:446
  104.7 19.5 %collective-permute-start.9 = (f32[8,88,128]{2,1,0:T(8,128)S(1)}, f32[8,88,128]{2,1,0:T(8,128)S(1)}, u32[]{:S(2)}, u32[]{:S(2)}) collective-permute-start(f32[8,88,128]{2,1,0:T(8,128)S(1)} %get-tuple-element.59), channel_id=1, source_target_pairs={{0,2},{1,3},{2,4},{3,5},{4,6},{5,7},{6,0},{7,1},{16,18},{17,19},{1... | collective-permute-start | bytes 1081352 | tf_op jit(solution)/shard_map/ppermute | solution.py:446
  107.4 19.7 %collective-permute-start.16 = (f32[8,88,128]{2,1,0:T(8,128)S(1)}, f32[8,88,128]{2,1,0:T(8,128)S(1)}, u32[]{:S(2)}, u32[]{:S(2)}) collective-permute-start(f32[8,88,128]{2,1,0:T(8,128)S(1)} %get-tuple-element.62), channel_id=1, source_target_pairs={{0,32},{1,33},{2,34},{3,35},{4,36},{5,37},{6,38},{7,39},{16,48},{1... | collective-permute-start | bytes 1081352 | tf_op jit(solution)/shard_map/ppermute | solution.py:446
  107.5 20.2 %collective-permute-start.17 = (f32[8,88,128]{2,1,0:T(8,128)S(1)}, f32[8,88,128]{2,1,0:T(8,128)S(1)}, u32[]{:S(2)}, u32[]{:S(2)}) collective-permute-start(f32[8,88,128]{2,1,0:T(8,128)S(1)} %get-tuple-element.61), channel_id=1, source_target_pairs={{0,64},{1,65},{2,66},{3,67},{4,68},{5,69},{6,70},{7,71},{16,80},{1... | collective-permute-start | bytes 1081352 | tf_op jit(solution)/shard_map/ppermute | solution.py:446
  117.4 10.2 %collective-permute-start.18 = (f32[8,88,128]{2,1,0:T(8,128)S(1)}, f32[8,88,128]{2,1,0:T(8,128)S(1)}, u32[]{:S(2)}, u32[]{:S(2)}) collective-permute-start(f32[8,88,128]{2,1,0:T(8,128)S(1)} %get-tuple-element.60), channel_id=1, source_target_pairs={{0,96},{1,97},{2,98},{3,99},{4,100},{5,101},{6,102},{7,103},{16,11... | collective-permute-start | bytes 1081352 | tf_op jit(solution)/shard_map/ppermute | solution.py:446
  124.3 7.8 %collective-permute-start.12 = (f32[2,88,128]{2,1,0:T(8,128)S(1)}, f32[2,88,128]{2,1,0:T(8,128)S(1)}, u32[]{:S(2)}, u32[]{:S(2)}) collective-permute-start(f32[2,88,128]{2,1,0:T(8,128)S(1)} %get-tuple-element.65), channel_id=1, source_target_pairs={{0,32},{1,33},{2,34},{3,35},{4,36},{5,37},{6,38},{7,39},{16,48},{1... | collective-permute-start | bytes 270344 | tf_op jit(solution)/shard_map/ppermute | solution.py:446
  124.4 9.6 %collective-permute-start.13 = (f32[2,88,128]{2,1,0:T(8,128)S(1)}, f32[2,88,128]{2,1,0:T(8,128)S(1)}, u32[]{:S(2)}, u32[]{:S(2)}) collective-permute-start(f32[2,88,128]{2,1,0:T(8,128)S(1)} %get-tuple-element.67), channel_id=1, source_target_pairs={{0,64},{1,65},{2,66},{3,67},{4,68},{5,69},{6,70},{7,71},{16,80},{1... | collective-permute-start | bytes 270344 | tf_op jit(solution)/shard_map/ppermute | solution.py:446
  127.1 7.0 %collective-permute-start.14 = (f32[2,88,128]{2,1,0:T(8,128)S(1)}, f32[2,88,128]{2,1,0:T(8,128)S(1)}, u32[]{:S(2)}, u32[]{:S(2)}) collective-permute-start(f32[2,88,128]{2,1,0:T(8,128)S(1)} %get-tuple-element.66), channel_id=1, source_target_pairs={{0,96},{1,97},{2,98},{3,99},{4,100},{5,101},{6,102},{7,103},{16,11... | collective-permute-start | bytes 270344 | tf_op jit(solution)/shard_map/ppermute | solution.py:446
  127.8 6.3 %collective-permute-start.19 = (f32[2,88,128]{2,1,0:T(8,128)S(1)}, f32[2,88,128]{2,1,0:T(8,128)S(1)}, u32[]{:S(2)}, u32[]{:S(2)}) collective-permute-start(f32[2,88,128]{2,1,0:T(8,128)S(1)} %get-tuple-element.68), channel_id=1, source_target_pairs={{0,2},{1,3},{2,4},{3,5},{4,6},{5,7},{6,0},{7,1},{16,18},{17,19},{1... | collective-permute-start | bytes 270344 | tf_op jit(solution)/shard_map/ppermute | solution.py:446
  129.8 6.0 %collective-permute-start.20 = (f32[2,88,128]{2,1,0:T(8,128)S(1)}, f32[2,88,128]{2,1,0:T(8,128)S(1)}, u32[]{:S(2)}, u32[]{:S(2)}) collective-permute-start(f32[2,88,128]{2,1,0:T(8,128)S(1)} %get-tuple-element.70), channel_id=1, source_target_pairs={{0,4},{1,5},{2,6},{3,7},{4,0},{5,1},{6,2},{7,3},{16,20},{17,21},{1... | collective-permute-start | bytes 270344 | tf_op jit(solution)/shard_map/ppermute | solution.py:446
  132.1 4.5 %collective-permute-start.21 = (f32[2,88,128]{2,1,0:T(8,128)S(1)}, f32[2,88,128]{2,1,0:T(8,128)S(1)}, u32[]{:S(2)}, u32[]{:S(2)}) collective-permute-start(f32[2,88,128]{2,1,0:T(8,128)S(1)} %get-tuple-element.69), channel_id=1, source_target_pairs={{0,6},{1,7},{2,0},{3,1},{4,2},{5,3},{6,4},{7,5},{16,22},{17,23},{1... | collective-permute-start | bytes 270344 | tf_op jit(solution)/shard_map/ppermute | solution.py:446
  136.7 4.8 %collective-permute-start.22 = (f32[88,128]{1,0:T(8,128)S(1)}, f32[88,128]{1,0:T(8,128)S(1)}, u32[]{:S(2)}, u32[]{:S(2)}) collective-permute-start(f32[88,128]{1,0:T(8,128)S(1)} %slice_bitcast_fusion.2), channel_id=1, source_target_pairs={{0,16},{1,17},{2,18},{3,19},{4,20},{5,21},{6,22},{7,23},{16,0},{17... | collective-permute-start | bytes 135176 | tf_op jit(solution)/shard_map/ppermute | solution.py:506
  138.3 5.6 %collective-permute-start.23 = (f32[88,128]{1,0:T(8,128)S(1)}, f32[88,128]{1,0:T(8,128)S(1)}, u32[]{:S(2)}, u32[]{:S(2)}) collective-permute-start(f32[88,128]{1,0:T(8,128)S(1)} %get-tuple-element.72), channel_id=1, source_target_pairs={{0,8},{1,9},{2,10},{3,11},{4,12},{5,13},{6,14},{7,15},{16,24},{17,... | collective-permute-start | bytes 135176 | tf_op jit(solution)/shard_map/ppermute | solution.py:507
  140.2 5.3 %collective-permute-start.24 = (f32[88,128]{1,0:T(8,128)S(1)}, f32[88,128]{1,0:T(8,128)S(1)}, u32[]{:S(2)}, u32[]{:S(2)}) collective-permute-start(f32[88,128]{1,0:T(8,128)S(1)} %get-tuple-element.71), channel_id=1, source_target_pairs={{0,24},{1,25},{2,26},{3,27},{4,28},{5,29},{6,30},{7,31},{16,8},{17... | collective-permute-start | bytes 135176 | tf_op jit(solution)/shard_map/ppermute | solution.py:507
  (9 other events, 122.7 us)

commit v7 on v6

--- a/solution.py
+++ b/solution.py
@@ -62,7 +62,8 @@
 
 
 FORWARD = meridian()
-CIRCLE = FORWARD + [(t, s) for s, t in FORWARD]
+BACKWARD = [(t, s) for s, t in FORWARD]
+CIRCLE = FORWARD + BACKWARD
 SWAP_A = [(s, t) for s, t in CIRCLE if s // 16 // 2 == t // 16 // 2 and s // 16 != t // 16]
 SWAP_B = [pair for pair in CIRCLE if pair not in SWAP_A]
 EASTWARD = [(b, (b + 1) % 16) for b in range(16)]
@@ -92,7 +93,7 @@
 
 
 def lead_kernel(
-    info, vec_ids, pool, winds, edge_a, edge_b, chosen, ends, held_winds, made, sems
+    info, vec_ids, pool, winds, edge_next, edge_last, chosen, ends, held_winds, made, sems
 ):
     fetch = [
         pltpu.make_async_copy(pool.at[:, :16, :], ends.at[0], sems.at[0]),
@@ -109,8 +110,8 @@
         picked = jnp.dot(rows, chosen[...], preferred_element_type=jnp.float32)
         made[i] = picked.reshape(ROWS, 16, CH)
     for r in range(4):
-        for edge, flag in ((edge_a, info[7]), (edge_b, 1 - info[7])):
-            row = jnp.where(flag == 0, 4 + r, r)
+        for edge, end in ((edge_next, 1), (edge_last, 0)):
+            row = end * 4 + r
             own = jnp.where(info[0] == 0, row, ROWS - 1 - row)
             for m in range(CH // 128):
                 lanes = slice(m * 128, (m + 1) * 128)
@@ -120,8 +121,8 @@
                 )
     for r in range(3):
         lanes = slice(r * WCH, (r + 1) * WCH)
-        for edge, flag in ((edge_a, info[7]), (edge_b, 1 - info[7])):
-            row = jnp.where(flag == 0, ROWS - 3 + r, r)
+        for edge, end in ((edge_next, 1), (edge_last, 0)):
+            row = end * (ROWS - 3) + r
             edge[:, lanes] = turned_wind(held_winds, info, row)
 
 
@@ -463,10 +464,9 @@
             (lat_index + flip) % 2,
         ]
     )
-    edge_a, edge_b = lead(info, vec_ids, pool, winds)
-    edge_a, edge_b = lax.ppermute(edge_a, ALL, SWAP_A), lax.ppermute(edge_b, ALL, SWAP_B)
-    before_edge = jnp.where(info[7] == 0, edge_b, edge_a)
-    after_edge = jnp.where(info[7] == 0, edge_a, edge_b)
+    edge_next, edge_last = lead(info, vec_ids, pool, winds)
+    before_edge = lax.ppermute(edge_next, ALL, FORWARD)
+    after_edge = lax.ppermute(edge_last, ALL, BACKWARD)
     low, high, wind, a_0, a_1, b_0, b_1, basis_main, basis_rest = pack(
         info, vec_ids, pool, winds, basis
     )

time: 147 us -> 148 us (level)
  starting transfers between devices: 28.8 us -> 50.1 us
  waiting for transfers between devices: 75.7 us -> 55.7 us
    ppermute x1, starting transfers between devices: 1.52 us -> 22.7 us  [shards(): lax.ppermute(bulk[3], ALL, SWAP_B)]
    ppermute x1, waiting for transfers between devices: 17 us -> 0.01 us  [shards(): east = lax.ppermute(to_west, 'lon', WESTWARD)]
    ppermute x1, waiting for transfers between devices: 6.2 us -> 0.81 us  [shards(): lax.ppermute(bulk[0], ALL, SWAP_A)]
    ppermute x1, waiting for transfers between devices: 10.3 us -> 13.1 us  [shards(): lax.ppermute(bulk[1], ALL, SWAP_B)]
    ppermute x1, starting transfers between devices: 2.46 us -> 0.09 us  [shards(): lax.ppermute(bulk[0], ALL, SWAP_A)]
    ppermute x1, starting transfers between devices: 1.95 us -> 3.64 us  [shards(): lax.ppermute(bulk[1], ALL, SWAP_B)]
    ppermute x1, starting transfers between devices: 1.94 us -> 3.54 us  [shards(): lax.ppermute(far[0], ALL, turned(2)) + lax.ppermute(far[1], ALL, turned(3))]
    ppermute x1, starting transfers between devices: 1.58 us -> 0.09 us  [shards(): block = near[0] + lax.ppermute(near[1], ALL, turned(1))]
  transfers between devices with their start and end apart: 25 -> 25, of which waited for: 16 -> 15; matrix products, arithmetic and copies ran while one was open for 2% -> 2% of each run, Pallas kernels for 22% -> 22%
where the time goes in v7:
time: 148 us
  waiting for transfers between devices  55.7 us (38%)
  starting transfers between devices  50.1 us (34%)
  Pallas kernels  36.8 us (25%)
  local copies, waits for them, and re-layouts  2.63 us (2%)
    pallas_call x2, Pallas kernels, window(): pl.pallas_call(functools.partial(window_kernel, part), out_shape=[jax.Sha...  26.8 us
    ppermute x1, starting transfers between devices, shards(): lax.ppermute(bulk[3], ALL, SWAP_B)  22.7 us
    ppermute x12, waiting for transfers between devices, line_sum(): sent = [lax.ppermute(parts[k], ALL, moved(**{name: k})) for k in (1, 2, 3)]  22.4 us
    ppermute x1, waiting for transfers between devices, shards(): lax.ppermute(bulk[1], ALL, SWAP_B)  13.1 us
    ppermute x1, waiting for transfers between devices, shards(): before_edge = lax.ppermute(edge_next, ALL, FORWARD)  10.4 us
    ppermute x12, starting transfers between devices, line_sum(): sent = [lax.ppermute(parts[k], ALL, moved(**{name: k})) for k in (1, 2, 3)]  8.75 us
    ppermute x1, starting transfers between devices, shards(): east = lax.ppermute(to_west, 'lon', WESTWARD)  5.98 us
    pallas_call x1, Pallas kernels, lead(): pl.pallas_call(lead_kernel, out_shape=[jax.ShapeDtypeStruct((COLS, WPACK...  4.02 us
  transfers between devices with their start and end apart: 25, of which 15 were waited for; matrix products, arithmetic and copies ran while one was open for 2% of the time, Pallas kernels for 22%

profile of v7, /device:TPU:0, one launch (start us, length us, event | category | flops | bytes accessed | tf_op | source)
XLA Modules:
  0.0 147.6 jit_solution(5053575033234308490)
XLA Ops:
  1.4 4.0 %lead.1 = (f32[48,1664]{1,0:T(8,128)}, f32[48,1664]{1,0:T(8,128)}) custom-call(s32[8]{0:T(128)} %stack.49.info, s32[8]{0:T(128)} %vec_ids.3, bf16[8,48,1152]{2,1,0:T(8,128)(2,1)} %pool.3, f32[8,48,288]{2,1,0:T(8,128)} %winds.3), custom_call_target="tpu_custom_call" | custom-call | flops 1073741824 | bytes 4194304 | tf_op jit(solution)/shard_map/lead/pallas_call | solution.py:131
  5.4 1.7 %collective-permute-start = (f32[48,1664]{1,0:T(8,128)}, f32[48,1664]{1,0:T(8,128)S(1)}, u32[]{:S(2)}, u32[]{:S(2)}) collective-permute-start(f32[48,1664]{1,0:T(8,128)} %get-tuple-element.27), channel_id=1, source_target_pairs={{0,16},{8,0},{16,32},{24,8},{32,48},{40,24},{48,64},{56,40},{64,80... | collective-permute-start | bytes 958472 | tf_op jit(solution)/shard_map/ppermute | solution.py:468
  7.1 1.9 %collective-permute-start.1 = (f32[48,1664]{1,0:T(8,128)}, f32[48,1664]{1,0:T(8,128)S(1)}, u32[]{:S(2)}, u32[]{:S(2)}) collective-permute-start(f32[48,1664]{1,0:T(8,128)} %get-tuple-element.30), channel_id=1, source_target_pairs={{16,0},{0,8},{32,16},{8,24},{48,32},{24,40},{64,48},{40,56},{80,64... | collective-permute-start | bytes 958472 | tf_op jit(solution)/shard_map/ppermute | solution.py:469
  10.7 3.3 %pack.1 = (f32[4,48,1152]{2,1,0:T(8,128)S(1)}, f32[4,48,1152]{2,1,0:T(8,128)S(1)}, f32[8,48,288]{2,1,0:T(8,128)S(1)}, f32[4,40,640]{2,1,0:T(8,128)S(1)}, f32[4,4...) custom-call(s32[8]{0:T(128)S(1)} %copy-done, ...), custom_call_target="tpu_custom_call" | custom-call | flops 1073741824 | bytes 4194304 | tf_op jit(solution)/shard_map/pack/pallas_call | solution.py:188
  14.0 10.4 %collective-permute-done.before.before_edge = f32[48,1664]{1,0:T(8,128)S(1)} collective-permute-done((f32[48,1664]{1,0:T(8,128)}, f32[48,1664]{1,0:T(8,128)S(1)}, u32[]{:S(2)}, u32[]{:S(2)}) %collective-permute-start) | collective-permute-done | bytes 319520 | tf_op jit(solution)/shard_map/ppermute | solution.py:468
  24.4 3.5 %collective-permute-done.1.after.after_edge = f32[48,1664]{1,0:T(8,128)S(1)} collective-permute-done((f32[48,1664]{1,0:T(8,128)}, f32[48,1664]{1,0:T(8,128)S(1)}, u32[]{:S(2)}, u32[]{:S(2)}) %collective-permute-start.1) | collective-permute-done | bytes 319520 | tf_op jit(solution)/shard_map/ppermute | solution.py:469
  28.1 6.0 %collective-permute-start.3 = (f32[18,4,1152]{2,1,0:T(4,128)S(1)}, f32[18,4,1152]{2,1,0:T(4,128)S(1)}, u32[]{:S(2)}, u32[]{:S(2)}) collective-permute-start(f32[18,4,1152]{2,1,0:T(4,128)S(1)} %get-tuple-element.37), channel_id=1, source_target_pairs={{1,0},{2,1},{3,2},{4,3},{5,4},{6,5},{7,6},{8,7},{9,8},{10,9},{11,1... | collective-permute-start | bytes 995336 | tf_op jit(solution)/shard_map/ppermute | solution.py:477
  34.2 3.6 %collective-permute-start.5 = (f32[4,40,640]{2,1,0:T(8,128)S(1)}, f32[4,40,640]{2,1,0:T(8,128)S(1)}, u32[]{:S(2)}, u32[]{:S(2)}) collective-permute-start(f32[4,40,640]{2,1,0:T(8,128)S(1)} %get-tuple-element.42), channel_id=1, source_target_pairs={{8,0},{16,32},{40,24},{48,64},{72,56},{80,96},{104,88},{112,120},{... | collective-permute-start | bytes 1228808 | tf_op jit(solution)/shard_map/ppermute | solution.py:478
  38.8 22.7 %collective-permute-start.7 = (f32[4,40,512]{2,1,0:T(8,128)S(1)}, f32[4,40,512]{2,1,0:T(8,128)S(1)}, u32[]{:S(2)}, u32[]{:S(2)}) collective-permute-start(f32[4,40,512]{2,1,0:T(8,128)S(1)} %get-tuple-element.44), channel_id=1, source_target_pairs={{8,0},{16,32},{40,24},{48,64},{72,56},{80,96},{104,88},{112,120},{... | collective-permute-start | bytes 983048 | tf_op jit(solution)/shard_map/ppermute | solution.py:479
  61.5 2.6 %frame.1 = (f32[14,64,288]{2,1,0:T(8,128)S(1)}, f32[4,14,64,640]{3,2,1,0:T(8,128)S(1)}) custom-call(s32[8]{0:T(128)S(1)} %copy-done, f32[48,1664]{1,0:T(8,128)S(1)} %collective-permute-done.before.before_edge, f32[48,1664]{1,0:T(8,128)S(1)} %collective-permute-done.1.after.after_edge, f32[8,48,288]{2,1,0:T(8,128)S(1)} %get-tuple-element.31.wind, ...), custom_call_target="tpu_custom_call" | custom-call | flops 17179869184 | bytes 4194304 | tf_op jit(solution)/shard_map/frame/pallas_call | solution.py:277
  64.9 13.1 %collective-permute-done.5.b_0 = f32[4,40,640]{2,1,0:T(8,128)S(1)} collective-permute-done((f32[4,40,640]{2,1,0:T(8,128)S(1)}, f32[4,40,640]{2,1,0:T(8,128)S(1)}, u32[]{:S(2)}, u32[]{:S(2)}) %collective-permute-start.5) | collective-permute-done | bytes 409632 | tf_op jit(solution)/shard_map/ppermute | solution.py:478
  78.0 13.5 %window_0.1 = (f32[8,48,640]{2,1,0:T(8,128)S(1)}, f32[32,88,128]{2,1,0:T(8,128)S(1)}, f32[32,88,128]{2,1,0:T(8,128)S(1)}) custom-call(s32[8]{0:T(128)S(1)} %copy-done, s32[4]{0:T(128)S(1)} %copy-done.5, f32[8]{0:T(128)S(1)} %add_cosine_fusion.cosine, f32[48,1664]{1,0:T(8,128)S(1)} %collective-permute-done.before.before_edge, ...), custom_call_target="tpu_custom_call" | custom-call | flops 8589934592 | bytes 16777216 | tf_op jit(solution)/shard_map/window_0/pallas_call | solution.py:422
  91.6 13.3 %window_1.1 = (f32[8,48,1152]{2,1,0:T(8,128)}, f32[32,88,128]{2,1,0:T(8,128)S(1)}, f32[32,88,128]{2,1,0:T(8,128)S(1)}) custom-call(s32[8]{0:T(128)S(1)} %copy-done, s32[4]{0:T(128)S(1)} %copy-done.5, f32[8]{0:T(128)S(1)} %add_cosine_fusion.cosine, f32[48,1664]{1,0:T(8,128)S(1)} %collective-permute-done.before.before_edge, ...), custom_call_target="tpu_custom_call" | custom-call | flops 8589934592 | bytes 16777216 | tf_op jit(solution)/shard_map/window_1/pallas_call | solution.py:422
  105.8 2.0 %collective-permute-start.9 = (f32[8,88,128]{2,1,0:T(8,128)S(1)}, f32[8,88,128]{2,1,0:T(8,128)S(1)}, u32[]{:S(2)}, u32[]{:S(2)}) collective-permute-start(f32[8,88,128]{2,1,0:T(8,128)S(1)} %get-tuple-element.59), channel_id=1, source_target_pairs={{0,2},{1,3},{2,4},{3,5},{4,6},{5,7},{6,0},{7,1},{16,18},{17,19},{1... | collective-permute-start | bytes 1081352 | tf_op jit(solution)/shard_map/ppermute | solution.py:447
  108.7 9.9 %collective-permute-done.10 = f32[8,88,128]{2,1,0:T(8,128)S(1)} collective-permute-done((f32[8,88,128]{2,1,0:T(8,128)S(1)}, f32[8,88,128]{2,1,0:T(8,128)S(1)}, u32[]{:S(2)}, u32[]{:S(2)}) %collective-permute-start.10) | collective-permute-done | bytes 360480 | tf_op jit(solution)/shard_map/ppermute | solution.py:447
  118.5 1.8 %collective-permute-done.11 = f32[8,88,128]{2,1,0:T(8,128)S(1)} collective-permute-done((f32[8,88,128]{2,1,0:T(8,128)S(1)}, f32[8,88,128]{2,1,0:T(8,128)S(1)}, u32[]{:S(2)}, u32[]{:S(2)}) %collective-permute-start.11) | collective-permute-done | bytes 360480 | tf_op jit(solution)/shard_map/ppermute | solution.py:447
  120.4 4.9 %collective-permute-done.9 = f32[8,88,128]{2,1,0:T(8,128)S(1)} collective-permute-done((f32[8,88,128]{2,1,0:T(8,128)S(1)}, f32[8,88,128]{2,1,0:T(8,128)S(1)}, u32[]{:S(2)}, u32[]{:S(2)}) %collective-permute-start.9) | collective-permute-done | bytes 360480 | tf_op jit(solution)/shard_map/ppermute | solution.py:447
  125.6 2.6 %collective-permute-done.16 = f32[8,88,128]{2,1,0:T(8,128)S(1)} collective-permute-done((f32[8,88,128]{2,1,0:T(8,128)S(1)}, f32[8,88,128]{2,1,0:T(8,128)S(1)}, u32[]{:S(2)}, u32[]{:S(2)}) %collective-permute-start.16) | collective-permute-done | bytes 360480 | tf_op jit(solution)/shard_map/ppermute | solution.py:447
  128.9 2.0 %collective-permute-start.19 = (f32[2,88,128]{2,1,0:T(8,128)S(1)}, f32[2,88,128]{2,1,0:T(8,128)S(1)}, u32[]{:S(2)}, u32[]{:S(2)}) collective-permute-start(f32[2,88,128]{2,1,0:T(8,128)S(1)} %get-tuple-element.66), channel_id=1, source_target_pairs={{0,2},{1,3},{2,4},{3,5},{4,6},{5,7},{6,0},{7,1},{16,18},{17,19},{1... | collective-permute-start | bytes 270344 | tf_op jit(solution)/shard_map/ppermute | solution.py:447
  130.9 1.7 %collective-permute-start.20 = (f32[2,88,128]{2,1,0:T(8,128)S(1)}, f32[2,88,128]{2,1,0:T(8,128)S(1)}, u32[]{:S(2)}, u32[]{:S(2)}) collective-permute-start(f32[2,88,128]{2,1,0:T(8,128)S(1)} %get-tuple-element.68), channel_id=1, source_target_pairs={{0,4},{1,5},{2,6},{3,7},{4,0},{5,1},{6,2},{7,3},{16,20},{17,21},{1... | collective-permute-start | bytes 270344 | tf_op jit(solution)/shard_map/ppermute | solution.py:447
  133.2 2.0 %collective-permute-start.21 = (f32[2,88,128]{2,1,0:T(8,128)S(1)}, f32[2,88,128]{2,1,0:T(8,128)S(1)}, u32[]{:S(2)}, u32[]{:S(2)}) collective-permute-start(f32[2,88,128]{2,1,0:T(8,128)S(1)} %get-tuple-element.67), channel_id=1, source_target_pairs={{0,6},{1,7},{2,0},{3,1},{4,2},{5,3},{6,4},{7,5},{16,22},{17,23},{1... | collective-permute-start | bytes 270344 | tf_op jit(solution)/shard_map/ppermute | solution.py:447
  135.2 1.8 %collective-permute-done.20 = f32[2,88,128]{2,1,0:T(8,128)S(1)} collective-permute-done((f32[2,88,128]{2,1,0:T(8,128)S(1)}, f32[2,88,128]{2,1,0:T(8,128)S(1)}, u32[]{:S(2)}, u32[]{:S(2)}) %collective-permute-start.20) | collective-permute-done | bytes 90144 | tf_op jit(solution)/shard_map/ppermute | solution.py:447
  137.9 3.5 %collective-permute-start.23 = (f32[88,128]{1,0:T(8,128)S(1)}, f32[88,128]{1,0:T(8,128)S(1)}, u32[]{:S(2)}, u32[]{:S(2)}) collective-permute-start(f32[88,128]{1,0:T(8,128)S(1)} %get-tuple-element.70), channel_id=1, source_target_pairs={{0,8},{1,9},{2,10},{3,11},{4,12},{5,13},{6,14},{7,15},{16,24},{17,... | collective-permute-start | bytes 135176 | tf_op jit(solution)/shard_map/ppermute | solution.py:507
  143.9 2.8 %collective-permute-done.24 = f32[88,128]{1,0:T(8,128)S(1)} collective-permute-done((f32[88,128]{1,0:T(8,128)S(1)}, f32[88,128]{1,0:T(8,128)S(1)}, u32[]{:S(2)}, u32[]{:S(2)}) %collective-permute-start.24) | collective-permute-done | bytes 45088 | tf_op jit(solution)/shard_map/ppermute | solution.py:507
  (78 shorter events, 12.0 us)
Async XLA Ops:
  5.4 19.0 %collective-permute-start = (f32[48,1664]{1,0:T(8,128)}, f32[48,1664]{1,0:T(8,128)S(1)}, u32[]{:S(2)}, u32[]{:S(2)}) collective-permute-start(f32[48,1664]{1,0:T(8,128)} %get-tuple-element.27), channel_id=1, source_target_pairs={{0,16},{8,0},{16,32},{24,8},{32,48},{40,24},{48,64},{56,40},{64,80... | collective-permute-start | bytes 958472 | tf_op jit(solution)/shard_map/ppermute | solution.py:468
  7.1 20.8 %collective-permute-start.1 = (f32[48,1664]{1,0:T(8,128)}, f32[48,1664]{1,0:T(8,128)S(1)}, u32[]{:S(2)}, u32[]{:S(2)}) collective-permute-start(f32[48,1664]{1,0:T(8,128)} %get-tuple-element.30), channel_id=1, source_target_pairs={{16,0},{0,8},{32,16},{8,24},{48,32},{24,40},{64,48},{40,56},{80,64... | collective-permute-start | bytes 958472 | tf_op jit(solution)/shard_map/ppermute | solution.py:469
  28.0 10.8 %collective-permute-start.2 = (f32[18,4,1152]{2,1,0:T(4,128)S(1)}, f32[18,4,1152]{2,1,0:T(4,128)S(1)}, u32[]{:S(2)}, u32[]{:S(2)}) collective-permute-start(f32[18,4,1152]{2,1,0:T(4,128)S(1)} %get-tuple-element.36), channel_id=1, source_target_pairs={{0,1},{1,2},{2,3},{3,4},{4,5},{5,6},{6,7},{7,8},{8,9},{9,10},{10,1... | collective-permute-start | bytes 995336 | tf_op jit(solution)/shard_map/ppermute | solution.py:476
  28.1 33.4 %collective-permute-start.3 = (f32[18,4,1152]{2,1,0:T(4,128)S(1)}, f32[18,4,1152]{2,1,0:T(4,128)S(1)}, u32[]{:S(2)}, u32[]{:S(2)}) collective-permute-start(f32[18,4,1152]{2,1,0:T(4,128)S(1)} %get-tuple-element.37), channel_id=1, source_target_pairs={{1,0},{2,1},{3,2},{4,3},{5,4},{6,5},{7,6},{8,7},{9,8},{10,9},{11,1... | collective-permute-start | bytes 995336 | tf_op jit(solution)/shard_map/ppermute | solution.py:477
  34.1 30.7 %collective-permute-start.4 = (f32[4,40,640]{2,1,0:T(8,128)S(1)}, f32[4,40,640]{2,1,0:T(8,128)S(1)}, u32[]{:S(2)}, u32[]{:S(2)}) collective-permute-start(f32[4,40,640]{2,1,0:T(8,128)S(1)} %get-tuple-element.41), channel_id=1, source_target_pairs={{0,16},{24,8},{32,48},{56,40},{64,80},{88,72},{96,112},{120,104},{... | collective-permute-start | bytes 1228808 | tf_op jit(solution)/shard_map/ppermute | solution.py:478
  34.2 43.8 %collective-permute-start.5 = (f32[4,40,640]{2,1,0:T(8,128)S(1)}, f32[4,40,640]{2,1,0:T(8,128)S(1)}, u32[]{:S(2)}, u32[]{:S(2)}) collective-permute-start(f32[4,40,640]{2,1,0:T(8,128)S(1)} %get-tuple-element.42), channel_id=1, source_target_pairs={{8,0},{16,32},{40,24},{48,64},{72,56},{80,96},{104,88},{112,120},{... | collective-permute-start | bytes 1228808 | tf_op jit(solution)/shard_map/ppermute | solution.py:478
  37.9 53.7 %collective-permute-start.6 = (f32[4,40,512]{2,1,0:T(8,128)S(1)}, f32[4,40,512]{2,1,0:T(8,128)S(1)}, u32[]{:S(2)}, u32[]{:S(2)}) collective-permute-start(f32[4,40,512]{2,1,0:T(8,128)S(1)} %get-tuple-element.43), channel_id=1, source_target_pairs={{0,16},{24,8},{32,48},{56,40},{64,80},{88,72},{96,112},{120,104},{... | collective-permute-start | bytes 983048 | tf_op jit(solution)/shard_map/ppermute | solution.py:479
  38.8 52.8 %collective-permute-start.7 = (f32[4,40,512]{2,1,0:T(8,128)S(1)}, f32[4,40,512]{2,1,0:T(8,128)S(1)}, u32[]{:S(2)}, u32[]{:S(2)}) collective-permute-start(f32[4,40,512]{2,1,0:T(8,128)S(1)} %get-tuple-element.44), channel_id=1, source_target_pairs={{8,0},{16,32},{40,24},{48,64},{72,56},{80,96},{104,88},{112,120},{... | collective-permute-start | bytes 983048 | tf_op jit(solution)/shard_map/ppermute | solution.py:479
  91.5 13.9 %collective-permute-start.8 = (f32[32,88,128]{2,1,0:T(8,128)S(1)}, f32[32,88,128]{2,1,0:T(8,128)S(1)}, u32[]{:S(2)}, u32[]{:S(2)}) collective-permute-start(f32[32,88,128]{2,1,0:T(8,128)S(1)} %get-tuple-element.49), channel_id=1, source_target_pairs={{0,1},{1,0},{2,3},{3,2},{4,5},{5,4},{6,7},{7,6},{16,17},{17,16},{1... | collective-permute-start | bytes 4325384 | tf_op jit(solution)/shard_map/ppermute | solution.py:494
  105.6 12.9 %collective-permute-start.10 = (f32[8,88,128]{2,1,0:T(8,128)S(1)}, f32[8,88,128]{2,1,0:T(8,128)S(1)}, u32[]{:S(2)}, u32[]{:S(2)}) collective-permute-start(f32[8,88,128]{2,1,0:T(8,128)S(1)} %get-tuple-element.58), channel_id=1, source_target_pairs={{0,4},{1,5},{2,6},{3,7},{4,0},{5,1},{6,2},{7,3},{16,20},{17,21},{1... | collective-permute-start | bytes 1081352 | tf_op jit(solution)/shard_map/ppermute | solution.py:447
  105.7 14.6 %collective-permute-start.11 = (f32[8,88,128]{2,1,0:T(8,128)S(1)}, f32[8,88,128]{2,1,0:T(8,128)S(1)}, u32[]{:S(2)}, u32[]{:S(2)}) collective-permute-start(f32[8,88,128]{2,1,0:T(8,128)S(1)} %get-tuple-element.57), channel_id=1, source_target_pairs={{0,6},{1,7},{2,0},{3,1},{4,2},{5,3},{6,4},{7,5},{16,22},{17,23},{1... | collective-permute-start | bytes 1081352 | tf_op jit(solution)/shard_map/ppermute | solution.py:447
  105.8 19.5 %collective-permute-start.9 = (f32[8,88,128]{2,1,0:T(8,128)S(1)}, f32[8,88,128]{2,1,0:T(8,128)S(1)}, u32[]{:S(2)}, u32[]{:S(2)}) collective-permute-start(f32[8,88,128]{2,1,0:T(8,128)S(1)} %get-tuple-element.59), channel_id=1, source_target_pairs={{0,2},{1,3},{2,4},{3,5},{4,6},{5,7},{6,0},{7,1},{16,18},{17,19},{1... | collective-permute-start | bytes 1081352 | tf_op jit(solution)/shard_map/ppermute | solution.py:447
  108.5 19.7 %collective-permute-start.16 = (f32[8,88,128]{2,1,0:T(8,128)S(1)}, f32[8,88,128]{2,1,0:T(8,128)S(1)}, u32[]{:S(2)}, u32[]{:S(2)}) collective-permute-start(f32[8,88,128]{2,1,0:T(8,128)S(1)} %get-tuple-element.62), channel_id=1, source_target_pairs={{0,32},{1,33},{2,34},{3,35},{4,36},{5,37},{6,38},{7,39},{16,48},{1... | collective-permute-start | bytes 1081352 | tf_op jit(solution)/shard_map/ppermute | solution.py:447
  108.6 20.2 %collective-permute-start.17 = (f32[8,88,128]{2,1,0:T(8,128)S(1)}, f32[8,88,128]{2,1,0:T(8,128)S(1)}, u32[]{:S(2)}, u32[]{:S(2)}) collective-permute-start(f32[8,88,128]{2,1,0:T(8,128)S(1)} %get-tuple-element.61), channel_id=1, source_target_pairs={{0,64},{1,65},{2,66},{3,67},{4,68},{5,69},{6,70},{7,71},{16,80},{1... | collective-permute-start | bytes 1081352 | tf_op jit(solution)/shard_map/ppermute | solution.py:447
  118.5 10.2 %collective-permute-start.18 = (f32[8,88,128]{2,1,0:T(8,128)S(1)}, f32[8,88,128]{2,1,0:T(8,128)S(1)}, u32[]{:S(2)}, u32[]{:S(2)}) collective-permute-start(f32[8,88,128]{2,1,0:T(8,128)S(1)} %get-tuple-element.60), channel_id=1, source_target_pairs={{0,96},{1,97},{2,98},{3,99},{4,100},{5,101},{6,102},{7,103},{16,11... | collective-permute-start | bytes 1081352 | tf_op jit(solution)/shard_map/ppermute | solution.py:447
  125.4 7.8 %collective-permute-start.12 = (f32[2,88,128]{2,1,0:T(8,128)S(1)}, f32[2,88,128]{2,1,0:T(8,128)S(1)}, u32[]{:S(2)}, u32[]{:S(2)}) collective-permute-start(f32[2,88,128]{2,1,0:T(8,128)S(1)} %get-tuple-element.63), channel_id=1, source_target_pairs={{0,32},{1,33},{2,34},{3,35},{4,36},{5,37},{6,38},{7,39},{16,48},{1... | collective-permute-start | bytes 270344 | tf_op jit(solution)/shard_map/ppermute | solution.py:447
  125.5 9.6 %collective-permute-start.13 = (f32[2,88,128]{2,1,0:T(8,128)S(1)}, f32[2,88,128]{2,1,0:T(8,128)S(1)}, u32[]{:S(2)}, u32[]{:S(2)}) collective-permute-start(f32[2,88,128]{2,1,0:T(8,128)S(1)} %get-tuple-element.65), channel_id=1, source_target_pairs={{0,64},{1,65},{2,66},{3,67},{4,68},{5,69},{6,70},{7,71},{16,80},{1... | collective-permute-start | bytes 270344 | tf_op jit(solution)/shard_map/ppermute | solution.py:447
  128.2 7.0 %collective-permute-start.14 = (f32[2,88,128]{2,1,0:T(8,128)S(1)}, f32[2,88,128]{2,1,0:T(8,128)S(1)}, u32[]{:S(2)}, u32[]{:S(2)}) collective-permute-start(f32[2,88,128]{2,1,0:T(8,128)S(1)} %get-tuple-element.64), channel_id=1, source_target_pairs={{0,96},{1,97},{2,98},{3,99},{4,100},{5,101},{6,102},{7,103},{16,11... | collective-permute-start | bytes 270344 | tf_op jit(solution)/shard_map/ppermute | solution.py:447
  128.9 6.3 %collective-permute-start.19 = (f32[2,88,128]{2,1,0:T(8,128)S(1)}, f32[2,88,128]{2,1,0:T(8,128)S(1)}, u32[]{:S(2)}, u32[]{:S(2)}) collective-permute-start(f32[2,88,128]{2,1,0:T(8,128)S(1)} %get-tuple-element.66), channel_id=1, source_target_pairs={{0,2},{1,3},{2,4},{3,5},{4,6},{5,7},{6,0},{7,1},{16,18},{17,19},{1... | collective-permute-start | bytes 270344 | tf_op jit(solution)/shard_map/ppermute | solution.py:447
  130.9 6.0 %collective-permute-start.20 = (f32[2,88,128]{2,1,0:T(8,128)S(1)}, f32[2,88,128]{2,1,0:T(8,128)S(1)}, u32[]{:S(2)}, u32[]{:S(2)}) collective-permute-start(f32[2,88,128]{2,1,0:T(8,128)S(1)} %get-tuple-element.68), channel_id=1, source_target_pairs={{0,4},{1,5},{2,6},{3,7},{4,0},{5,1},{6,2},{7,3},{16,20},{17,21},{1... | collective-permute-start | bytes 270344 | tf_op jit(solution)/shard_map/ppermute | solution.py:447
  133.2 4.5 %collective-permute-start.21 = (f32[2,88,128]{2,1,0:T(8,128)S(1)}, f32[2,88,128]{2,1,0:T(8,128)S(1)}, u32[]{:S(2)}, u32[]{:S(2)}) collective-permute-start(f32[2,88,128]{2,1,0:T(8,128)S(1)} %get-tuple-element.67), channel_id=1, source_target_pairs={{0,6},{1,7},{2,0},{3,1},{4,2},{5,3},{6,4},{7,5},{16,22},{17,23},{1... | collective-permute-start | bytes 270344 | tf_op jit(solution)/shard_map/ppermute | solution.py:447
  137.8 4.8 %collective-permute-start.22 = (f32[88,128]{1,0:T(8,128)S(1)}, f32[88,128]{1,0:T(8,128)S(1)}, u32[]{:S(2)}, u32[]{:S(2)}) collective-permute-start(f32[88,128]{1,0:T(8,128)S(1)} %slice_bitcast_fusion.2), channel_id=1, source_target_pairs={{0,16},{1,17},{2,18},{3,19},{4,20},{5,21},{6,22},{7,23},{16,0},{17... | collective-permute-start | bytes 135176 | tf_op jit(solution)/shard_map/ppermute | solution.py:506
  137.9 6.0 %collective-permute-start.23 = (f32[88,128]{1,0:T(8,128)S(1)}, f32[88,128]{1,0:T(8,128)S(1)}, u32[]{:S(2)}, u32[]{:S(2)}) collective-permute-start(f32[88,128]{1,0:T(8,128)S(1)} %get-tuple-element.70), channel_id=1, source_target_pairs={{0,8},{1,9},{2,10},{3,11},{4,12},{5,13},{6,14},{7,15},{16,24},{17,... | collective-permute-start | bytes 135176 | tf_op jit(solution)/shard_map/ppermute | solution.py:507
  141.5 5.3 %collective-permute-start.24 = (f32[88,128]{1,0:T(8,128)S(1)}, f32[88,128]{1,0:T(8,128)S(1)}, u32[]{:S(2)}, u32[]{:S(2)}) collective-permute-start(f32[88,128]{1,0:T(8,128)S(1)} %get-tuple-element.69), channel_id=1, source_target_pairs={{0,24},{1,25},{2,26},{3,27},{4,28},{5,29},{6,30},{7,31},{16,8},{17... | collective-permute-start | bytes 135176 | tf_op jit(solution)/shard_map/ppermute | solution.py:507
  (9 other events, 130.5 us)

commit v8 on v4

--- a/solution.py
+++ b/solution.py
@@ -410,7 +410,7 @@
             target[at, LEV:] = rest[g, pl.ds(pl.multiple_of(a * 16, 16), 16), :]
         return carry
 
-    lax.fori_loop(0, 32, place_blocks, 0, unroll=8)
+    lax.fori_loop(0, 32, place_blocks, 0, unroll=32)
 
 
 def window(part, scalars, arrays):

time: 145 us -> 143 us (0.986)
  Pallas kernels: 36.6 us -> 34.6 us
    pallas_call x2, Pallas kernels: 26.8 us -> 24.8 us  [window(): pl.pallas_call(functools.partial(window_kernel, part), out_shape=[jax.Sha...]
  transfers between devices with their start and end apart: 25 -> 25, of which waited for: 10 -> 11; matrix products, arithmetic and copies ran while one was open for 2% -> 2% of each run, Pallas kernels for 22% -> 21%
where the time goes in v8:
time: 143 us
  starting transfers between devices  57.8 us (40%)
  waiting for transfers between devices  45.3 us (32%)
  Pallas kernels  34.6 us (24%)
  local copies, waits for them, and re-layouts  2.63 us (2%)
    ppermute x12, starting transfers between devices, line_sum(): sent = [lax.ppermute(parts[k], ALL, moved(**{name: k})) for k in (1, 2, 3)]  34.6 us
    pallas_call x2, Pallas kernels, window(): pl.pallas_call(functools.partial(window_kernel, part), out_shape=[jax.Sha...  24.8 us
    ppermute x1, waiting for transfers between devices, shards(): west = lax.ppermute(to_east, 'lon', EASTWARD)  17.4 us
    ppermute x1, waiting for transfers between devices, shards(): before_edge = lax.ppermute(edge_next, ALL, FORWARD)  10.6 us
    ppermute x1, starting transfers between devices, shards(): east = lax.ppermute(to_west, 'lon', WESTWARD)  6 us
    ppermute x1, waiting for transfers between devices, shards(): lax.ppermute(bulk[0], ALL, FORWARD)  5.2 us
    ppermute x1, starting transfers between devices, shards(): lax.ppermute(bulk[3], ALL, BACKWARD)  4.93 us
    pallas_call x1, Pallas kernels, lead(): pl.pallas_call(lead_kernel, out_shape=[jax.ShapeDtypeStruct((COLS, WPACK...  4.01 us
  transfers between devices with their start and end apart: 25, of which 11 were waited for; matrix products, arithmetic and copies ran while one was open for 2% of the time, Pallas kernels for 21%

profile of v8, /device:TPU:0, one launch (start us, length us, event | category | flops | bytes accessed | tf_op | source)
XLA Modules:
  0.0 142.7 jit_solution(16202004757115686255)
XLA Ops:
  1.3 4.0 %lead.1 = (f32[48,1664]{1,0:T(8,128)}, f32[48,1664]{1,0:T(8,128)}) custom-call(s32[7]{0:T(128)} %stack.45.info, s32[8]{0:T(128)} %vec_ids.3, bf16[8,48,1152]{2,1,0:T(8,128)(2,1)} %pool.3, f32[8,48,288]{2,1,0:T(8,128)} %winds.3), custom_call_target="tpu_custom_call" | custom-call | flops 1073741824 | bytes 4194304 | tf_op jit(solution)/shard_map/lead/pallas_call | solution.py:126
  5.4 1.7 %collective-permute-start = (f32[48,1664]{1,0:T(8,128)}, f32[48,1664]{1,0:T(8,128)S(1)}, u32[]{:S(2)}, u32[]{:S(2)}) collective-permute-start(f32[48,1664]{1,0:T(8,128)} %get-tuple-element.27), channel_id=1, source_target_pairs={{0,16},{8,0},{16,32},{24,8},{32,48},{40,24},{48,64},{56,40},{64,80... | collective-permute-start | bytes 958472 | tf_op jit(solution)/shard_map/ppermute | solution.py:464
  7.1 1.9 %collective-permute-start.1 = (f32[48,1664]{1,0:T(8,128)}, f32[48,1664]{1,0:T(8,128)S(1)}, u32[]{:S(2)}, u32[]{:S(2)}) collective-permute-start(f32[48,1664]{1,0:T(8,128)} %get-tuple-element.30), channel_id=1, source_target_pairs={{16,0},{0,8},{32,16},{8,24},{48,32},{24,40},{64,48},{40,56},{80,64... | collective-permute-start | bytes 958472 | tf_op jit(solution)/shard_map/ppermute | solution.py:465
  10.7 3.1 %pack.1 = (f32[4,48,1152]{2,1,0:T(8,128)S(1)}, f32[4,48,1152]{2,1,0:T(8,128)S(1)}, f32[8,48,288]{2,1,0:T(8,128)S(1)}, f32[4,40,640]{2,1,0:T(8,128)S(1)}, f32[4,4...) custom-call(s32[7]{0:T(128)S(1)} %copy-done, ...), custom_call_target="tpu_custom_call" | custom-call | flops 1073741824 | bytes 4194304 | tf_op jit(solution)/shard_map/pack/pallas_call | solution.py:182
  13.8 10.6 %collective-permute-done.before.before_edge = f32[48,1664]{1,0:T(8,128)S(1)} collective-permute-done((f32[48,1664]{1,0:T(8,128)}, f32[48,1664]{1,0:T(8,128)S(1)}, u32[]{:S(2)}, u32[]{:S(2)}) %collective-permute-start) | collective-permute-done | bytes 319520 | tf_op jit(solution)/shard_map/ppermute | solution.py:464
  24.4 3.5 %collective-permute-done.1.after.after_edge = f32[48,1664]{1,0:T(8,128)S(1)} collective-permute-done((f32[48,1664]{1,0:T(8,128)}, f32[48,1664]{1,0:T(8,128)S(1)}, u32[]{:S(2)}, u32[]{:S(2)}) %collective-permute-start.1) | collective-permute-done | bytes 319520 | tf_op jit(solution)/shard_map/ppermute | solution.py:465
  28.1 6.0 %collective-permute-start.3 = (f32[18,4,1152]{2,1,0:T(4,128)S(1)}, f32[18,4,1152]{2,1,0:T(4,128)S(1)}, u32[]{:S(2)}, u32[]{:S(2)}) collective-permute-start(f32[18,4,1152]{2,1,0:T(4,128)S(1)} %get-tuple-element.37), channel_id=1, source_target_pairs={{1,0},{2,1},{3,2},{4,3},{5,4},{6,5},{7,6},{8,7},{9,8},{10,9},{11,1... | collective-permute-start | bytes 995336 | tf_op jit(solution)/shard_map/ppermute | solution.py:473
  34.2 3.5 %collective-permute-start.5 = (f32[4,40,640]{2,1,0:T(8,128)S(1)}, f32[4,40,640]{2,1,0:T(8,128)S(1)}, u32[]{:S(2)}, u32[]{:S(2)}) collective-permute-start(f32[4,40,640]{2,1,0:T(8,128)S(1)} %get-tuple-element.42), channel_id=1, source_target_pairs={{16,0},{0,8},{32,16},{8,24},{48,32},{24,40},{64,48},{40,56},{80,64... | collective-permute-start | bytes 1228808 | tf_op jit(solution)/shard_map/ppermute | solution.py:474
  37.8 17.4 %collective-permute-done.2.west = f32[18,4,1152]{2,1,0:T(4,128)S(1)} collective-permute-done((f32[18,4,1152]{2,1,0:T(4,128)S(1)}, f32[18,4,1152]{2,1,0:T(4,128)S(1)}, u32[]{:S(2)}, u32[]{:S(2)}) %collective-permute-start.2) | collective-permute-done | bytes 331808 | tf_op jit(solution)/shard_map/ppermute | solution.py:472
  55.2 4.9 %collective-permute-start.7 = (f32[4,40,512]{2,1,0:T(8,128)S(1)}, f32[4,40,512]{2,1,0:T(8,128)S(1)}, u32[]{:S(2)}, u32[]{:S(2)}) collective-permute-start(f32[4,40,512]{2,1,0:T(8,128)S(1)} %get-tuple-element.44), channel_id=1, source_target_pairs={{16,0},{0,8},{32,16},{8,24},{48,32},{24,40},{64,48},{40,56},{80,64... | collective-permute-start | bytes 983048 | tf_op jit(solution)/shard_map/ppermute | solution.py:475
  60.1 2.6 %frame.1 = (f32[14,64,288]{2,1,0:T(8,128)S(1)}, f32[4,14,64,640]{3,2,1,0:T(8,128)S(1)}) custom-call(s32[7]{0:T(128)S(1)} %copy-done, f32[48,1664]{1,0:T(8,128)S(1)} %collective-permute-done.before.before_edge, f32[48,1664]{1,0:T(8,128)S(1)} %collective-permute-done.1.after.after_edge, f32[8,48,288]{2,1,0:T(8,128)S(1)} %get-tuple-element.31.wind, ...), custom_call_target="tpu_custom_call" | custom-call | flops 17179869184 | bytes 4194304 | tf_op jit(solution)/shard_map/frame/pallas_call | solution.py:271
  62.7 5.2 %collective-permute-done.4.before_0 = f32[4,40,640]{2,1,0:T(8,128)S(1)} collective-permute-done((f32[4,40,640]{2,1,0:T(8,128)S(1)}, f32[4,40,640]{2,1,0:T(8,128)S(1)}, u32[]{:S(2)}, u32[]{:S(2)}) %collective-permute-start.4) | collective-permute-done | bytes 409632 | tf_op jit(solution)/shard_map/ppermute | solution.py:474
  69.5 12.5 %window_0.1 = (f32[8,48,640]{2,1,0:T(8,128)S(1)}, f32[32,88,128]{2,1,0:T(8,128)S(1)}, f32[32,88,128]{2,1,0:T(8,128)S(1)}) custom-call(s32[7]{0:T(128)S(1)} %copy-done, s32[4]{0:T(128)S(1)} %copy-done.5, f32[8]{0:T(128)S(1)} %add_cosine_fusion.cosine, f32[48,1664]{1,0:T(8,128)S(1)} %collective-permute-done.before.before_edge, ...), custom_call_target="tpu_custom_call" | custom-call | flops 8589934592 | bytes 16777216 | tf_op jit(solution)/shard_map/window_0/pallas_call | solution.py:419
  82.4 12.2 %window_1.1 = (f32[8,48,1152]{2,1,0:T(8,128)}, f32[32,88,128]{2,1,0:T(8,128)S(1)}, f32[32,88,128]{2,1,0:T(8,128)S(1)}) custom-call(s32[7]{0:T(128)S(1)} %copy-done, s32[4]{0:T(128)S(1)} %copy-done.5, f32[8]{0:T(128)S(1)} %add_cosine_fusion.cosine, f32[48,1664]{1,0:T(8,128)S(1)} %collective-permute-done.before.before_edge, ...), custom_call_target="tpu_custom_call" | custom-call | flops 8589934592 | bytes 16777216 | tf_op jit(solution)/shard_map/window_1/pallas_call | solution.py:419
  95.2 4.5 %collective-permute-start.11 = (f32[8,88,128]{2,1,0:T(8,128)S(1)}, f32[8,88,128]{2,1,0:T(8,128)S(1)}, u32[]{:S(2)}, u32[]{:S(2)}) collective-permute-start(f32[8,88,128]{2,1,0:T(8,128)S(1)} %get-tuple-element.57), channel_id=1, source_target_pairs={{0,6},{1,7},{2,0},{3,1},{4,2},{5,3},{6,4},{7,5},{16,22},{17,23},{1... | collective-permute-start | bytes 1081352 | tf_op jit(solution)/shard_map/ppermute | solution.py:444
  100.8 8.1 %collective-permute-start.17 = (f32[8,88,128]{2,1,0:T(8,128)S(1)}, f32[8,88,128]{2,1,0:T(8,128)S(1)}, u32[]{:S(2)}, u32[]{:S(2)}) collective-permute-start(f32[8,88,128]{2,1,0:T(8,128)S(1)} %get-tuple-element.61), channel_id=1, source_target_pairs={{0,64},{1,65},{2,66},{3,67},{4,68},{5,69},{6,70},{7,71},{16,80},{1... | collective-permute-start | bytes 1081352 | tf_op jit(solution)/shard_map/ppermute | solution.py:444
  108.8 8.5 %collective-permute-start.18 = (f32[8,88,128]{2,1,0:T(8,128)S(1)}, f32[8,88,128]{2,1,0:T(8,128)S(1)}, u32[]{:S(2)}, u32[]{:S(2)}) collective-permute-start(f32[8,88,128]{2,1,0:T(8,128)S(1)} %get-tuple-element.60), channel_id=1, source_target_pairs={{0,96},{1,97},{2,98},{3,99},{4,100},{5,101},{6,102},{7,103},{16,11... | collective-permute-start | bytes 1081352 | tf_op jit(solution)/shard_map/ppermute | solution.py:444
  117.5 8.2 %collective-permute-start.13 = (f32[2,88,128]{2,1,0:T(8,128)S(1)}, f32[2,88,128]{2,1,0:T(8,128)S(1)}, u32[]{:S(2)}, u32[]{:S(2)}) collective-permute-start(f32[2,88,128]{2,1,0:T(8,128)S(1)} %get-tuple-element.65), channel_id=1, source_target_pairs={{0,64},{1,65},{2,66},{3,67},{4,68},{5,69},{6,70},{7,71},{16,80},{1... | collective-permute-start | bytes 270344 | tf_op jit(solution)/shard_map/ppermute | solution.py:444
  126.0 2.0 %collective-permute-start.20 = (f32[2,88,128]{2,1,0:T(8,128)S(1)}, f32[2,88,128]{2,1,0:T(8,128)S(1)}, u32[]{:S(2)}, u32[]{:S(2)}) collective-permute-start(f32[2,88,128]{2,1,0:T(8,128)S(1)} %get-tuple-element.68), channel_id=1, source_target_pairs={{0,4},{1,5},{2,6},{3,7},{4,0},{5,1},{6,2},{7,3},{16,20},{17,21},{1... | collective-permute-start | bytes 270344 | tf_op jit(solution)/shard_map/ppermute | solution.py:444
  128.0 2.2 %collective-permute-start.21 = (f32[2,88,128]{2,1,0:T(8,128)S(1)}, f32[2,88,128]{2,1,0:T(8,128)S(1)}, u32[]{:S(2)}, u32[]{:S(2)}) collective-permute-start(f32[2,88,128]{2,1,0:T(8,128)S(1)} %get-tuple-element.67), channel_id=1, source_target_pairs={{0,6},{1,7},{2,0},{3,1},{4,2},{5,3},{6,4},{7,5},{16,22},{17,23},{1... | collective-permute-start | bytes 270344 | tf_op jit(solution)/shard_map/ppermute | solution.py:444
  130.3 2.8 %collective-permute-done.19 = f32[2,88,128]{2,1,0:T(8,128)S(1)} collective-permute-done((f32[2,88,128]{2,1,0:T(8,128)S(1)}, f32[2,88,128]{2,1,0:T(8,128)S(1)}, u32[]{:S(2)}, u32[]{:S(2)}) %collective-permute-start.19) | collective-permute-done | bytes 90144 | tf_op jit(solution)/shard_map/ppermute | solution.py:444
  133.9 2.7 %collective-permute-start.23 = (f32[88,128]{1,0:T(8,128)S(1)}, f32[88,128]{1,0:T(8,128)S(1)}, u32[]{:S(2)}, u32[]{:S(2)}) collective-permute-start(f32[88,128]{1,0:T(8,128)S(1)} %get-tuple-element.70), channel_id=1, source_target_pairs={{0,8},{1,9},{2,10},{3,11},{4,12},{5,13},{6,14},{7,15},{16,24},{17,... | collective-permute-start | bytes 135176 | tf_op jit(solution)/shard_map/ppermute | solution.py:503
  136.6 2.0 %collective-permute-start.24 = (f32[88,128]{1,0:T(8,128)S(1)}, f32[88,128]{1,0:T(8,128)S(1)}, u32[]{:S(2)}, u32[]{:S(2)}) collective-permute-start(f32[88,128]{1,0:T(8,128)S(1)} %get-tuple-element.69), channel_id=1, source_target_pairs={{0,24},{1,25},{2,26},{3,27},{4,28},{5,29},{6,30},{7,31},{16,8},{17... | collective-permute-start | bytes 135176 | tf_op jit(solution)/shard_map/ppermute | solution.py:503
  139.5 2.3 %collective-permute-done.24 = f32[88,128]{1,0:T(8,128)S(1)} collective-permute-done((f32[88,128]{1,0:T(8,128)S(1)}, f32[88,128]{1,0:T(8,128)S(1)}, u32[]{:S(2)}, u32[]{:S(2)}) %collective-permute-start.24) | collective-permute-done | bytes 45088 | tf_op jit(solution)/shard_map/ppermute | solution.py:503
  (78 shorter events, 9.2 us)
Async XLA Ops:
  5.4 19.0 %collective-permute-start = (f32[48,1664]{1,0:T(8,128)}, f32[48,1664]{1,0:T(8,128)S(1)}, u32[]{:S(2)}, u32[]{:S(2)}) collective-permute-start(f32[48,1664]{1,0:T(8,128)} %get-tuple-element.27), channel_id=1, source_target_pairs={{0,16},{8,0},{16,32},{24,8},{32,48},{40,24},{48,64},{56,40},{64,80... | collective-permute-start | bytes 958472 | tf_op jit(solution)/shard_map/ppermute | solution.py:464
  7.1 20.8 %collective-permute-start.1 = (f32[48,1664]{1,0:T(8,128)}, f32[48,1664]{1,0:T(8,128)S(1)}, u32[]{:S(2)}, u32[]{:S(2)}) collective-permute-start(f32[48,1664]{1,0:T(8,128)} %get-tuple-element.30), channel_id=1, source_target_pairs={{16,0},{0,8},{32,16},{8,24},{48,32},{24,40},{64,48},{40,56},{80,64... | collective-permute-start | bytes 958472 | tf_op jit(solution)/shard_map/ppermute | solution.py:465
  28.0 27.2 %collective-permute-start.2 = (f32[18,4,1152]{2,1,0:T(4,128)S(1)}, f32[18,4,1152]{2,1,0:T(4,128)S(1)}, u32[]{:S(2)}, u32[]{:S(2)}) collective-permute-start(f32[18,4,1152]{2,1,0:T(4,128)S(1)} %get-tuple-element.36), channel_id=1, source_target_pairs={{0,1},{1,2},{2,3},{3,4},{4,5},{5,6},{6,7},{7,8},{8,9},{9,10},{10,1... | collective-permute-start | bytes 995336 | tf_op jit(solution)/shard_map/ppermute | solution.py:472
  28.1 32.0 %collective-permute-start.3 = (f32[18,4,1152]{2,1,0:T(4,128)S(1)}, f32[18,4,1152]{2,1,0:T(4,128)S(1)}, u32[]{:S(2)}, u32[]{:S(2)}) collective-permute-start(f32[18,4,1152]{2,1,0:T(4,128)S(1)} %get-tuple-element.37), channel_id=1, source_target_pairs={{1,0},{2,1},{3,2},{4,3},{5,4},{6,5},{7,6},{8,7},{9,8},{10,9},{11,1... | collective-permute-start | bytes 995336 | tf_op jit(solution)/shard_map/ppermute | solution.py:473
  34.2 33.7 %collective-permute-start.4 = (f32[4,40,640]{2,1,0:T(8,128)S(1)}, f32[4,40,640]{2,1,0:T(8,128)S(1)}, u32[]{:S(2)}, u32[]{:S(2)}) collective-permute-start(f32[4,40,640]{2,1,0:T(8,128)S(1)} %get-tuple-element.41), channel_id=1, source_target_pairs={{0,16},{8,0},{16,32},{24,8},{32,48},{40,24},{48,64},{56,40},{64,80... | collective-permute-start | bytes 1228808 | tf_op jit(solution)/shard_map/ppermute | solution.py:474
  34.2 35.2 %collective-permute-start.5 = (f32[4,40,640]{2,1,0:T(8,128)S(1)}, f32[4,40,640]{2,1,0:T(8,128)S(1)}, u32[]{:S(2)}, u32[]{:S(2)}) collective-permute-start(f32[4,40,640]{2,1,0:T(8,128)S(1)} %get-tuple-element.42), channel_id=1, source_target_pairs={{16,0},{0,8},{32,16},{8,24},{48,32},{24,40},{64,48},{40,56},{80,64... | collective-permute-start | bytes 1228808 | tf_op jit(solution)/shard_map/ppermute | solution.py:474
  37.8 44.7 %collective-permute-start.6 = (f32[4,40,512]{2,1,0:T(8,128)S(1)}, f32[4,40,512]{2,1,0:T(8,128)S(1)}, u32[]{:S(2)}, u32[]{:S(2)}) collective-permute-start(f32[4,40,512]{2,1,0:T(8,128)S(1)} %get-tuple-element.43), channel_id=1, source_target_pairs={{0,16},{8,0},{16,32},{24,8},{32,48},{40,24},{48,64},{56,40},{64,80... | collective-permute-start | bytes 983048 | tf_op jit(solution)/shard_map/ppermute | solution.py:475
  55.2 27.2 %collective-permute-start.7 = (f32[4,40,512]{2,1,0:T(8,128)S(1)}, f32[4,40,512]{2,1,0:T(8,128)S(1)}, u32[]{:S(2)}, u32[]{:S(2)}) collective-permute-start(f32[4,40,512]{2,1,0:T(8,128)S(1)} %get-tuple-element.44), channel_id=1, source_target_pairs={{16,0},{0,8},{32,16},{8,24},{48,32},{24,40},{64,48},{40,56},{80,64... | collective-permute-start | bytes 983048 | tf_op jit(solution)/shard_map/ppermute | solution.py:475
  82.0 12.8 %collective-permute-start.8 = (f32[32,88,128]{2,1,0:T(8,128)S(1)}, f32[32,88,128]{2,1,0:T(8,128)S(1)}, u32[]{:S(2)}, u32[]{:S(2)}) collective-permute-start(f32[32,88,128]{2,1,0:T(8,128)S(1)} %get-tuple-element.49), channel_id=1, source_target_pairs={{0,1},{1,0},{2,3},{3,2},{4,5},{5,4},{6,7},{7,6},{16,17},{17,16},{1... | collective-permute-start | bytes 4325384 | tf_op jit(solution)/shard_map/ppermute | solution.py:490
  94.7 5.8 %collective-permute-start.15 = (f32[32,88,128]{2,1,0:T(8,128)S(1)}, f32[32,88,128]{2,1,0:T(8,128)S(1)}, u32[]{:S(2)}, u32[]{:S(2)}) collective-permute-start(f32[32,88,128]{2,1,0:T(8,128)S(1)} %get-tuple-element.51), channel_id=1, source_target_pairs={{0,1},{1,0},{2,3},{3,2},{4,5},{5,4},{6,7},{7,6},{16,17},{17,16},{1... | collective-permute-start | bytes 4325384 | tf_op jit(solution)/shard_map/ppermute | solution.py:494
  95.1 13.7 %collective-permute-start.10 = (f32[8,88,128]{2,1,0:T(8,128)S(1)}, f32[8,88,128]{2,1,0:T(8,128)S(1)}, u32[]{:S(2)}, u32[]{:S(2)}) collective-permute-start(f32[8,88,128]{2,1,0:T(8,128)S(1)} %get-tuple-element.58), channel_id=1, source_target_pairs={{0,4},{1,5},{2,6},{3,7},{4,0},{5,1},{6,2},{7,3},{16,20},{17,21},{1... | collective-permute-start | bytes 1081352 | tf_op jit(solution)/shard_map/ppermute | solution.py:444
  95.2 22.2 %collective-permute-start.11 = (f32[8,88,128]{2,1,0:T(8,128)S(1)}, f32[8,88,128]{2,1,0:T(8,128)S(1)}, u32[]{:S(2)}, u32[]{:S(2)}) collective-permute-start(f32[8,88,128]{2,1,0:T(8,128)S(1)} %get-tuple-element.57), channel_id=1, source_target_pairs={{0,6},{1,7},{2,0},{3,1},{4,2},{5,3},{6,4},{7,5},{16,22},{17,23},{1... | collective-permute-start | bytes 1081352 | tf_op jit(solution)/shard_map/ppermute | solution.py:444
  99.7 17.7 %collective-permute-start.9 = (f32[8,88,128]{2,1,0:T(8,128)S(1)}, f32[8,88,128]{2,1,0:T(8,128)S(1)}, u32[]{:S(2)}, u32[]{:S(2)}) collective-permute-start(f32[8,88,128]{2,1,0:T(8,128)S(1)} %get-tuple-element.59), channel_id=1, source_target_pairs={{0,2},{1,3},{2,4},{3,5},{4,6},{5,7},{6,0},{7,1},{16,18},{17,19},{1... | collective-permute-start | bytes 1081352 | tf_op jit(solution)/shard_map/ppermute | solution.py:444
  100.7 25.1 %collective-permute-start.16 = (f32[8,88,128]{2,1,0:T(8,128)S(1)}, f32[8,88,128]{2,1,0:T(8,128)S(1)}, u32[]{:S(2)}, u32[]{:S(2)}) collective-permute-start(f32[8,88,128]{2,1,0:T(8,128)S(1)} %get-tuple-element.62), channel_id=1, source_target_pairs={{0,32},{1,33},{2,34},{3,35},{4,36},{5,37},{6,38},{7,39},{16,48},{1... | collective-permute-start | bytes 1081352 | tf_op jit(solution)/shard_map/ppermute | solution.py:444
  100.8 25.0 %collective-permute-start.17 = (f32[8,88,128]{2,1,0:T(8,128)S(1)}, f32[8,88,128]{2,1,0:T(8,128)S(1)}, u32[]{:S(2)}, u32[]{:S(2)}) collective-permute-start(f32[8,88,128]{2,1,0:T(8,128)S(1)} %get-tuple-element.61), channel_id=1, source_target_pairs={{0,64},{1,65},{2,66},{3,67},{4,68},{5,69},{6,70},{7,71},{16,80},{1... | collective-permute-start | bytes 1081352 | tf_op jit(solution)/shard_map/ppermute | solution.py:444
  108.8 17.0 %collective-permute-start.18 = (f32[8,88,128]{2,1,0:T(8,128)S(1)}, f32[8,88,128]{2,1,0:T(8,128)S(1)}, u32[]{:S(2)}, u32[]{:S(2)}) collective-permute-start(f32[8,88,128]{2,1,0:T(8,128)S(1)} %get-tuple-element.60), channel_id=1, source_target_pairs={{0,96},{1,97},{2,98},{3,99},{4,100},{5,101},{6,102},{7,103},{16,11... | collective-permute-start | bytes 1081352 | tf_op jit(solution)/shard_map/ppermute | solution.py:444
  117.5 10.6 %collective-permute-start.12 = (f32[2,88,128]{2,1,0:T(8,128)S(1)}, f32[2,88,128]{2,1,0:T(8,128)S(1)}, u32[]{:S(2)}, u32[]{:S(2)}) collective-permute-start(f32[2,88,128]{2,1,0:T(8,128)S(1)} %get-tuple-element.63), channel_id=1, source_target_pairs={{0,32},{1,33},{2,34},{3,35},{4,36},{5,37},{6,38},{7,39},{16,48},{1... | collective-permute-start | bytes 270344 | tf_op jit(solution)/shard_map/ppermute | solution.py:444
  117.5 12.7 %collective-permute-start.13 = (f32[2,88,128]{2,1,0:T(8,128)S(1)}, f32[2,88,128]{2,1,0:T(8,128)S(1)}, u32[]{:S(2)}, u32[]{:S(2)}) collective-permute-start(f32[2,88,128]{2,1,0:T(8,128)S(1)} %get-tuple-element.65), channel_id=1, source_target_pairs={{0,64},{1,65},{2,66},{3,67},{4,68},{5,69},{6,70},{7,71},{16,80},{1... | collective-permute-start | bytes 270344 | tf_op jit(solution)/shard_map/ppermute | solution.py:444
  125.9 7.2 %collective-permute-start.19 = (f32[2,88,128]{2,1,0:T(8,128)S(1)}, f32[2,88,128]{2,1,0:T(8,128)S(1)}, u32[]{:S(2)}, u32[]{:S(2)}) collective-permute-start(f32[2,88,128]{2,1,0:T(8,128)S(1)} %get-tuple-element.66), channel_id=1, source_target_pairs={{0,2},{1,3},{2,4},{3,5},{4,6},{5,7},{6,0},{7,1},{16,18},{17,19},{1... | collective-permute-start | bytes 270344 | tf_op jit(solution)/shard_map/ppermute | solution.py:444
  126.0 7.1 %collective-permute-start.20 = (f32[2,88,128]{2,1,0:T(8,128)S(1)}, f32[2,88,128]{2,1,0:T(8,128)S(1)}, u32[]{:S(2)}, u32[]{:S(2)}) collective-permute-start(f32[2,88,128]{2,1,0:T(8,128)S(1)} %get-tuple-element.68), channel_id=1, source_target_pairs={{0,4},{1,5},{2,6},{3,7},{4,0},{5,1},{6,2},{7,3},{16,20},{17,21},{1... | collective-permute-start | bytes 270344 | tf_op jit(solution)/shard_map/ppermute | solution.py:444
  128.0 5.6 %collective-permute-start.21 = (f32[2,88,128]{2,1,0:T(8,128)S(1)}, f32[2,88,128]{2,1,0:T(8,128)S(1)}, u32[]{:S(2)}, u32[]{:S(2)}) collective-permute-start(f32[2,88,128]{2,1,0:T(8,128)S(1)} %get-tuple-element.67), channel_id=1, source_target_pairs={{0,6},{1,7},{2,0},{3,1},{4,2},{5,3},{6,4},{7,5},{16,22},{17,23},{1... | collective-permute-start | bytes 270344 | tf_op jit(solution)/shard_map/ppermute | solution.py:444
  133.7 4.8 %collective-permute-start.22 = (f32[88,128]{1,0:T(8,128)S(1)}, f32[88,128]{1,0:T(8,128)S(1)}, u32[]{:S(2)}, u32[]{:S(2)}) collective-permute-start(f32[88,128]{1,0:T(8,128)S(1)} %slice_bitcast_fusion.2), channel_id=1, source_target_pairs={{0,16},{1,17},{2,18},{3,19},{4,20},{5,21},{6,22},{7,23},{16,0},{17... | collective-permute-start | bytes 135176 | tf_op jit(solution)/shard_map/ppermute | solution.py:502
  133.9 5.6 %collective-permute-start.23 = (f32[88,128]{1,0:T(8,128)S(1)}, f32[88,128]{1,0:T(8,128)S(1)}, u32[]{:S(2)}, u32[]{:S(2)}) collective-permute-start(f32[88,128]{1,0:T(8,128)S(1)} %get-tuple-element.70), channel_id=1, source_target_pairs={{0,8},{1,9},{2,10},{3,11},{4,12},{5,13},{6,14},{7,15},{16,24},{17,... | collective-permute-start | bytes 135176 | tf_op jit(solution)/shard_map/ppermute | solution.py:503
  136.6 5.3 %collective-permute-start.24 = (f32[88,128]{1,0:T(8,128)S(1)}, f32[88,128]{1,0:T(8,128)S(1)}, u32[]{:S(2)}, u32[]{:S(2)}) collective-permute-start(f32[88,128]{1,0:T(8,128)S(1)} %get-tuple-element.69), channel_id=1, source_target_pairs={{0,24},{1,25},{2,26},{3,27},{4,28},{5,29},{6,30},{7,31},{16,8},{17... | collective-permute-start | bytes 135176 | tf_op jit(solution)/shard_map/ppermute | solution.py:503
  (9 other events, 105.4 us)
